TPU v7x, 256 devices: a whole 4x4x8 slice. The times are simulated.
256 devices in a mesh: owner: 128 (over x, z, y), replica: 2 (over core).
Axes of the slice: x: 4, y: 4, z: 8, core: 2. Of those that a mesh axis runs over, the one named last changes fastest.
Arguments:
- queries: bfloat16 [2048, 32, 128], P(('owner', 'replica')), may hold values from -8 to 8
- pages: bfloat16 [128, 1024, 128], P('owner'), may hold values from -3 to 3
- pair_page: int32 [16384, 1], P(('owner', 'replica')), may hold values from 0 to 127, as said below
- pair_query: int32 [16384], P(('owner', 'replica')), may hold values from 0 to 7
- pair_label: int32 [16384], P(('owner', 'replica')), may hold values 0 or 1
- hot_pages: int32 [2], replicated, may hold values from 0 to 127, as said below
Outputs:
- query_grad: bfloat16 [2048, 32, 128], P(('owner', 'replica'))
- page_grad: bfloat16 [128, 1024, 128], P('owner', 'replica')
Inputs may be any that keep to these rules, and one draw needn't show every extreme that they name: `pair_page`: the rows of one device name no page more than 2 times, and some page exactly 2 times. `hot_pages`: 2 different page numbers; the last page is always among them.
All inputs are finite; a program needn't handle non-finite values. No bound on the sum of `pair_label` on one device may be relied on, other than what follows from the above.
Results may differ from a plain program's by a relative error of at most 0.0085.
Values may be sent and summed in bfloat16 or wider, within the bound.
No kernel may reach another device: no remote copies, remote signals or barrier semaphores. Data moves between devices by JAX's collectives and lax.ppermute only.
A program may use at most 64 MiB of HBM per device.

v0:
```python
import math

import jax
import jax.numpy as jnp
from jax import lax
from jax.sharding import PartitionSpec as P

SHARPNESS = 4.0
SLOPE_SCALE = 0.5
HOT_SHIFT = 2.0


def score_block(token_rows, label_rows, page_rows, offset, shift):
    count = token_rows.shape[0]
    tokens_each = token_rows.shape[1]
    flat_rows = token_rows.reshape(count * tokens_each, token_rows.shape[2])
    logits = SHARPNESS * lax.dot_general(
        flat_rows, page_rows, (((1,), (1,)), ((), ())), preferred_element_type=jnp.float32
    )
    peak = jnp.max(logits, axis=1, keepdims=True)
    expo = jnp.exp(logits - peak)
    totals = jnp.sum(expo, axis=1, keepdims=True)
    log_total = peak + jnp.log(totals)
    score = jnp.sum(log_total.reshape(count, tokens_each), axis=1) / SHARPNESS
    logit = SLOPE_SCALE * score + offset - shift
    slope = SLOPE_SCALE * (jax.nn.sigmoid(logit) - label_rows[:, 0]) * label_rows[:, 1]
    slope_rows = jnp.repeat(slope, tokens_each)[:, None]
    weight = (expo / totals * slope_rows).astype(jnp.bfloat16)
    grads = jnp.dot(weight, page_rows, preferred_element_type=jnp.float32).astype(jnp.bfloat16)
    page_part = lax.dot_general(
        weight, flat_rows, (((0,), (0,)), ((), ())), preferred_element_type=jnp.float32
    )
    return (grads.reshape(token_rows.shape), page_part)


def shards(queries, pages, pair_page, pair_query, pair_label, hot_pages):
    owners = lax.axis_size("owner")
    owner_place = lax.axis_index("owner")
    local_pairs = pair_page.shape[0]
    local_queries = queries.shape[0]
    tokens_each = queries.shape[1]
    width = queries.shape[2]
    patch_count = pages.shape[1]
    capacity = max(2, 4 * local_pairs // owners)
    slots = owners * capacity
    offset = -SLOPE_SCALE * tokens_each * (math.log(patch_count) / SHARPNESS + SHARPNESS / 2.0)
    targets = pair_page[:, 0]
    owned_hot = (hot_pages == owner_place).astype(jnp.float32)
    target_hot = (targets[:, None] == jnp.arange(owners, dtype=jnp.int32)[None, :]).astype(
        jnp.int32
    )
    earlier = jnp.cumsum(target_hot, axis=0) - target_hot
    rank_within = jnp.sum(earlier * target_hot, axis=1)
    slot_of = targets * capacity + rank_within
    select = (slot_of[None, :] == jnp.arange(slots, dtype=jnp.int32)[:, None]).astype(jnp.bfloat16)
    query_hot = (pair_query[:, None] == jnp.arange(local_queries, dtype=jnp.int32)[None, :]).astype(
        jnp.bfloat16
    )
    pair_tokens = jnp.dot(
        query_hot,
        queries.reshape(local_queries, tokens_each * width),
        preferred_element_type=jnp.float32,
    ).astype(jnp.bfloat16)
    send_tokens = jnp.dot(select, pair_tokens, preferred_element_type=jnp.float32).astype(
        jnp.bfloat16
    )
    pair_flags = jnp.stack(
        [pair_label.astype(jnp.float32), jnp.ones((local_pairs,), jnp.float32)], axis=1
    ).astype(jnp.bfloat16)
    send_flags = jnp.dot(select, pair_flags, preferred_element_type=jnp.float32).astype(
        jnp.bfloat16
    )
    got_tokens, got_flags = (
        lax.all_to_all(
            send_tokens.reshape(owners, capacity * tokens_each * width),
            "owner",
            split_axis=0,
            concat_axis=0,
            tiled=True,
        ),
        lax.all_to_all(
            send_flags.reshape(owners, capacity * 2),
            "owner",
            split_axis=0,
            concat_axis=0,
            tiled=True,
        ),
    )
    slot_tokens = got_tokens.reshape(slots, tokens_each, width)
    slot_flags = got_flags.reshape(slots, 2).astype(jnp.float32)
    page_rows = pages[0]
    own_shift = HOT_SHIFT * jnp.sum(owned_hot)
    block_rows = slots // max(1, slots // 64)
    block_count = slots // block_rows

    def step(carry, inputs):
        grads, page_part = score_block(inputs[0], inputs[1], page_rows, offset, own_shift)
        return (carry + page_part, grads)

    page_terms, slot_grads = lax.scan(
        step,
        jnp.zeros((patch_count, width), jnp.float32),
        (
            slot_tokens.reshape(block_count, block_rows, tokens_each, width),
            slot_flags.reshape(block_count, block_rows, 2),
        ),
    )
    slot_grads = slot_grads.reshape(slots, tokens_each, width)
    returned = lax.all_to_all(
        slot_grads.reshape(owners, capacity * tokens_each * width),
        "owner",
        split_axis=0,
        concat_axis=0,
        tiled=True,
    )
    pair_grads = lax.dot_general(
        select,
        returned.reshape(slots, tokens_each * width),
        (((0,), (0,)), ((), ())),
        preferred_element_type=jnp.float32,
    )
    summed = lax.dot_general(
        query_hot.astype(jnp.float32),
        pair_grads,
        (((0,), (0,)), ((), ())),
        precision=lax.Precision.HIGHEST,
        preferred_element_type=jnp.float32,
    )
    query_grad = summed.reshape(local_queries, tokens_each, width).astype(jnp.bfloat16)
    page_share = lax.psum_scatter(
        page_terms.astype(jnp.bfloat16), "replica", scatter_dimension=0, tiled=True
    )
    return (query_grad, page_share[None])


def solution(mesh):
    placed = (
        P(("owner", "replica"), None, None),
        P("owner", None, None),
        P(("owner", "replica"), None),
        P(("owner", "replica")),
        P(("owner", "replica")),
        P(),
    )
    return jax.shard_map(
        shards,
        mesh=mesh,
        in_specs=placed,
        out_specs=(P(("owner", "replica"), None, None), P("owner", "replica", None)),
        check_vma=False,
    )
```

profile of v0, /device:TPU:1, one launch (start us, length us, event | category | flops | bytes accessed | tf_op | source)
XLA Modules:
  0.0 324.0 jit_solution(1860347391199224043)
XLA Ops:
  7.2 0.7 fusion.10
  8.0 0.8 select_reduce_fusion
  8.8 0.7 multiply_add_fusion
  9.5 0.7 convert_bitcast_fusion
  10.3 0.1 copy.18
  10.5 0.7 all_to_all.25
  11.2 16.3 %all-to-all-start.1 = ((bf16[128,1,4]{2,1,0:T(2,128)(2,1)}), bf16[128,1,4]{2,1,0:T(2,128)(2,1)S(1)}, u32[]{:S(2)}, u32[]{:S(2)}) async-start(bf16[128,1,4]{2,1,0:T(2,128)(2,1)} %all_to_all.25), calls=%async_computation.1 | async-start | bytes 131072 | tf_op jit(solution)/shard_map/all_to_all | solution.py:81
  27.5 1.7 convolution_convert_fusion.1
  29.3 7.6 %all_to_all.24 = bf16[128,1,8192]{2,1,0:T(2,128)(2,1)} reshape(bf16[256,4096]{1,0:T(8,128)(2,1)S(1)} %convolution_convert_fusion.1) | data formatting | bytes 4194304 | tf_op jit(solution)/shard_map/all_to_all | solution.py:74
  36.9 0.5 broadcast.65
  37.4 13.2 %reduce.6 = bf16[128,8192]{1,0:T(8,128)(2,1)S(1)} reduce(bf16[128,1,8192]{2,1,0:T(2,128)(2,1)} %all_to_all.24, bf16[]{:T(256)} %broadcast.65), dimensions={1}, to_apply=%all_to_all.24.reduce_sub_computation | reduce | bytes 4194306 | tf_op jit(solution)/shard_map/all_to_all | solution.py:74
  50.7 2.8 reshape.81
  53.5 13.4 %all-to-all-start = ((bf16[128,2,4096]{2,1,0:T(2,128)(2,1)}), bf16[128,2,4096]{2,1,0:T(2,128)(2,1)S(1)}, u32[]{:S(2)}, u32[]{:S(2)}) async-start(bf16[128,2,4096]{2,1,0:T(2,128)(2,1)} %reshape.81), calls=%async_computation | async-start | bytes 4194304 | tf_op jit(solution)/shard_map/all_to_all | solution.py:74
  66.9 0.7 fusion.14
  68.3 0.2 convert_reduce_fusion
  68.6 47.0 %all-to-all-done = bf16[128,2,4096]{2,1,0:T(2,128)(2,1)S(1)} async-done(((bf16[128,2,4096]{2,1,0:T(2,128)(2,1)}), bf16[128,2,4096]{2,1,0:T(2,128)(2,1)S(1)}, u32[]{:S(2)}, u32[]{:S(2)}) %all-to-all-start) | async-done | bytes 2097184 | tf_op jit(solution)/shard_map/all_to_all | solution.py:74
  115.7 6.8 %reshape.82 = bf16[128,1,8192]{2,1,0:T(2,128)(2,1)} reshape(bf16[128,2,4096]{2,1,0:T(2,128)(2,1)S(1)} %all-to-all-done) | data formatting | bytes 4194304
  122.4 13.9 %reduce = bf16[128,8192]{1,0:T(8,128)(2,1)} reduce(bf16[128,1,8192]{2,1,0:T(2,128)(2,1)} %reshape.82, bf16[]{:T(256)} %constant.88), dimensions={1}, to_apply=%all_to_all.19.reduce_sub_computation | reduce | bytes 4194306 | tf_op jit(solution)/shard_map/all_to_all | solution.py:74
  136.4 2.9 reshape_reshape.4
  139.3 67.9 %while.15 = (s32[]{:T(128)}, f32[1024,128]{1,0:T(8,128)S(1)}, bf16[4,64,32,128]{3,2,1,0:T(8,128)(2,1)}, bf16[4,64,32,128]{3,2,1,0:T(8,128)(2,1)S(1)}, bf16[1024,...) while((s32[]{:T(128)}, f32[1024,128]{1,0:T(8,128)S(1)}, ...), condition=%wide.region_7.8_spmd.clone, body=%wide.region_3.7_spmd.clone.sunk | while | flops 1632109056 | bytes 93449400 | solution.py:100
  139.3 1.3 multiply_reduce_fusion.2
  140.6 1.4 fusion.38
  142.0 1.8 copy-done
  144.2 4.4 %multiply_convert_fusion.2 = bf16[2048,1024]{0,1:T(8,128)(2,1)S(1)} fusion(f32[2048,1024]{0,1:T(8,128)} %copy-done, f32[2048]{0:T(1024)S(1)} %mul.103, f32[2048]{0:T(1024)S(1)} %fusion.38, f32[2048]{0:T(1024)S(1)} %get-tuple-element.209), kind=kLoop, calls=%fused_computation.clone.1 | loop fusion | flops 10485760 | bytes 12607488 | tf_op jit(solution)/shard_map/while/body/eval_jaxpr/convert_element_type | solution.py:28
  148.6 1.9 copy-done.1
  150.5 1.3 convolution_convert_fusion.6
  151.8 0.9 constant_dynamic-update-slice_fusion.2
  152.7 3.5 %convolution_add_fusion.2 = f32[1024,128]{1,0:T(8,128)S(1)} fusion(bf16[2048,1024]{0,1:T(8,128)(2,1)} %copy-done.1, bf16[2048,128]{1,0:T(8,128)(2,1)S(1)} %bitcast.56, f32[1024,128]{1,0:T(8,128)S(1)} %get-tuple-element.221, pred[]{:T(512)S(6)} %compare.4), kind=kOutput, calls=%fused_computation.5.clone.1 | convolution fusion | flops 537133056 | bytes 5767169 | tf_op jit(solution)/shard_map/while/body/eval_jaxpr/dot_general | solution.py:30
  156.3 1.3 multiply_reduce_fusion.2
  157.6 1.4 fusion.38
  159.0 1.8 copy-done
  161.2 4.4 %multiply_convert_fusion.2 = bf16[2048,1024]{0,1:T(8,128)(2,1)S(1)} fusion(f32[2048,1024]{0,1:T(8,128)} %copy-done, f32[2048]{0:T(1024)S(1)} %mul.103, f32[2048]{0:T(1024)S(1)} %fusion.38, f32[2048]{0:T(1024)S(1)} %get-tuple-element.209), kind=kLoop, calls=%fused_computation.clone.1 | loop fusion | flops 10485760 | bytes 12607488 | tf_op jit(solution)/shard_map/while/body/eval_jaxpr/convert_element_type | solution.py:28
  165.6 1.9 copy-done.1
  167.5 1.3 convolution_convert_fusion.6
  168.8 0.9 constant_dynamic-update-slice_fusion.2
  169.7 3.5 %convolution_add_fusion.2 = f32[1024,128]{1,0:T(8,128)S(1)} fusion(bf16[2048,1024]{0,1:T(8,128)(2,1)} %copy-done.1, bf16[2048,128]{1,0:T(8,128)(2,1)S(1)} %bitcast.56, f32[1024,128]{1,0:T(8,128)S(1)} %get-tuple-element.221, pred[]{:T(512)S(6)} %compare.4), kind=kOutput, calls=%fused_computation.5.clone.1 | convolution fusion | flops 537133056 | bytes 5767169 | tf_op jit(solution)/shard_map/while/body/eval_jaxpr/dot_general | solution.py:30
  173.3 1.3 multiply_reduce_fusion.2
  174.6 1.4 fusion.38
  176.0 1.8 copy-done
  178.2 4.4 %multiply_convert_fusion.2 = bf16[2048,1024]{0,1:T(8,128)(2,1)S(1)} fusion(f32[2048,1024]{0,1:T(8,128)} %copy-done, f32[2048]{0:T(1024)S(1)} %mul.103, f32[2048]{0:T(1024)S(1)} %fusion.38, f32[2048]{0:T(1024)S(1)} %get-tuple-element.209), kind=kLoop, calls=%fused_computation.clone.1 | loop fusion | flops 10485760 | bytes 12607488 | tf_op jit(solution)/shard_map/while/body/eval_jaxpr/convert_element_type | solution.py:28
  182.6 1.9 copy-done.1
  184.5 1.3 convolution_convert_fusion.6
  185.8 0.8 constant_dynamic-update-slice_fusion.2
  186.7 3.5 %convolution_add_fusion.2 = f32[1024,128]{1,0:T(8,128)S(1)} fusion(bf16[2048,1024]{0,1:T(8,128)(2,1)} %copy-done.1, bf16[2048,128]{1,0:T(8,128)(2,1)S(1)} %bitcast.56, f32[1024,128]{1,0:T(8,128)S(1)} %get-tuple-element.221, pred[]{:T(512)S(6)} %compare.4), kind=kOutput, calls=%fused_computation.5.clone.1 | convolution fusion | flops 537133056 | bytes 5767169 | tf_op jit(solution)/shard_map/while/body/eval_jaxpr/dot_general | solution.py:30
  190.3 1.3 multiply_reduce_fusion.2
  191.5 1.4 fusion.38
  192.9 1.8 copy-done
  195.1 4.4 %multiply_convert_fusion.2 = bf16[2048,1024]{0,1:T(8,128)(2,1)S(1)} fusion(f32[2048,1024]{0,1:T(8,128)} %copy-done, f32[2048]{0:T(1024)S(1)} %mul.103, f32[2048]{0:T(1024)S(1)} %fusion.38, f32[2048]{0:T(1024)S(1)} %get-tuple-element.209), kind=kLoop, calls=%fused_computation.clone.1 | loop fusion | flops 10485760 | bytes 12607488 | tf_op jit(solution)/shard_map/while/body/eval_jaxpr/convert_element_type | solution.py:28
  199.6 1.9 copy-done.1
  201.5 1.3 convolution_convert_fusion.6
  202.8 0.8 constant_dynamic-update-slice_fusion.2
  203.6 3.5 %convolution_add_fusion.2 = f32[1024,128]{1,0:T(8,128)S(1)} fusion(bf16[2048,1024]{0,1:T(8,128)(2,1)} %copy-done.1, bf16[2048,128]{1,0:T(8,128)(2,1)S(1)} %bitcast.56, f32[1024,128]{1,0:T(8,128)S(1)} %get-tuple-element.221, pred[]{:T(512)S(6)} %compare.4), kind=kOutput, calls=%fused_computation.5.clone.1 | convolution fusion | flops 537133056 | bytes 5767169 | tf_op jit(solution)/shard_map/while/body/eval_jaxpr/dot_general | solution.py:30
  207.1 10.0 %all_to_all.26 = bf16[128,1,8192]{2,1,0:T(2,128)(2,1)} reshape(bf16[4,64,32,128]{3,2,1,0:T(8,128)(2,1)} %get-tuple-element.92) | data formatting | bytes 4194304 | tf_op jit(solution)/shard_map/all_to_all | solution.py:109
  217.2 13.2 %reduce.7 = bf16[128,8192]{1,0:T(8,128)(2,1)S(1)} reduce(bf16[128,1,8192]{2,1,0:T(2,128)(2,1)} %all_to_all.26, bf16[]{:T(256)} %broadcast.65), dimensions={1}, to_apply=%all_to_all.26.reduce_sub_computation | reduce | bytes 4194306 | tf_op jit(solution)/shard_map/all_to_all | solution.py:109
  230.4 2.8 reshape.83
  233.2 10.1 %all-to-all-start.2 = ((bf16[128,2,4096]{2,1,0:T(2,128)(2,1)}), bf16[128,2,4096]{2,1,0:T(2,128)(2,1)S(1)}, u32[]{:S(2)}, u32[]{:S(2)}) async-start(bf16[128,2,4096]{2,1,0:T(2,128)(2,1)} %reshape.83), calls=%async_computation.2 | async-start | bytes 4194304 | tf_op jit(solution)/shard_map/all_to_all | solution.py:109
  243.3 0.7 convert_element_type.60
  244.1 48.2 %all-to-all-done.2 = bf16[128,2,4096]{2,1,0:T(2,128)(2,1)S(1)} async-done(((bf16[128,2,4096]{2,1,0:T(2,128)(2,1)}), bf16[128,2,4096]{2,1,0:T(2,128)(2,1)S(1)}, u32[]{:S(2)}, u32[]{:S(2)}) %all-to-all-start.2) | async-done | bytes 2097184 | tf_op jit(solution)/shard_map/all_to_all | solution.py:109
  292.3 6.8 %reshape.84 = bf16[128,1,8192]{2,1,0:T(2,128)(2,1)} reshape(bf16[128,2,4096]{2,1,0:T(2,128)(2,1)S(1)} %all-to-all-done.2) | data formatting | bytes 4194304
  299.1 12.6 %reduce.2 = bf16[128,8192]{1,0:T(8,128)(2,1)S(1)} reduce(bf16[128,1,8192]{2,1,0:T(2,128)(2,1)} %reshape.84, bf16[]{:T(256)} %constant.88), dimensions={1}, to_apply=%all_to_all.23.reduce_sub_computation | reduce | bytes 4194306 | tf_op jit(solution)/shard_map/all_to_all | solution.py:109
  311.7 2.2 reshape.69
  313.9 2.1 fusion.2
  316.0 0.5 fusion.1
  316.5 0.6 copy.22
  (56 shorter events, 2.1 us)
Async XLA Ops:
  11.2 42.3 %all-to-all-start.1 = ((bf16[128,1,4]{2,1,0:T(2,128)(2,1)}), bf16[128,1,4]{2,1,0:T(2,128)(2,1)S(1)}, u32[]{:S(2)}, u32[]{:S(2)}) async-start(bf16[128,1,4]{2,1,0:T(2,128)(2,1)} %all_to_all.25), calls=%async_computation.1 | async-start | bytes 131072 | tf_op jit(solution)/shard_map/all_to_all | solution.py:81
  50.6 16.3 %copy-start.4 = (s32[2]{0:T(128)S(1)}, s32[2]{0:T(128)}, u32[]{:S(2)}) copy-start(s32[2]{0:T(128)} %param.13) | copy-start | bytes 28
  53.5 62.2 %all-to-all-start = ((bf16[128,2,4096]{2,1,0:T(2,128)(2,1)}), bf16[128,2,4096]{2,1,0:T(2,128)(2,1)S(1)}, u32[]{:S(2)}, u32[]{:S(2)}) async-start(bf16[128,2,4096]{2,1,0:T(2,128)(2,1)} %reshape.81), calls=%async_computation | async-start | bytes 4194304 | tf_op jit(solution)/shard_map/all_to_all | solution.py:74
  122.4 16.8 %copy-start.2 = (bf16[1,1024,128]{2,1,0:T(8,128)(2,1)S(1)}, bf16[1,1024,128]{2,1,0:T(8,128)(2,1)}, u32[]{:S(2)}) copy-start(bf16[1,1024,128]{2,1,0:T(8,128)(2,1)} %param.9) | copy-start | bytes 786436
  140.6 3.2 copy-start
  148.6 1.9 copy-start.1
  157.6 3.2 copy-start
  165.6 1.9 copy-start.1
  174.6 3.2 copy-start
  182.6 1.9 copy-start.1
  191.5 3.2 copy-start
  199.5 1.9 copy-start.1
  233.2 59.1 %all-to-all-start.2 = ((bf16[128,2,4096]{2,1,0:T(2,128)(2,1)}), bf16[128,2,4096]{2,1,0:T(2,128)(2,1)S(1)}, u32[]{:S(2)}, u32[]{:S(2)}) async-start(bf16[128,2,4096]{2,1,0:T(2,128)(2,1)} %reshape.83), calls=%async_computation.2 | async-start | bytes 4194304 | tf_op jit(solution)/shard_map/all_to_all | solution.py:109
  243.3 73.9 %reduce-scatter.2.cloned.1.call-start = ((), (), s32[]{:S(2)}) async-start(), calls=%async_computation.4 | async-start | bytes 393216 | tf_op jit(solution)/shard_map/reduce_scatter | solution.py:130
  311.7 4.4 %copy-start.3 = (s32[64]{0:T(128)S(1)}, s32[64]{0:T(128)}, u32[]{:S(2)}) copy-start(s32[64]{0:T(128)} %param.11) | copy-start | bytes 772
Sparse Core Ops, SparseCore 0:
  247.2 15.7 reduce-scatter.1
where the time goes:
time: 327 us; the launch traced here: 324 us
  waiting for transfers between devices  95.3 us (29%)
  other arithmetic  81.3 us (25%)
  local copies, waits for them, and re-layouts  63.6 us (19%)
  starting transfers between devices  39.9 us (12%)
  matrix products  28.8 us (9%)
  between operations  14.9 us (5%)
    all_to_all x1, waiting for transfers between devices, shards(): lax.all_to_all(slot_grads.reshape(owners, capacity * tokens_each * width)...  48.2 us
    all_to_all x1, waiting for transfers between devices, shards(): lax.all_to_all(send_tokens.reshape(owners, capacity * tokens_each * width...  47 us
    all_to_all x2, other arithmetic, shards(): lax.all_to_all(send_tokens.reshape(owners, capacity * tokens_each * width...  27.1 us
    all_to_all x2, other arithmetic, shards(): lax.all_to_all(slot_grads.reshape(owners, capacity * tokens_each * width)...  25.8 us
    unnamed x12, local copies, waits for them, and re-layouts  19.9 us
    convert_element_type x4, other arithmetic, score_block(): weight = (expo / totals * slope_rows).astype(jnp.bfloat16)  17.6 us
    all_to_all x1, starting transfers between devices, shards(): lax.all_to_all(send_flags.reshape(owners, capacity * 2), 'owner', split_a...  16.3 us
    while x16, local copies, waits for them, and re-layouts  14.9 us
  transfers between devices with their start and end apart: 4, of which 2 were waited for; matrix products, arithmetic and copies ran while one was open for 14% of the time, Pallas kernels for 0%

commit v1 on v0

v1 whole, which is shorter than its diff:
```python
import functools
import math

import jax
import jax.numpy as jnp
from jax import lax
from jax.experimental import pallas as pl
from jax.experimental.pallas import tpu as pltpu
from jax.sharding import Mesh, PartitionSpec as P

SHARPNESS = 4.0
SLOPE_SCALE = 0.5
HOT_SHIFT = 2.0

NX, NZ, NY, NC = 4, 8, 4, 2
PLANE = NX * NY
QT = 32
W = 128
Q_DEV = 8
PAIR_DEV = 64
PATCHES = 1024
HALF = PATCHES // 2
CAP = 2
ROWS = Q_DEV * QT
SEND_ROWS = ROWS + 16
ENTRIES = NZ * CAP
GROUP = 8
SLOTS = PLANE * CAP
LIST = SLOTS + GROUP


def pack_kernel(page_ref, query_ref, label_ref, rows_ref, out_ref):
    dest = lax.broadcasted_iota(jnp.int32, (PLANE, W), 0)
    lane = lax.broadcasted_iota(jnp.int32, (PLANE, W), 1)
    entry = lane % ENTRIES
    rank = entry % CAP
    wanted = (dest // NY) * (NZ * NY) + (entry // CAP) * NY + dest % NY
    is_query = lane < ENTRIES
    is_label = jnp.logical_and(lane >= ENTRIES, lane < 2 * ENTRIES)

    def visit(i, carry):
        table, seen = carry
        hit = wanted == page_ref[i]
        value = jnp.where(is_query, query_ref[i] + 1, jnp.where(is_label, label_ref[i], 0))
        table = jnp.where(jnp.logical_and(hit, seen == rank), value, table)
        return table, seen + hit.astype(jnp.int32)

    zeros = jnp.zeros((PLANE, W), jnp.int32)
    table, _ = lax.fori_loop(0, PAIR_DEV, visit, (zeros, zeros), unroll=8)
    table = table.astype(jnp.float32)
    rows = rows_ref[...]
    for d in range(PLANE):
        out_ref[d, :ROWS, :] = rows
        out_ref[d, ROWS:, :] = jnp.broadcast_to(table[d : d + 1, :], (16, W)).astype(jnp.bfloat16)


def score_kernel(
    offset, place_ref, hot_ref, table_ref, got_ref, mine_ref, other_ref,
    query_out, mine_out, other_out,
    slot_query, slot_label, tokens, expo, query_acc, mine_acc, other_acc,
):
    rows = GROUP * QT
    query_acc[...] = jnp.zeros_like(query_acc)
    first_page = place_ref[0]

    def per_page(page, _):
        page_id = first_page + page * NY
        hot = jnp.logical_or(hot_ref[0] == page_id, hot_ref[1] == page_id)
        shift = jnp.where(hot, HOT_SHIFT, 0.0).astype(jnp.float32)

        count = jnp.int32(0)
        for s in range(PLANE):
            for r in range(CAP):
                code = table_ref[s, page * CAP + r]
                slot_query[count] = s * Q_DEV + code - 1
                slot_label[count] = table_ref[s, ENTRIES + page * CAP + r]
                count = count + (code > 0).astype(jnp.int32)
        for g in range(GROUP - 1):
            slot_query[count + g] = 0
            slot_label[count + g] = 0

        mine_acc[...] = jnp.zeros_like(mine_acc)
        other_acc[...] = jnp.zeros_like(other_acc)
        mine = mine_ref.at[page]
        other = other_ref.at[page]

        def per_group(step, _):
            base = step * GROUP
            for g in range(GROUP):
                q = slot_query[base + g]
                src = q // Q_DEV
                tokens[g * QT : (g + 1) * QT, :] = got_ref[
                    src, pl.ds(pl.multiple_of((q % Q_DEV) * QT, QT), QT), :
                ]
            tok = tokens[...]
            dims = (((1,), (1,)), ((), ()))
            la = lax.dot_general(tok, mine[...], dims, preferred_element_type=jnp.float32)
            lb = lax.dot_general(tok, other[...], dims, preferred_element_type=jnp.float32)
            peak = jnp.maximum(
                jnp.max(la, axis=1, keepdims=True), jnp.max(lb, axis=1, keepdims=True)
            )
            ea = jnp.exp(SHARPNESS * (la - peak))
            eb = jnp.exp(SHARPNESS * (lb - peak))
            totals = jnp.sum(ea, axis=1, keepdims=True) + jnp.sum(eb, axis=1, keepdims=True)
            expo[:, :HALF] = ea.astype(jnp.bfloat16)
            expo[:, HALF:] = eb.astype(jnp.bfloat16)
            lse = SHARPNESS * peak + jnp.log(totals)
            scales = []
            for g in range(GROUP):
                score = jnp.sum(lse[g * QT : (g + 1) * QT], axis=0, keepdims=True) / SHARPNESS
                logit = SLOPE_SCALE * score + offset - shift
                label = slot_label[base + g].astype(jnp.float32)
                live = jnp.where(base + g < count, SLOPE_SCALE, 0.0)
                slope = live * (1.0 / (1.0 + jnp.exp(-logit)) - label)
                scales.append(slope / totals[g * QT : (g + 1) * QT])
            scale = jnp.concatenate(scales, axis=0)
            weight = expo[...]
            grads = jnp.dot(weight[:, :HALF], mine[...], preferred_element_type=jnp.float32)
            grads += jnp.dot(weight[:, HALF:], other[...], preferred_element_type=jnp.float32)
            grads = grads * scale
            scaled = (tok.astype(jnp.float32) * scale).astype(jnp.bfloat16)
            dims = (((0,), (0,)), ((), ()))
            mine_acc[...] += lax.dot_general(
                weight[:, :HALF], scaled, dims, preferred_element_type=jnp.float32
            )
            other_acc[...] += lax.dot_general(
                weight[:, HALF:], scaled, dims, preferred_element_type=jnp.float32
            )
            for g in range(GROUP):
                at = pl.ds(pl.multiple_of(slot_query[base + g] * QT, QT), QT)
                query_acc[at, :] += grads[g * QT : (g + 1) * QT]
            return 0

        lax.fori_loop(0, (count + GROUP - 1) // GROUP, per_group, 0)
        mine_out[page] = mine_acc[...].astype(jnp.bfloat16)
        other_out[page] = other_acc[...].astype(jnp.bfloat16)
        return 0

    lax.fori_loop(0, NZ, per_page, 0)
    query_out[...] = query_acc[...].astype(jnp.bfloat16)


def exchange(array, axes):
    return lax.all_to_all(array, axes, split_axis=0, concat_axis=0, tiled=True)


def swap_cores(array):
    return lax.ppermute(array, "core", [(0, 1), (1, 0)])


def shards(queries, pages, pair_page, pair_query, pair_label, hot_pages):
    offset = -SLOPE_SCALE * QT * (math.log(PATCHES) / SHARPNESS + SHARPNESS / 2.0)
    smem = pl.BlockSpec(memory_space=pltpu.SMEM)
    vmem = pl.BlockSpec(memory_space=pltpu.VMEM)
    send = pl.pallas_call(
        pack_kernel,
        out_shape=jax.ShapeDtypeStruct((PLANE, SEND_ROWS, W), jnp.bfloat16),
        in_specs=[smem, smem, smem, vmem],
        out_specs=vmem,
    )(pair_page[:, 0], pair_query, pair_label, queries.reshape(ROWS, W))
    core = lax.axis_index("core")
    half = lax.dynamic_slice(pages[0], (core * HALF, 0), (HALF, W))
    mine = exchange(jnp.broadcast_to(half[None], (NZ, HALF, W)), "z")
    other = swap_cores(mine)
    got = exchange(send, ("x", "y"))
    table = got[:, ROWS, : 2 * ENTRIES].astype(jnp.int32)
    place = (lax.axis_index("x") * (NZ * NY) + lax.axis_index("y")).reshape(1)
    query_part, mine_part, other_part = pl.pallas_call(
        functools.partial(score_kernel, offset),
        out_shape=(
            jax.ShapeDtypeStruct((PLANE * ROWS, W), jnp.bfloat16),
            jax.ShapeDtypeStruct((NZ, HALF, W), jnp.bfloat16),
            jax.ShapeDtypeStruct((NZ, HALF, W), jnp.bfloat16),
        ),
        in_specs=[smem, smem, smem, vmem, vmem, vmem],
        out_specs=(vmem, vmem, vmem),
        scratch_shapes=[
            pltpu.SMEM((LIST,), jnp.int32),
            pltpu.SMEM((LIST,), jnp.int32),
            pltpu.VMEM((GROUP * QT, W), jnp.bfloat16),
            pltpu.VMEM((GROUP * QT, PATCHES), jnp.bfloat16),
            pltpu.VMEM((PLANE * ROWS, W), jnp.float32),
            pltpu.VMEM((HALF, W), jnp.float32),
            pltpu.VMEM((HALF, W), jnp.float32),
        ],
        compiler_params=pltpu.CompilerParams(vmem_limit_bytes=48 << 20),
    )(place, hot_pages, table, got, mine, other)
    page_terms = mine_part.astype(jnp.float32) + swap_cores(other_part).astype(jnp.float32)
    page_back = exchange(page_terms.astype(jnp.bfloat16), "z")
    query_back = exchange(query_part.reshape(PLANE, ROWS, W), ("x", "y"))
    query_grad = jnp.sum(query_back.astype(jnp.float32), axis=0).astype(jnp.bfloat16)
    page_grad = jnp.sum(page_back.astype(jnp.float32), axis=0).astype(jnp.bfloat16)
    return query_grad.reshape(Q_DEV, QT, W), page_grad[None]


def solution(mesh):
    torus = Mesh(mesh.devices.reshape(NX, NZ, NY, NC), ("x", "z", "y", "core"))
    owner = ("x", "z", "y")
    device = ("x", "z", "y", "core")
    return jax.shard_map(
        shards,
        mesh=torus,
        in_specs=(P(device), P(owner), P(device), P(device), P(device), P()),
        out_specs=(P(device), P(owner, "core")),
        check_vma=False,
    )
```

time: 327 us -> 139 us (0.43)
  other arithmetic: 81.3 us -> 3.66 us
  local copies, waits for them, and re-layouts: 63.6 us -> 3.02 us
  matrix products: 28.8 us -> 0 us
  Pallas kernels: 0 us -> 15.8 us
  between operations: 14.9 us -> 0.7 us
  starting transfers between devices: 39.9 us -> 29.6 us
  waiting for transfers between devices: 95.3 us -> 86.5 us
    all_to_all x4 -> x0, other arithmetic: 53 us -> none  [the longest x2 27.1 us: shards(): lax.all_to_all(send_tokens.reshape(owners, capacity * tokens_each * width...]
    dot_general x16 -> x0, matrix products: 28.8 us -> none  [the longest x4 14 us: score_block(): lax.dot_general(weight, flat_rows, (((0,), (0,)), ((), ())), preferred_el...]
    all_to_all x4 -> x0, local copies, waits for them, and re-layouts: 18.9 us -> none  [the longest x1 10 us: shards(): lax.all_to_all(slot_grads.reshape(owners, capacity * tokens_each * width)...]
    unnamed x12 -> x6, local copies, waits for them, and re-layouts: 19.9 us -> 1.91 us
    convert_element_type x7 -> x2, other arithmetic: 19.2 us -> 2.07 us  [the longest x1 1.3 us: shards(): page_back = exchange(page_terms.astype(jnp.bfloat16), 'z')]
    pallas_call x0 -> x2, Pallas kernels: none -> 15.8 us  [the longest x1 13.6 us: shards(): pl.pallas_call(functools.partial(score_kernel, offset), out_shape=(jax.Sh...]
    all_to_all x3 -> x4, starting transfers between devices: 39.9 us -> 24.5 us  [exchange(): return lax.all_to_all(array, axes, split_axis=0, concat_axis=0, tiled=True)]
    while x16 -> x0, local copies, waits for them, and re-layouts: 14.9 us -> none
  transfers between devices with their start and end apart: 4 -> 6, of which waited for: 2 -> 4; matrix products, arithmetic and copies ran while one was open for 14% -> 2% of each run, Pallas kernels for 0% -> 2%
where the time goes in v1:
time: 139 us
  waiting for transfers between devices  86.5 us (62%)
  starting transfers between devices  29.6 us (21%)
  Pallas kernels  15.8 us (11%)
  other arithmetic  3.66 us (3%)
  local copies, waits for them, and re-layouts  3.02 us (2%)
    all_to_all x4, waiting for transfers between devices, exchange(): return lax.all_to_all(array, axes, split_axis=0, concat_axis=0, tiled=True)  86.5 us
    all_to_all x4, starting transfers between devices, exchange(): return lax.all_to_all(array, axes, split_axis=0, concat_axis=0, tiled=True)  24.5 us
    pallas_call x1, Pallas kernels, shards(): pl.pallas_call(functools.partial(score_kernel, offset), out_shape=(jax.Sh...  13.6 us
    ppermute x2, starting transfers between devices, swap_cores(): return lax.ppermute(array, 'core', [(0, 1), (1, 0)])  5.09 us
  transfers between devices with their start and end apart: 6, of which 4 were waited for; matrix products, arithmetic and copies ran while one was open for 2% of the time, Pallas kernels for 2%

profile of v1, /device:TPU:1, one launch (start us, length us, event | category | flops | bytes accessed | tf_op | source)
XLA Modules:
  0.0 139.2 jit_solution(12214734638010408546)
XLA Ops:
  0.6 0.0 copy-start
  0.6 0.9 copy-done
  1.6 1.1 broadcast_in_dim.12
  2.7 9.0 %all-to-all-start.1 = ((bf16[8,512,128]{2,1,0:T(8,128)(2,1)}), bf16[8,512,128]{2,1,0:T(8,128)(2,1)S(1)}, u32[]{:S(2)}, u32[]{:S(2)}) async-start(bf16[8,512,128]{2,1,0:T(8,128)(2,1)} %broadcast_in_dim.12), calls=%async_computation.1 | async-start | bytes 2097152 | tf_op jit(solution)/shard_map/all_to_all | solution.py:144
  11.7 2.2 %shard_map.77 = bf16[16,272,128]{2,1,0:T(8,128)(2,1)} custom-call(s32[64]{0:T(128)} %bitcast.14, s32[64]{0:T(128)} %query_ref.1, s32[64]{0:T(128)} %label_ref.1, bf16[256,128]{1,0:T(8,128)(2,1)} %bitcast.12), custom_call_target="tpu_custom_call" | custom-call | tf_op jit(solution)/shard_map/pallas_call | solution.py:155
  13.9 0.0 copy-start.2
  13.9 27.0 %all-to-all-done.1.mine_ref = bf16[8,512,128]{2,1,0:T(8,128)(2,1)S(1)} async-done(((bf16[8,512,128]{2,1,0:T(8,128)(2,1)}), bf16[8,512,128]{2,1,0:T(8,128)(2,1)S(1)}, u32[]{:S(2)}, u32[]{:S(2)}) %all-to-all-start.1) | async-done | bytes 1048608 | tf_op jit(solution)/shard_map/all_to_all | solution.py:144
  40.9 6.8 %all-to-all-start = ((bf16[16,272,128]{2,1,0:T(8,128)(2,1)}), bf16[16,272,128]{2,1,0:T(8,128)(2,1)}, u32[]{:S(2)}, u32[]{:S(2)}) async-start(bf16[16,272,128]{2,1,0:T(8,128)(2,1)} %shard_map.77), calls=%async_computation | async-start | bytes 2228224 | tf_op jit(solution)/shard_map/all_to_all | solution.py:144
  47.7 0.9 collective-permute-start
  48.6 15.5 %all-to-all-done.got_ref = bf16[16,272,128]{2,1,0:T(8,128)(2,1)} async-done(((bf16[16,272,128]{2,1,0:T(8,128)(2,1)}), bf16[16,272,128]{2,1,0:T(8,128)(2,1)}, u32[]{:S(2)}, u32[]{:S(2)}) %all-to-all-start) | async-done | bytes 1114144 | tf_op jit(solution)/shard_map/all_to_all | solution.py:144
  64.0 0.8 slice_convert_fusion
  64.8 0.0 collective-permute-done.other_ref
  64.8 0.0 copy-done.2
  64.8 13.6 %shard_map.78 = (bf16[4096,128]{1,0:T(8,128)(2,1)S(1)}, bf16[8,512,128]{2,1,0:T(8,128)(2,1)S(1)}, bf16[8,512,128]{2,1,0:T(8,128)(2,1)}) custom-call(s32[1]{0:T(128)} %bitcast.place_ref, s32[2]{0:T(128)S(1)} %copy-done.2, s32[16,32]{1,0:T(8,128)S(1)} %bitcast.10, bf16[16,272,128]{2,1,0:T(8,128)(2,1)} %all-to-all-done.got_ref, ...), custom_call_target="tpu_custom_call" | custom-call | tf_op jit(solution)/shard_map/pallas_call | solution.py:168
  78.4 0.0 copy-start.1
  78.4 1.0 copy-done.1
  79.4 4.2 %collective-permute-start.1 = (bf16[8,512,128]{2,1,0:T(8,128)(2,1)}, bf16[8,512,128]{2,1,0:T(8,128)(2,1)S(1)}, u32[]{:S(2)}, u32[]{:S(2)}) collective-permute-start(bf16[8,512,128]{2,1,0:T(8,128)(2,1)} %get-tuple-element.7), channel_id=1, source_target_pairs={{0,1},{1,0},{2,3},{3,2},{4,5},{5,4},{6,7},{7,6},{8,9},{9,8},{10,11... | collective-permute-start | bytes 3145736 | tf_op jit(solution)/shard_map/ppermute | solution.py:148
  83.6 5.1 %all-to-all-start.2 = ((bf16[16,256,128]{2,1,0:T(8,128)(2,1)}), bf16[16,256,128]{2,1,0:T(8,128)(2,1)S(1)}, u32[]{:S(2)}, u32[]{:S(2)}) async-start(bf16[16,256,128]{2,1,0:T(8,128)(2,1)} %bitcast.9), calls=%async_computation.2 | async-start | bytes 2097152 | tf_op jit(solution)/shard_map/all_to_all | solution.py:144
  88.7 0.0 collective-permute-done.1
  88.7 1.3 add_convert_fusion
  90.0 15.7 %all-to-all-done.2 = bf16[16,256,128]{2,1,0:T(8,128)(2,1)S(1)} async-done(((bf16[16,256,128]{2,1,0:T(8,128)(2,1)}), bf16[16,256,128]{2,1,0:T(8,128)(2,1)S(1)}, u32[]{:S(2)}, u32[]{:S(2)}) %all-to-all-start.2) | async-done | bytes 1048608 | tf_op jit(solution)/shard_map/all_to_all | solution.py:144
  105.7 3.6 %all-to-all-start.3 = ((bf16[8,512,128]{2,1,0:T(8,128)(2,1)}), bf16[8,512,128]{2,1,0:T(8,128)(2,1)S(1)}, u32[]{:S(2)}, u32[]{:S(2)}) async-start(bf16[8,512,128]{2,1,0:T(8,128)(2,1)} %add_convert_fusion), calls=%async_computation.3 | async-start | bytes 2097152 | tf_op jit(solution)/shard_map/all_to_all | solution.py:144
  109.3 0.8 reduce_sum.24
  110.1 28.3 %all-to-all-done.3 = bf16[8,512,128]{2,1,0:T(8,128)(2,1)S(1)} async-done(((bf16[8,512,128]{2,1,0:T(8,128)(2,1)}), bf16[8,512,128]{2,1,0:T(8,128)(2,1)S(1)}, u32[]{:S(2)}, u32[]{:S(2)}) %all-to-all-start.3) | async-done | bytes 1048608 | tf_op jit(solution)/shard_map/all_to_all | solution.py:144
  138.4 0.8 reduce_sum.25
  (1 shorter events, 0.0 us)
Async XLA Ops:
  0.6 1.0 copy-start
  2.7 38.2 %all-to-all-start.1 = ((bf16[8,512,128]{2,1,0:T(8,128)(2,1)}), bf16[8,512,128]{2,1,0:T(8,128)(2,1)S(1)}, u32[]{:S(2)}, u32[]{:S(2)}) async-start(bf16[8,512,128]{2,1,0:T(8,128)(2,1)} %broadcast_in_dim.12), calls=%async_computation.1 | async-start | bytes 2097152 | tf_op jit(solution)/shard_map/all_to_all | solution.py:144
  13.9 50.9 %copy-start.2 = (s32[2]{0:T(128)S(1)}, s32[2]{0:T(128)}, u32[]{:S(2)}) copy-start(s32[2]{0:T(128)} %hot_ref.1) | copy-start | bytes 28
  40.9 23.1 %all-to-all-start = ((bf16[16,272,128]{2,1,0:T(8,128)(2,1)}), bf16[16,272,128]{2,1,0:T(8,128)(2,1)}, u32[]{:S(2)}, u32[]{:S(2)}) async-start(bf16[16,272,128]{2,1,0:T(8,128)(2,1)} %shard_map.77), calls=%async_computation | async-start | bytes 2228224 | tf_op jit(solution)/shard_map/all_to_all | solution.py:144
  47.7 17.1 %collective-permute-start = (bf16[8,512,128]{2,1,0:T(8,128)(2,1)S(1)}, bf16[8,512,128]{2,1,0:T(8,128)(2,1)S(1)}, u32[]{:S(2)}, u32[]{:S(2)}) collective-permute-start(bf16[8,512,128]{2,1,0:T(8,128)(2,1)S(1)} %all-to-all-done.1.mine_ref), channel_id=1, source_target_pairs={{0,1},{1,0},{2,3},{3,2},{4,5},{5,4},{6,7},{7,6},{8,9},{9,8},{10,11... | collective-permute-start | bytes 3145736 | tf_op jit(solution)/shard_map/ppermute | solution.py:148
  78.4 1.0 copy-start.1
  79.4 9.4 %collective-permute-start.1 = (bf16[8,512,128]{2,1,0:T(8,128)(2,1)}, bf16[8,512,128]{2,1,0:T(8,128)(2,1)S(1)}, u32[]{:S(2)}, u32[]{:S(2)}) collective-permute-start(bf16[8,512,128]{2,1,0:T(8,128)(2,1)} %get-tuple-element.7), channel_id=1, source_target_pairs={{0,1},{1,0},{2,3},{3,2},{4,5},{5,4},{6,7},{7,6},{8,9},{9,8},{10,11... | collective-permute-start | bytes 3145736 | tf_op jit(solution)/shard_map/ppermute | solution.py:148
  83.6 22.1 %all-to-all-start.2 = ((bf16[16,256,128]{2,1,0:T(8,128)(2,1)}), bf16[16,256,128]{2,1,0:T(8,128)(2,1)S(1)}, u32[]{:S(2)}, u32[]{:S(2)}) async-start(bf16[16,256,128]{2,1,0:T(8,128)(2,1)} %bitcast.9), calls=%async_computation.2 | async-start | bytes 2097152 | tf_op jit(solution)/shard_map/all_to_all | solution.py:144
  105.7 32.7 %all-to-all-start.3 = ((bf16[8,512,128]{2,1,0:T(8,128)(2,1)}), bf16[8,512,128]{2,1,0:T(8,128)(2,1)S(1)}, u32[]{:S(2)}, u32[]{:S(2)}) async-start(bf16[8,512,128]{2,1,0:T(8,128)(2,1)} %add_convert_fusion), calls=%async_computation.3 | async-start | bytes 2097152 | tf_op jit(solution)/shard_map/all_to_all | solution.py:144

commit v2 on v1

--- a/solution.py
+++ b/solution.py
@@ -27,6 +27,7 @@
 GROUP = 8
 SLOTS = PLANE * CAP
 LIST = SLOTS + GROUP
+STEPS = (0, -1, 1, 4, -2, 3, 2, -3)
 
 
 def pack_kernel(page_ref, query_ref, label_ref, rows_ref, out_ref):
@@ -55,25 +56,26 @@
 
 
 def score_kernel(
-    offset, place_ref, hot_ref, table_ref, got_ref, mine_ref, other_ref,
+    offset, column_ref, hot_ref, table_ref, got_ref, mine_ref, other_ref,
     query_out, mine_out, other_out,
     slot_query, slot_label, tokens, expo, query_acc, mine_acc, other_acc,
 ):
     rows = GROUP * QT
     query_acc[...] = jnp.zeros_like(query_acc)
-    first_page = place_ref[0]
+    first_page = column_ref[NZ]
 
     def per_page(page, _):
-        page_id = first_page + page * NY
+        height = column_ref[page]
+        page_id = first_page + height * NY
         hot = jnp.logical_or(hot_ref[0] == page_id, hot_ref[1] == page_id)
         shift = jnp.where(hot, HOT_SHIFT, 0.0).astype(jnp.float32)
 
         count = jnp.int32(0)
         for s in range(PLANE):
             for r in range(CAP):
-                code = table_ref[s, page * CAP + r]
+                code = table_ref[s, height * CAP + r]
                 slot_query[count] = s * Q_DEV + code - 1
-                slot_label[count] = table_ref[s, ENTRIES + page * CAP + r]
+                slot_label[count] = table_ref[s, ENTRIES + height * CAP + r]
                 count = count + (code > 0).astype(jnp.int32)
         for g in range(GROUP - 1):
             slot_query[count + g] = 0
@@ -148,23 +150,49 @@
     return lax.ppermute(array, "core", [(0, 1), (1, 0)])
 
 
+def move(array, step):
+    return lax.ppermute(array, "z", [(i, (i + step) % NZ) for i in range(NZ)])
+
+
+def gather_column(half):
+    below, above, across = move(half, 1), move(half, -1), move(half, 4)
+    far_below = move(jnp.stack([below, across]), 1)
+    far_above = move(jnp.stack([above, across]), -1)
+    return jnp.concatenate([jnp.stack([half, below, above, across]), far_below, far_above])
+
+
+def reduce_column(terms):
+    sent = terms.astype(jnp.bfloat16)
+    from_below, from_above = move(sent[6:8], 1), move(sent[4:6], -1)
+    up = (terms[2] + from_below[0].astype(jnp.float32)).astype(jnp.bfloat16)
+    down = (terms[1] + from_above[0].astype(jnp.float32)).astype(jnp.bfloat16)
+    over = terms[3] + from_below[1].astype(jnp.float32) + from_above[1].astype(jnp.float32)
+    over = over.astype(jnp.bfloat16)
+    total = terms[0]
+    for part in (move(up, 1), move(down, -1), move(over, 4)):
+        total = total + part.astype(jnp.float32)
+    return total.astype(jnp.bfloat16)
+
+
 def shards(queries, pages, pair_page, pair_query, pair_label, hot_pages):
     offset = -SLOPE_SCALE * QT * (math.log(PATCHES) / SHARPNESS + SHARPNESS / 2.0)
     smem = pl.BlockSpec(memory_space=pltpu.SMEM)
     vmem = pl.BlockSpec(memory_space=pltpu.VMEM)
+    core = lax.axis_index("core")
+    half = lax.dynamic_slice(pages[0], (core * HALF, 0), (HALF, W))
     send = pl.pallas_call(
         pack_kernel,
         out_shape=jax.ShapeDtypeStruct((PLANE, SEND_ROWS, W), jnp.bfloat16),
         in_specs=[smem, smem, smem, vmem],
         out_specs=vmem,
     )(pair_page[:, 0], pair_query, pair_label, queries.reshape(ROWS, W))
-    core = lax.axis_index("core")
-    half = lax.dynamic_slice(pages[0], (core * HALF, 0), (HALF, W))
-    mine = exchange(jnp.broadcast_to(half[None], (NZ, HALF, W)), "z")
+    mine = gather_column(half)
     other = swap_cores(mine)
     got = exchange(send, ("x", "y"))
     table = got[:, ROWS, : 2 * ENTRIES].astype(jnp.int32)
-    place = (lax.axis_index("x") * (NZ * NY) + lax.axis_index("y")).reshape(1)
+    heights = (lax.axis_index("z") + jnp.array(STEPS, jnp.int32)) % NZ
+    first_page = lax.axis_index("x") * (NZ * NY) + lax.axis_index("y")
+    column = jnp.concatenate([heights, first_page.reshape(1)])
     query_part, mine_part, other_part = pl.pallas_call(
         functools.partial(score_kernel, offset),
         out_shape=(
@@ -184,12 +212,11 @@
             pltpu.VMEM((HALF, W), jnp.float32),
         ],
         compiler_params=pltpu.CompilerParams(vmem_limit_bytes=48 << 20),
-    )(place, hot_pages, table, got, mine, other)
-    page_terms = mine_part.astype(jnp.float32) + swap_cores(other_part).astype(jnp.float32)
-    page_back = exchange(page_terms.astype(jnp.bfloat16), "z")
+    )(column, hot_pages, table, got, mine, other)
+    terms = mine_part.astype(jnp.float32) + swap_cores(other_part).astype(jnp.float32)
     query_back = exchange(query_part.reshape(PLANE, ROWS, W), ("x", "y"))
+    page_grad = reduce_column(terms)
     query_grad = jnp.sum(query_back.astype(jnp.float32), axis=0).astype(jnp.bfloat16)
-    page_grad = jnp.sum(page_back.astype(jnp.float32), axis=0).astype(jnp.bfloat16)
     return query_grad.reshape(Q_DEV, QT, W), page_grad[None]
 
 

time: 139 us -> 87.2 us (0.63)
  the two profiles are of different devices: /device:TPU:1 before, /device:TPU:34 now
where the time goes in v2:
time: 87.2 us; the launch traced here: 86.4 us
  starting transfers between devices  30.2 us (35%)
  waiting for transfers between devices  29.1 us (33%)
  Pallas kernels  19 us (22%)
  other arithmetic  5.29 us (6%)
  local copies, waits for them, and re-layouts  2.09 us (2%)
    ppermute x10, waiting for transfers between devices, move(): return lax.ppermute(array, 'z', [(i, (i + step) % NZ) for i in range(NZ)])  21.5 us
    ppermute x10, starting transfers between devices, move(): return lax.ppermute(array, 'z', [(i, (i + step) % NZ) for i in range(NZ)])  17.1 us
    pallas_call x1, Pallas kernels, shards(): pl.pallas_call(functools.partial(score_kernel, offset), out_shape=(jax.Sh...  16.8 us
    all_to_all x2, starting transfers between devices, exchange(): return lax.all_to_all(array, axes, split_axis=0, concat_axis=0, tiled=True)  13 us
    all_to_all x2, waiting for transfers between devices, exchange(): return lax.all_to_all(array, axes, split_axis=0, concat_axis=0, tiled=True)  7.55 us
    pallas_call x1, Pallas kernels, shards(): pl.pallas_call(pack_kernel, out_shape=jax.ShapeDtypeStruct((PLANE, SEND_R...  2.17 us
    reduce_sum x1, other arithmetic, shards(): jnp.sum(query_back.astype(jnp.float32), axis=0).astype(jnp.bfloat16)  2.01 us
  transfers between devices with their start and end apart: 14, of which 5 were waited for; matrix products, arithmetic and copies ran while one was open for 5% of the time, Pallas kernels for 3%

profile of v2, /device:TPU:34, one launch (start us, length us, event | category | flops | bytes accessed | tf_op | source)
XLA Modules:
  0.0 86.4 jit_solution(2149239678005668927)
XLA Ops:
  0.6 0.9 %dynamic-slice_bitcast_fusion = (bf16[512,128]{1,0:T(8,128)(2,1)S(1)}, bf16[8,512,128]{2,1,0:T(8,128)(2,1)S(1)}) fusion(bf16[1,1024,128]{2,1,0:T(8,128)(2,1)} %param.8, s32[]{:T(128)S(6)} %select_n.11), kind=kLoop, calls=%fused_computation.20 | loop fusion | bytes 393220 | tf_op jit(solution)/shard_map/dynamic_slice | solution.py:182
  1.6 6.4 %collective-permute-start.2 = (bf16[512,128]{1,0:T(8,128)(2,1)S(1)}, bf16[512,128]{1,0:T(8,128)(2,1)S(1)}, u32[]{:S(2)}, u32[]{:S(2)}) collective-permute-start(bf16[512,128]{1,0:T(8,128)(2,1)S(1)} %get-tuple-element.15), channel_id=1, source_target_pairs={{0,32},{8,40},{16,48},{24,56},{32,0},{40,8},{48,16},{56,24},{1,33}... | collective-permute-start | bytes 393224 | tf_op jit(solution)/shard_map/ppermute | solution.py:154
  8.0 1.0 %collective-permute-start.1 = (bf16[512,128]{1,0:T(8,128)(2,1)S(1)}, bf16[512,128]{1,0:T(8,128)(2,1)S(1)}, u32[]{:S(2)}, u32[]{:S(2)}) collective-permute-start(bf16[512,128]{1,0:T(8,128)(2,1)S(1)} %get-tuple-element.15), channel_id=1, source_target_pairs={{0,56},{8,0},{16,8},{24,16},{32,24},{40,32},{48,40},{56,48},{1,57}... | collective-permute-start | bytes 393224 | tf_op jit(solution)/shard_map/ppermute | solution.py:154
  9.0 1.0 %collective-permute-start = (bf16[512,128]{1,0:T(8,128)(2,1)S(1)}, bf16[512,128]{1,0:T(8,128)(2,1)S(1)}, u32[]{:S(2)}, u32[]{:S(2)}) collective-permute-start(bf16[512,128]{1,0:T(8,128)(2,1)S(1)} %get-tuple-element.15), channel_id=1, source_target_pairs={{0,8},{8,16},{16,24},{24,32},{32,40},{40,48},{48,56},{56,0},{1,9},... | collective-permute-start | bytes 393224 | tf_op jit(solution)/shard_map/ppermute | solution.py:154
  10.0 2.2 %shard_map.86 = bf16[16,272,128]{2,1,0:T(8,128)(2,1)} custom-call(s32[64]{0:T(128)} %bitcast.40, s32[64]{0:T(128)} %query_ref.1, s32[64]{0:T(128)} %label_ref.1, bf16[256,128]{1,0:T(8,128)(2,1)} %bitcast.38), custom_call_target="tpu_custom_call" | custom-call | tf_op jit(solution)/shard_map/pallas_call | solution.py:183
  12.2 0.0 copy-start.2
  12.2 0.0 copy-start
  12.2 7.6 %all-to-all-start = ((bf16[16,272,128]{2,1,0:T(8,128)(2,1)}), bf16[16,272,128]{2,1,0:T(8,128)(2,1)}, u32[]{:S(2)}, u32[]{:S(2)}) async-start(bf16[16,272,128]{2,1,0:T(8,128)(2,1)} %shard_map.86), calls=%async_computation | async-start | bytes 2228224 | tf_op jit(solution)/shard_map/all_to_all | solution.py:146
  19.8 0.0 collective-permute-done.2
  19.8 0.0 collective-permute-done.1
  19.8 0.0 collective-permute-done
  19.9 1.1 %collective-permute-start.4 = (bf16[2,512,128]{2,1,0:T(8,128)(2,1)S(1)}, bf16[2,512,128]{2,1,0:T(8,128)(2,1)S(1)}, u32[]{:S(2)}, u32[]{:S(2)}) collective-permute-start(bf16[2,512,128]{2,1,0:T(8,128)(2,1)S(1)} %get-tuple-element.17), channel_id=1, source_target_pairs={{0,56},{8,0},{16,8},{24,16},{32,24},{40,32},{48,40},{56,48},{1,57}... | collective-permute-start | bytes 786440 | tf_op jit(solution)/shard_map/ppermute | solution.py:154
  20.9 1.0 %collective-permute-start.3 = (bf16[2,512,128]{2,1,0:T(8,128)(2,1)S(1)}, bf16[2,512,128]{2,1,0:T(8,128)(2,1)S(1)}, u32[]{:S(2)}, u32[]{:S(2)}) collective-permute-start(bf16[2,512,128]{2,1,0:T(8,128)(2,1)S(1)} %get-tuple-element.18), channel_id=1, source_target_pairs={{0,8},{8,16},{16,24},{24,32},{32,40},{40,48},{48,56},{56,0},{1,9},... | collective-permute-start | bytes 786440 | tf_op jit(solution)/shard_map/ppermute | solution.py:154
  22.0 5.3 %collective-permute-done.3 = bf16[2,512,128]{2,1,0:T(8,128)(2,1)S(1)} collective-permute-done((bf16[2,512,128]{2,1,0:T(8,128)(2,1)S(1)}, bf16[2,512,128]{2,1,0:T(8,128)(2,1)S(1)}, u32[]{:S(2)}, u32[]{:S(2)}) %collective-permute-start.3) | collective-permute-done | bytes 262176 | tf_op jit(solution)/shard_map/ppermute | solution.py:154
  27.3 0.0 collective-permute-done.4
  27.4 0.1 collective-permute-start.5
  27.5 0.0 copy-done.2
  27.5 0.1 pad_add_fusion.column_ref
  27.6 7.6 %all-to-all-done.got_ref = bf16[16,272,128]{2,1,0:T(8,128)(2,1)} async-done(((bf16[16,272,128]{2,1,0:T(8,128)(2,1)}), bf16[16,272,128]{2,1,0:T(8,128)(2,1)}, u32[]{:S(2)}, u32[]{:S(2)}) %all-to-all-start) | async-done | bytes 1114144 | tf_op jit(solution)/shard_map/all_to_all | solution.py:146
  35.2 0.8 slice_convert_fusion
  35.9 0.0 collective-permute-done.5.other_ref
  35.9 0.0 copy-done
  35.9 16.8 %shard_map.87 = (bf16[4096,128]{1,0:T(8,128)(2,1)}, bf16[8,512,128]{2,1,0:T(8,128)(2,1)S(1)}, bf16[8,512,128]{2,1,0:T(8,128)(2,1)}) custom-call(s32[9]{0:T(128)S(1)} %pad_add_fusion.column_ref, s32[2]{0:T(128)S(1)} %copy-done, s32[16,32]{1,0:T(8,128)S(1)} %bitcast.34, bf16[16,272,128]{2,1,0:T(8,128)(2,1)} %all-to-all-done.got_ref, ...), custom_call_target="tpu_custom_call" | custom-call | tf_op jit(solution)/shard_map/pallas_call | solution.py:196
  52.7 0.0 collective-permute-start.6
  52.7 5.4 %all-to-all-start.1 = ((bf16[16,256,128]{2,1,0:T(8,128)(2,1)}), bf16[16,256,128]{2,1,0:T(8,128)(2,1)}, u32[]{:S(2)}, u32[]{:S(2)}) async-start(bf16[16,256,128]{2,1,0:T(8,128)(2,1)} %bitcast.8), calls=%async_computation.1 | async-start | bytes 2097152 | tf_op jit(solution)/shard_map/all_to_all | solution.py:146
  58.1 0.0 collective-permute-done.6
  58.1 0.0 copy-start.1
  58.1 1.0 %copy-done.1 = bf16[8,512,128]{2,1,0:T(8,128)(2,1)} copy-done((bf16[8,512,128]{2,1,0:T(8,128)(2,1)}, bf16[8,512,128]{2,1,0:T(8,128)(2,1)S(1)}, u32[]{:S(2)}) %copy-start.1) | copy-done | bytes 1048600
  59.1 1.6 %fusion.13 = (bf16[8,512,128]{2,1,0:T(8,128)(2,1)S(1)}, f32[8,512,128]{2,1,0:T(8,128)S(1)}) fusion(bf16[8,512,128]{2,1,0:T(8,128)(2,1)} %copy-done.1, bf16[8,512,128]{2,1,0:T(8,128)(2,1)S(1)} %get-tuple-element.6), kind=kLoop, calls=%fused_computation.32 | loop fusion | flops 2097152 | bytes 5242880 | tf_op jit(solution)/shard_map/convert_element_type | solution.py:165
  60.7 1.2 %collective-permute-start.7 = (bf16[2,512,128]{2,1,0:T(8,128)(2,1)S(1)}, bf16[2,512,128]{2,1,0:T(8,128)(2,1)S(1)}, u32[]{:S(2)}, u32[]{:S(2)}) collective-permute-start(bf16[2,512,128]{2,1,0:T(8,128)(2,1)S(1)} %get-tuple-element.13), channel_id=1, source_target_pairs={{0,8},{8,16},{16,24},{24,32},{32,40},{40,48},{48,56},{56,0},{1,9},... | collective-permute-start | bytes 786440 | tf_op jit(solution)/shard_map/ppermute | solution.py:154
  61.9 0.9 %collective-permute-start.9 = (bf16[2,512,128]{2,1,0:T(8,128)(2,1)S(1)}, bf16[2,512,128]{2,1,0:T(8,128)(2,1)S(1)}, u32[]{:S(2)}, u32[]{:S(2)}) collective-permute-start(bf16[2,512,128]{2,1,0:T(8,128)(2,1)S(1)} %get-tuple-element.14), channel_id=1, source_target_pairs={{0,56},{8,0},{16,8},{24,16},{32,24},{40,32},{48,40},{56,48},{1,57}... | collective-permute-start | bytes 786440 | tf_op jit(solution)/shard_map/ppermute | solution.py:154
  62.8 6.2 %collective-permute-done.7 = bf16[2,512,128]{2,1,0:T(8,128)(2,1)S(1)} collective-permute-done((bf16[2,512,128]{2,1,0:T(8,128)(2,1)S(1)}, bf16[2,512,128]{2,1,0:T(8,128)(2,1)S(1)}, u32[]{:S(2)}, u32[]{:S(2)}) %collective-permute-start.7) | collective-permute-done | bytes 262176 | tf_op jit(solution)/shard_map/ppermute | solution.py:154
  69.0 2.5 %collective-permute-done.9 = bf16[2,512,128]{2,1,0:T(8,128)(2,1)S(1)} collective-permute-done((bf16[2,512,128]{2,1,0:T(8,128)(2,1)S(1)}, bf16[2,512,128]{2,1,0:T(8,128)(2,1)S(1)}, u32[]{:S(2)}, u32[]{:S(2)}) %collective-permute-start.9) | collective-permute-done | bytes 262176 | tf_op jit(solution)/shard_map/ppermute | solution.py:154
  71.6 0.1 fusion.9
  71.7 1.8 %collective-permute-start.8 = (bf16[512,128]{1,0:T(8,128)(2,1)S(1)}, bf16[512,128]{1,0:T(8,128)(2,1)S(1)}, u32[]{:S(2)}, u32[]{:S(2)}) collective-permute-start(bf16[512,128]{1,0:T(8,128)(2,1)S(1)} %get-tuple-element.8), channel_id=1, source_target_pairs={{0,8},{8,16},{16,24},{24,32},{32,40},{40,48},{48,56},{56,0},{1,9},... | collective-permute-start | bytes 393224 | tf_op jit(solution)/shard_map/ppermute | solution.py:154
  73.5 0.0 collective-permute-start.11
  73.5 2.7 %collective-permute-start.10 = (bf16[512,128]{1,0:T(8,128)(2,1)S(1)}, bf16[512,128]{1,0:T(8,128)(2,1)S(1)}, u32[]{:S(2)}, u32[]{:S(2)}) collective-permute-start(bf16[512,128]{1,0:T(8,128)(2,1)S(1)} %get-tuple-element.10), channel_id=1, source_target_pairs={{0,56},{8,0},{16,8},{24,16},{32,24},{40,32},{48,40},{56,48},{1,57}... | collective-permute-start | bytes 393224 | tf_op jit(solution)/shard_map/ppermute | solution.py:154
  76.2 0.0 all-to-all-done.1
  76.2 2.0 %reduce_sum.12 = bf16[256,128]{1,0:T(8,128)(2,1)} reduce(bf16[16,256,128]{2,1,0:T(8,128)(2,1)} %all-to-all-done.1, bf16[]{:T(256)} %constant.43.clone.1), dimensions={0}, to_apply=%region_0.1 | reduce | flops 491520 | bytes 1114114 | tf_op jit(solution)/shard_map/reduce_sum | solution.py:219
  78.2 0.0 collective-permute-done.8
  78.2 7.5 %collective-permute-done.11 = bf16[512,128]{1,0:T(8,128)(2,1)S(1)} collective-permute-done((bf16[512,128]{1,0:T(8,128)(2,1)S(1)}, bf16[512,128]{1,0:T(8,128)(2,1)S(1)}, u32[]{:S(2)}, u32[]{:S(2)}) %collective-permute-start.11) | collective-permute-done | bytes 131104 | tf_op jit(solution)/shard_map/ppermute | solution.py:154
  85.7 0.0 collective-permute-done.10
  85.7 0.7 fusion.8
  (8 shorter events, 0.2 us)
Async XLA Ops:
  1.6 18.2 %collective-permute-start.2 = (bf16[512,128]{1,0:T(8,128)(2,1)S(1)}, bf16[512,128]{1,0:T(8,128)(2,1)S(1)}, u32[]{:S(2)}, u32[]{:S(2)}) collective-permute-start(bf16[512,128]{1,0:T(8,128)(2,1)S(1)} %get-tuple-element.15), channel_id=1, source_target_pairs={{0,32},{8,40},{16,48},{24,56},{32,0},{40,8},{48,16},{56,24},{1,33}... | collective-permute-start | bytes 393224 | tf_op jit(solution)/shard_map/ppermute | solution.py:154
  8.0 11.8 %collective-permute-start.1 = (bf16[512,128]{1,0:T(8,128)(2,1)S(1)}, bf16[512,128]{1,0:T(8,128)(2,1)S(1)}, u32[]{:S(2)}, u32[]{:S(2)}) collective-permute-start(bf16[512,128]{1,0:T(8,128)(2,1)S(1)} %get-tuple-element.15), channel_id=1, source_target_pairs={{0,56},{8,0},{16,8},{24,16},{32,24},{40,32},{48,40},{56,48},{1,57}... | collective-permute-start | bytes 393224 | tf_op jit(solution)/shard_map/ppermute | solution.py:154
  9.0 10.8 %collective-permute-start = (bf16[512,128]{1,0:T(8,128)(2,1)S(1)}, bf16[512,128]{1,0:T(8,128)(2,1)S(1)}, u32[]{:S(2)}, u32[]{:S(2)}) collective-permute-start(bf16[512,128]{1,0:T(8,128)(2,1)S(1)} %get-tuple-element.15), channel_id=1, source_target_pairs={{0,8},{8,16},{16,24},{24,32},{32,40},{40,48},{48,56},{56,0},{1,9},... | collective-permute-start | bytes 393224 | tf_op jit(solution)/shard_map/ppermute | solution.py:154
  12.2 15.4 %copy-start.2 = (s32[8]{0:T(128)S(1)}, s32[8]{0:T(128)}, u32[]{:S(2)}) copy-start(s32[8]{0:T(128)} %constant.44.clone) | copy-start | bytes 100
  12.2 23.8 %copy-start = (s32[2]{0:T(128)S(1)}, s32[2]{0:T(128)}, u32[]{:S(2)}) copy-start(s32[2]{0:T(128)} %hot_ref.1) | copy-start | bytes 28
  12.2 23.0 %all-to-all-start = ((bf16[16,272,128]{2,1,0:T(8,128)(2,1)}), bf16[16,272,128]{2,1,0:T(8,128)(2,1)}, u32[]{:S(2)}, u32[]{:S(2)}) async-start(bf16[16,272,128]{2,1,0:T(8,128)(2,1)} %shard_map.86), calls=%async_computation | async-start | bytes 2228224 | tf_op jit(solution)/shard_map/all_to_all | solution.py:146
  19.9 7.5 %collective-permute-start.4 = (bf16[2,512,128]{2,1,0:T(8,128)(2,1)S(1)}, bf16[2,512,128]{2,1,0:T(8,128)(2,1)S(1)}, u32[]{:S(2)}, u32[]{:S(2)}) collective-permute-start(bf16[2,512,128]{2,1,0:T(8,128)(2,1)S(1)} %get-tuple-element.17), channel_id=1, source_target_pairs={{0,56},{8,0},{16,8},{24,16},{32,24},{40,32},{48,40},{56,48},{1,57}... | collective-permute-start | bytes 786440 | tf_op jit(solution)/shard_map/ppermute | solution.py:154
  20.9 6.4 %collective-permute-start.3 = (bf16[2,512,128]{2,1,0:T(8,128)(2,1)S(1)}, bf16[2,512,128]{2,1,0:T(8,128)(2,1)S(1)}, u32[]{:S(2)}, u32[]{:S(2)}) collective-permute-start(bf16[2,512,128]{2,1,0:T(8,128)(2,1)S(1)} %get-tuple-element.18), channel_id=1, source_target_pairs={{0,8},{8,16},{16,24},{24,32},{32,40},{40,48},{48,56},{56,0},{1,9},... | collective-permute-start | bytes 786440 | tf_op jit(solution)/shard_map/ppermute | solution.py:154
  27.4 8.5 %collective-permute-start.5 = (bf16[8,512,128]{2,1,0:T(8,128)(2,1)S(1)}, bf16[8,512,128]{2,1,0:T(8,128)(2,1)S(1)}, u32[]{:S(2)}, u32[]{:S(2)}) collective-permute-start(bf16[8,512,128]{2,1,0:T(8,128)(2,1)S(1)} %constant_dynamic-update-slice_fusion.mine_ref), channel_id=1, source_target_pairs={{0,1},{1,0},{2,3},{3,2},{4,5},{5,4},{6,7},{7,6},{8,9},{9,8},{10,11... | collective-permute-start | bytes 3145736 | tf_op jit(solution)/shard_map/ppermute | solution.py:150
  52.7 5.4 %collective-permute-start.6 = (bf16[8,512,128]{2,1,0:T(8,128)(2,1)}, bf16[8,512,128]{2,1,0:T(8,128)(2,1)S(1)}, u32[]{:S(2)}, u32[]{:S(2)}) collective-permute-start(bf16[8,512,128]{2,1,0:T(8,128)(2,1)} %get-tuple-element.7), channel_id=1, source_target_pairs={{0,1},{1,0},{2,3},{3,2},{4,5},{5,4},{6,7},{7,6},{8,9},{9,8},{10,11... | collective-permute-start | bytes 3145736 | tf_op jit(solution)/shard_map/ppermute | solution.py:150
  52.7 23.5 %all-to-all-start.1 = ((bf16[16,256,128]{2,1,0:T(8,128)(2,1)}), bf16[16,256,128]{2,1,0:T(8,128)(2,1)}, u32[]{:S(2)}, u32[]{:S(2)}) async-start(bf16[16,256,128]{2,1,0:T(8,128)(2,1)} %bitcast.8), calls=%async_computation.1 | async-start | bytes 2097152 | tf_op jit(solution)/shard_map/all_to_all | solution.py:146
  58.1 1.0 %copy-start.1 = (bf16[8,512,128]{2,1,0:T(8,128)(2,1)}, bf16[8,512,128]{2,1,0:T(8,128)(2,1)S(1)}, u32[]{:S(2)}) copy-start(bf16[8,512,128]{2,1,0:T(8,128)(2,1)S(1)} %collective-permute-done.6) | copy-start | bytes 3145732
  60.7 8.3 %collective-permute-start.7 = (bf16[2,512,128]{2,1,0:T(8,128)(2,1)S(1)}, bf16[2,512,128]{2,1,0:T(8,128)(2,1)S(1)}, u32[]{:S(2)}, u32[]{:S(2)}) collective-permute-start(bf16[2,512,128]{2,1,0:T(8,128)(2,1)S(1)} %get-tuple-element.13), channel_id=1, source_target_pairs={{0,8},{8,16},{16,24},{24,32},{32,40},{40,48},{48,56},{56,0},{1,9},... | collective-permute-start | bytes 786440 | tf_op jit(solution)/shard_map/ppermute | solution.py:154
  61.9 9.7 %collective-permute-start.9 = (bf16[2,512,128]{2,1,0:T(8,128)(2,1)S(1)}, bf16[2,512,128]{2,1,0:T(8,128)(2,1)S(1)}, u32[]{:S(2)}, u32[]{:S(2)}) collective-permute-start(bf16[2,512,128]{2,1,0:T(8,128)(2,1)S(1)} %get-tuple-element.14), channel_id=1, source_target_pairs={{0,56},{8,0},{16,8},{24,16},{32,24},{40,32},{48,40},{56,48},{1,57}... | collective-permute-start | bytes 786440 | tf_op jit(solution)/shard_map/ppermute | solution.py:154
  71.7 6.5 %collective-permute-start.8 = (bf16[512,128]{1,0:T(8,128)(2,1)S(1)}, bf16[512,128]{1,0:T(8,128)(2,1)S(1)}, u32[]{:S(2)}, u32[]{:S(2)}) collective-permute-start(bf16[512,128]{1,0:T(8,128)(2,1)S(1)} %get-tuple-element.8), channel_id=1, source_target_pairs={{0,8},{8,16},{16,24},{24,32},{32,40},{40,48},{48,56},{56,0},{1,9},... | collective-permute-start | bytes 393224 | tf_op jit(solution)/shard_map/ppermute | solution.py:154
  73.5 12.2 %collective-permute-start.11 = (bf16[512,128]{1,0:T(8,128)(2,1)S(1)}, bf16[512,128]{1,0:T(8,128)(2,1)S(1)}, u32[]{:S(2)}, u32[]{:S(2)}) collective-permute-start(bf16[512,128]{1,0:T(8,128)(2,1)S(1)} %get-tuple-element.9), channel_id=1, source_target_pairs={{0,32},{8,40},{16,48},{24,56},{32,0},{40,8},{48,16},{56,24},{1,33}... | collective-permute-start | bytes 393224 | tf_op jit(solution)/shard_map/ppermute | solution.py:154
  73.5 12.2 %collective-permute-start.10 = (bf16[512,128]{1,0:T(8,128)(2,1)S(1)}, bf16[512,128]{1,0:T(8,128)(2,1)S(1)}, u32[]{:S(2)}, u32[]{:S(2)}) collective-permute-start(bf16[512,128]{1,0:T(8,128)(2,1)S(1)} %get-tuple-element.10), channel_id=1, source_target_pairs={{0,56},{8,0},{16,8},{24,16},{32,24},{40,32},{48,40},{56,48},{1,57}... | collective-permute-start | bytes 393224 | tf_op jit(solution)/shard_map/ppermute | solution.py:154

commit v3 on v2

v3 whole, which is shorter than its diff:
```python
import functools
import math

import jax
import jax.numpy as jnp
from jax import lax
from jax.experimental import pallas as pl
from jax.experimental.pallas import tpu as pltpu
from jax.sharding import Mesh, PartitionSpec as P

SHARPNESS = 4.0
SLOPE_SCALE = 0.5
HOT_SHIFT = 2.0

NX, NZ, NY, NC = 4, 8, 4, 2
PLANE = NX * NY
QT = 32
W = 128
Q_DEV = 8
PAIR_DEV = 64
PATCHES = 1024
HALF = PATCHES // 2
CAP = 2
ROWS = Q_DEV * QT
SEND_ROWS = ROWS + 16
ENTRIES = NZ * CAP
GROUP = 8
BLOCK = 128
ITEMS = 3
SLOTS = PLANE * CAP
LIST = SLOTS + GROUP
PART = NZ // 2
STEPS = (0, -1, 1, 4, -2, 3, 2, -3)


def pack_kernel(page_ref, query_ref, label_ref, rows_ref, out_ref):
    dest = lax.broadcasted_iota(jnp.int32, (PLANE, W), 0)
    lane = lax.broadcasted_iota(jnp.int32, (PLANE, W), 1)
    entry = lane % ENTRIES
    rank = entry % CAP
    wanted = (dest // NY) * (NZ * NY) + (entry // CAP) * NY + dest % NY
    is_query = lane < ENTRIES
    is_label = jnp.logical_and(lane >= ENTRIES, lane < 2 * ENTRIES)

    def visit(i, carry):
        table, seen = carry
        hit = wanted == page_ref[i]
        value = jnp.where(is_query, query_ref[i] + 1, jnp.where(is_label, label_ref[i], 0))
        table = jnp.where(jnp.logical_and(hit, seen == rank), value, table)
        return table, seen + hit.astype(jnp.int32)

    zeros = jnp.zeros((PLANE, W), jnp.int32)
    table, _ = lax.fori_loop(0, PAIR_DEV, visit, (zeros, zeros), unroll=8)
    table = table.astype(jnp.float32)
    rows = rows_ref[...]
    for d in range(PLANE):
        out_ref[d, :ROWS, :] = rows
        out_ref[d, ROWS:, :] = jnp.broadcast_to(table[d : d + 1, :], (16, W)).astype(jnp.bfloat16)


def score_kernel(
    offset, column_ref, hot_ref, table_ref, got_ref, mine_ref, other_ref, carried_ref,
    query_out, mine_out, other_out,
    slot_query, slot_label, item_page, item_base, item_left, turned, query_acc, page_acc, *work,
):
    rows = GROUP * QT
    if query_acc is None:
        query_acc = query_out
    token_refs, logit_refs, expo_refs = work[:ITEMS], work[ITEMS : 2 * ITEMS], work[2 * ITEMS :]
    if carried_ref is None:
        query_acc[...] = jnp.zeros_like(query_acc)
    else:
        query_acc[...] = carried_ref[...]
    page_acc[...] = jnp.zeros_like(page_acc)
    first_page = column_ref[PART]

    def list_page(page, items):
        height = column_ref[page]
        turned[page, :, :HALF] = mine_ref[page].T
        turned[page, :, HALF:] = other_ref[page].T
        start = page * LIST
        count = jnp.int32(0)
        for s in range(PLANE):
            for r in range(CAP):
                code = table_ref[s, height * CAP + r]
                slot_query[start + count] = s * Q_DEV + code - 1
                slot_label[start + count] = table_ref[s, ENTRIES + height * CAP + r]
                count = count + (code > 0).astype(jnp.int32)
        for g in range(GROUP - 1):
            slot_query[start + count + g] = 0
            slot_label[start + count + g] = 0
        for j in range(SLOTS // GROUP):
            item_page[items] = page
            item_base[items] = start + j * GROUP
            item_left[items] = count - j * GROUP
            items = items + (count > j * GROUP).astype(jnp.int32)
        return items

    items = lax.fori_loop(0, PART, list_page, jnp.int32(0))
    for g in range(GROUP):
        slot_query[PART * LIST + g] = 0
        slot_label[PART * LIST + g] = 0
    for u in range(ITEMS):
        item_page[items + u] = 0
        item_base[items + u] = PART * LIST
        item_left[items + u] = 0

    def per_round(step, _):
        at = [step * ITEMS + u for u in range(ITEMS)]
        page = [item_page[i] for i in at]
        base = [item_base[i] for i in at]
        left = [item_left[i] for i in at]
        query = [[slot_query[b + g] for g in range(GROUP)] for b in base]
        for u in range(ITEMS):
            for g in range(GROUP):
                token_refs[u][g * QT : (g + 1) * QT, :] = got_ref[
                    lax.shift_right_logical(query[u][g], 3),
                    pl.ds(pl.multiple_of(lax.bitwise_and(query[u][g], Q_DEV - 1) * QT, QT), QT),
                    :,
                ]
        dims = (((1,), (1,)), ((), ()))
        peaks, lses, inverses = [], [], []
        for u in range(ITEMS):
            tok = token_refs[u][...]
            peak = None
            for c in range(PATCHES // BLOCK):
                part = (mine_ref, other_ref)[c * BLOCK // HALF]
                first = c * BLOCK % HALF
                block = lax.dot_general(
                    part[page[u], first : first + BLOCK, :], tok, dims,
                    preferred_element_type=jnp.float32,
                )
                logit_refs[u][c * BLOCK : (c + 1) * BLOCK, :] = block
                top = jnp.max(block.reshape(BLOCK // 8, 8, rows), axis=0)
                peak = top if peak is None else jnp.maximum(peak, top)
            peaks.append(jnp.max(peak, axis=0, keepdims=True))
        for u in range(ITEMS):
            total = None
            for c in range(PATCHES // BLOCK):
                piece = logit_refs[u][c * BLOCK : (c + 1) * BLOCK, :]
                e = jnp.exp(SHARPNESS * (piece - peaks[u]))
                expo_refs[u][c * BLOCK : (c + 1) * BLOCK, :] = e.astype(jnp.bfloat16)
                low = jnp.sum(e.reshape(BLOCK // 8, 8, rows), axis=0)
                total = low if total is None else total + low
            total = jnp.sum(total, axis=0, keepdims=True)
            lse = SHARPNESS * peaks[u] + jnp.log(total)
            lses.append(jnp.broadcast_to(lse, (W, rows)).T)
            inverses.append(jnp.broadcast_to(1.0 / total, (W, rows)).T)
        grads = [
            jnp.dot(turned[page[u]], expo_refs[u][...], preferred_element_type=jnp.float32).T
            for u in range(ITEMS)
        ]
        scale = []
        for u in range(ITEMS):
            page_id = first_page + column_ref[page[u]] * NY
            hot = jnp.logical_or(hot_ref[0] == page_id, hot_ref[1] == page_id)
            shift = jnp.where(hot, HOT_SHIFT, 0.0).astype(jnp.float32)
            parts = []
            for g in range(GROUP):
                mine = slice(g * QT, (g + 1) * QT)
                score = jnp.sum(lses[u][mine], axis=0, keepdims=True) / SHARPNESS
                logit = SLOPE_SCALE * score + offset - shift
                label = slot_label[base[u] + g].astype(jnp.float32)
                live = jnp.where(g < left[u], SLOPE_SCALE, 0.0)
                slope = live * (1.0 / (1.0 + jnp.exp(-logit)) - label)
                parts.append(slope * inverses[u][mine])
            scale.append(jnp.concatenate(parts, axis=0))
        for u in range(ITEMS):
            scaled = (token_refs[u][...].astype(jnp.float32) * scale[u]).astype(jnp.bfloat16)
            page_acc[page[u]] += jnp.dot(
                expo_refs[u][...], scaled, preferred_element_type=jnp.float32
            )
        for u in range(ITEMS):
            grad = grads[u] * scale[u]
            for g in range(GROUP):
                rows_at = pl.ds(pl.multiple_of(query[u][g] * QT, QT), QT)
                query_acc[rows_at, :] += grad[g * QT : (g + 1) * QT]
        return 0

    lax.fori_loop(0, (items + ITEMS - 1) // ITEMS, per_round, 0)
    for k in range(PART):
        mine_out[k] = page_acc[k, :HALF, :].astype(jnp.bfloat16)
        other_out[k] = page_acc[k, HALF:, :].astype(jnp.bfloat16)
    if query_out is not query_acc:
        query_out[...] = query_acc[...].astype(jnp.bfloat16)


def exchange(array, axes):
    return lax.all_to_all(array, axes, split_axis=0, concat_axis=0, tiled=True)


def swap_cores(array):
    return lax.ppermute(array, "core", [(0, 1), (1, 0)])


def move(array, step):
    return lax.ppermute(array, "z", [(i, (i + step) % NZ) for i in range(NZ)])


def gather_column(half):
    below, above, across = move(half, 1), move(half, -1), move(half, 4)
    far_below = move(jnp.stack([below, across]), 1)
    far_above = move(jnp.stack([above, across]), -1)
    return jnp.stack([half, below, above, across]), jnp.concatenate([far_below, far_above])


def reduce_column(near, from_below, from_above):
    up = (near[2] + from_below[0].astype(jnp.float32)).astype(jnp.bfloat16)
    down = (near[1] + from_above[0].astype(jnp.float32)).astype(jnp.bfloat16)
    over = near[3] + from_below[1].astype(jnp.float32) + from_above[1].astype(jnp.float32)
    over = over.astype(jnp.bfloat16)
    total = near[0]
    for part in (move(up, 1), move(down, -1), move(over, 4)):
        total = total + part.astype(jnp.float32)
    return total.astype(jnp.bfloat16)


def first_kernel(offset, *refs):
    score_kernel(offset, *refs[:6], None, *refs[6:15], None, *refs[15:])


def second_kernel(offset, *refs):
    score_kernel(offset, *refs)


def score(column, hot_pages, table, got, mine, other, carried=None):
    offset = -SLOPE_SCALE * QT * (math.log(PATCHES) / SHARPNESS + SHARPNESS / 2.0)
    smem = pl.BlockSpec(memory_space=pltpu.SMEM)
    vmem = pl.BlockSpec(memory_space=pltpu.VMEM)
    last = carried is not None
    pages = jax.ShapeDtypeStruct((PART, HALF, W), jnp.bfloat16)
    sums = jax.ShapeDtypeStruct((PLANE * ROWS, W), jnp.bfloat16 if last else jnp.float32)
    items = PART * SLOTS // GROUP + ITEMS
    rows = GROUP * QT
    scratch = [
        pltpu.SMEM((PART * LIST + GROUP,), jnp.int32),
        pltpu.SMEM((PART * LIST + GROUP,), jnp.int32),
        pltpu.SMEM((items,), jnp.int32),
        pltpu.SMEM((items,), jnp.int32),
        pltpu.SMEM((items,), jnp.int32),
        pltpu.VMEM((PART, W, PATCHES), jnp.bfloat16),
    ]
    scratch += [pltpu.VMEM((PLANE * ROWS, W), jnp.float32)] * last
    scratch += [pltpu.VMEM((PART, PATCHES, W), jnp.float32)]
    scratch += [pltpu.VMEM((rows, W), jnp.bfloat16)] * ITEMS
    scratch += [pltpu.VMEM((PATCHES, rows), jnp.float32)] * ITEMS
    scratch += [pltpu.VMEM((PATCHES, rows), jnp.bfloat16)] * ITEMS
    return pl.pallas_call(
        functools.partial(second_kernel if last else first_kernel, offset),
        out_shape=(sums, pages, pages),
        in_specs=[smem] * 3 + [vmem] * (3 + last),
        out_specs=(vmem, vmem, vmem),
        scratch_shapes=scratch,
        compiler_params=pltpu.CompilerParams(vmem_limit_bytes=40 << 20),
        cost_estimate=pl.CostEstimate(
            flops=6 * PLANE * CAP * 2 * QT * PATCHES * W * 2,
            bytes_accessed=8 << 20,
            transcendentals=PLANE * CAP * 2 * QT * PATCHES,
        ),
    )(column, hot_pages, table, got, mine, other, *([carried] if last else []))


def shards(queries, pages, pair_page, pair_query, pair_label, hot_pages):
    smem = pl.BlockSpec(memory_space=pltpu.SMEM)
    vmem = pl.BlockSpec(memory_space=pltpu.VMEM)
    core = lax.axis_index("core")
    half = lax.dynamic_slice(pages[0], (core * HALF, 0), (HALF, W))
    send = pl.pallas_call(
        pack_kernel,
        out_shape=jax.ShapeDtypeStruct((PLANE, SEND_ROWS, W), jnp.bfloat16),
        in_specs=[smem, smem, smem, vmem],
        out_specs=vmem,
    )(pair_page[:, 0], pair_query, pair_label, queries.reshape(ROWS, W))
    near, far = gather_column(half)
    other_near, other_far = swap_cores(near), swap_cores(far)
    got = exchange(send, ("x", "y"))
    table = got[:, ROWS, : 2 * ENTRIES].astype(jnp.int32)
    heights = (lax.axis_index("z") + jnp.array(STEPS, jnp.int32)) % NZ
    first_page = (lax.axis_index("x") * (NZ * NY) + lax.axis_index("y")).reshape(1)
    near_column = jnp.concatenate([heights[:PART], first_page])
    far_column = jnp.concatenate([heights[PART:], first_page])
    sums, mine_terms, other_terms = score(far_column, hot_pages, table, got, far, other_far)
    far_terms = mine_terms.astype(jnp.float32) + swap_cores(other_terms).astype(jnp.float32)
    far_terms = far_terms.astype(jnp.bfloat16)
    query_part, mine_terms, other_terms = score(
        near_column, hot_pages, table, got, near, other_near, sums
    )
    near_terms = mine_terms.astype(jnp.float32) + swap_cores(other_terms).astype(jnp.float32)
    from_below, from_above = move(far_terms[2:4], 1), move(far_terms[0:2], -1)
    query_back = exchange(query_part.reshape(PLANE, ROWS, W), ("x", "y"))
    page_grad = reduce_column(near_terms, from_below, from_above)
    query_grad = jnp.sum(query_back.astype(jnp.float32), axis=0).astype(jnp.bfloat16)
    return query_grad.reshape(Q_DEV, QT, W), page_grad[None]


def solution(mesh):
    torus = Mesh(mesh.devices.reshape(NX, NZ, NY, NC), ("x", "z", "y", "core"))
    owner = ("x", "z", "y")
    device = ("x", "z", "y", "core")
    return jax.shard_map(
        shards,
        mesh=torus,
        in_specs=(P(device), P(owner), P(device), P(device), P(device), P()),
        out_specs=(P(device), P(owner, "core")),
        check_vma=False,
    )
```

time: 87.2 us -> 88.9 us (1.019)
  the two profiles are of different devices: /device:TPU:34 before, /device:TPU:1 now
where the time goes in v3:
time: 88.9 us; the launch traced here: 87.8 us
  starting transfers between devices  38.3 us (43%)
  waiting for transfers between devices  25 us (28%)
  Pallas kernels  15.6 us (18%)
  local copies, waits for them, and re-layouts  4.83 us (5%)
  other arithmetic  3.17 us (4%)
    ppermute x10, waiting for transfers between devices, move(): return lax.ppermute(array, 'z', [(i, (i + step) % NZ) for i in range(NZ)])  19.8 us
    ppermute x10, starting transfers between devices, move(): return lax.ppermute(array, 'z', [(i, (i + step) % NZ) for i in range(NZ)])  17.8 us
    pallas_call x2, Pallas kernels, score(): pl.pallas_call(functools.partial(second_kernel if last else first_kernel,...  13.4 us
    all_to_all x2, starting transfers between devices, exchange(): return lax.all_to_all(array, axes, split_axis=0, concat_axis=0, tiled=True)  10.5 us
    ppermute x4, starting transfers between devices, swap_cores(): return lax.ppermute(array, 'core', [(0, 1), (1, 0)])  9.98 us
    all_to_all x2, waiting for transfers between devices, exchange(): return lax.all_to_all(array, axes, split_axis=0, concat_axis=0, tiled=True)  5.24 us
    unnamed x15, local copies, waits for them, and re-layouts  4.67 us
    pallas_call x1, Pallas kernels, shards(): pl.pallas_call(pack_kernel, out_shape=jax.ShapeDtypeStruct((PLANE, SEND_R...  2.18 us
  transfers between devices with their start and end apart: 16, of which 7 were waited for; matrix products, arithmetic and copies ran while one was open for 3% of the time, Pallas kernels for 18%

profile of v3, /device:TPU:1, one launch (start us, length us, event | category | flops | bytes accessed | tf_op | source)
XLA Modules:
  0.0 87.8 jit_solution(4225401788421494875)
XLA Ops:
  0.6 0.0 copy-start
  0.7 0.9 %copy-done = bf16[1,1024,128]{2,1,0:T(8,128)(2,1)S(1)} copy-done((bf16[1,1024,128]{2,1,0:T(8,128)(2,1)S(1)}, bf16[1,1024,128]{2,1,0:T(8,128)(2,1)}, u32[]{:S(2)}) %copy-start) | copy-done | bytes 262168
  1.6 2.5 %collective-permute-start = (bf16[512,128]{1,0:T(8,128)(2,1)S(1)}, bf16[512,128]{1,0:T(8,128)(2,1)S(1)}, u32[]{:S(2)}, u32[]{:S(2)}) collective-permute-start(bf16[512,128]{1,0:T(8,128)(2,1)S(1)} %fusion.15), channel_id=1, source_target_pairs={{0,8},{8,16},{16,24},{24,32},{32,40},{40,48},{48,56},{56,0},{1,9},... | collective-permute-start | bytes 393224 | tf_op jit(solution)/shard_map/ppermute | solution.py:197
  4.1 4.0 %collective-permute-start.1 = (bf16[512,128]{1,0:T(8,128)(2,1)S(1)}, bf16[512,128]{1,0:T(8,128)(2,1)S(1)}, u32[]{:S(2)}, u32[]{:S(2)}) collective-permute-start(bf16[512,128]{1,0:T(8,128)(2,1)S(1)} %fusion.15), channel_id=1, source_target_pairs={{0,56},{8,0},{16,8},{24,16},{32,24},{40,32},{48,40},{56,48},{1,57}... | collective-permute-start | bytes 393224 | tf_op jit(solution)/shard_map/ppermute | solution.py:197
  8.2 3.9 %collective-permute-start.2 = (bf16[512,128]{1,0:T(8,128)(2,1)S(1)}, bf16[512,128]{1,0:T(8,128)(2,1)S(1)}, u32[]{:S(2)}, u32[]{:S(2)}) collective-permute-start(bf16[512,128]{1,0:T(8,128)(2,1)S(1)} %fusion.15), channel_id=1, source_target_pairs={{0,32},{8,40},{16,48},{24,56},{32,0},{40,8},{48,16},{56,24},{1,33}... | collective-permute-start | bytes 393224 | tf_op jit(solution)/shard_map/ppermute | solution.py:197
  12.1 2.2 %shard_map.86 = bf16[16,272,128]{2,1,0:T(8,128)(2,1)} custom-call(s32[64]{0:T(128)} %bitcast.41, s32[64]{0:T(128)} %query_ref.1, s32[64]{0:T(128)} %label_ref.1, bf16[256,128]{1,0:T(8,128)(2,1)} %bitcast.39), custom_call_target="tpu_custom_call" | custom-call | tf_op jit(solution)/shard_map/pallas_call | solution.py:268
  14.3 0.0 copy-start.6
  14.3 6.9 %all-to-all-start = ((bf16[16,272,128]{2,1,0:T(8,128)(2,1)}), bf16[16,272,128]{2,1,0:T(8,128)(2,1)S(1)}, u32[]{:S(2)}, u32[]{:S(2)}) async-start(bf16[16,272,128]{2,1,0:T(8,128)(2,1)} %shard_map.86), calls=%async_computation | async-start | bytes 2228224 | tf_op jit(solution)/shard_map/all_to_all | solution.py:189
  21.2 0.0 collective-permute-done
  21.2 0.0 collective-permute-done.1
  21.2 0.0 collective-permute-done.2
  21.3 0.1 collective-permute-start.4
  21.4 0.0 copy-done.6
  21.4 2.7 %collective-permute-start.5 = (bf16[2,512,128]{2,1,0:T(8,128)(2,1)S(1)}, bf16[2,512,128]{2,1,0:T(8,128)(2,1)S(1)}, u32[]{:S(2)}, u32[]{:S(2)}) collective-permute-start(bf16[2,512,128]{2,1,0:T(8,128)(2,1)S(1)} %get-tuple-element.19), channel_id=1, source_target_pairs={{0,56},{8,0},{16,8},{24,16},{32,24},{40,32},{48,40},{56,48},{1,57}... | collective-permute-start | bytes 786440 | tf_op jit(solution)/shard_map/ppermute | solution.py:197
  24.1 0.1 fusion.14
  24.2 0.0 copy-start.5
  24.2 4.4 %collective-permute-done.4 = bf16[2,512,128]{2,1,0:T(8,128)(2,1)S(1)} collective-permute-done((bf16[2,512,128]{2,1,0:T(8,128)(2,1)S(1)}, bf16[2,512,128]{2,1,0:T(8,128)(2,1)S(1)}, u32[]{:S(2)}, u32[]{:S(2)}) %collective-permute-start.4) | collective-permute-done | bytes 262176 | tf_op jit(solution)/shard_map/ppermute | solution.py:197
  28.6 0.0 collective-permute-done.5
  28.6 2.8 %collective-permute-start.6 = (bf16[4,512,128]{2,1,0:T(8,128)(2,1)S(1)}, bf16[4,512,128]{2,1,0:T(8,128)(2,1)S(1)}, u32[]{:S(2)}, u32[]{:S(2)}) collective-permute-start(bf16[4,512,128]{2,1,0:T(8,128)(2,1)S(1)} %constant_dynamic-update-slice_fusion.refs_4_), channel_id=1, source_target_pairs={{0,1},{1,0},{2,3},{3,2},{4,5},{5,4},{6,7},{7,6},{8,9},{9,8},{10,11... | collective-permute-start | bytes 1572872 | tf_op jit(solution)/shard_map/ppermute | solution.py:193
  31.4 0.1 pad_add_fusion.1.refs_0_
  31.5 0.1 pad_maximum_fusion.refs_4_
  31.6 0.1 collective-permute-start.3
  31.7 5.2 %all-to-all-done.refs_3_ = bf16[16,272,128]{2,1,0:T(8,128)(2,1)S(1)} async-done(((bf16[16,272,128]{2,1,0:T(8,128)(2,1)}), bf16[16,272,128]{2,1,0:T(8,128)(2,1)S(1)}, u32[]{:S(2)}, u32[]{:S(2)}) %all-to-all-start) | async-done | bytes 1114144 | tf_op jit(solution)/shard_map/all_to_all | solution.py:189
  37.0 0.0 collective-permute-done.6.refs_5_
  37.0 0.0 copy-start.3
  37.0 0.8 copy-done.3
  37.8 0.0 copy-done.5
  37.8 0.0 copy-start.4
  37.8 1.0 %copy-done.4 = bf16[4,512,128]{2,1,0:T(8,128)(2,1)S(1)} copy-done((bf16[4,512,128]{2,1,0:T(8,128)(2,1)S(1)}, bf16[4,512,128]{2,1,0:T(8,128)(2,1)}, u32[]{:S(2)}) %copy-start.4) | copy-done | bytes 524312
  38.8 6.6 %shard_map.87 = (f32[4096,128]{1,0:T(8,128)S(1)}, bf16[4,512,128]{2,1,0:T(8,128)(2,1)S(1)}, bf16[4,512,128]{2,1,0:T(8,128)(2,1)}) custom-call(s32[5]{0:T(128)S(1)} %pad_add_fusion.1.refs_0_, s32[2]{0:T(128)S(1)} %copy-done.5, s32[16,32]{1,0:T(8,128)S(1)} %bitcast.31, bf16[16,272,128]{2,1,0:T(8,128)(2,1)S(1)} %all-to-all-done.refs_3_, ...), custom_call_target="tpu_custom_call" | custom-call | flops 3221225472 | bytes 8388608 | tf_op jit(solution)/shard_map/pallas_call | solution.py:248
  45.4 5.2 %collective-permute-start.8 = (bf16[4,512,128]{2,1,0:T(8,128)(2,1)}, bf16[4,512,128]{2,1,0:T(8,128)(2,1)}, u32[]{:S(2)}, u32[]{:S(2)}) collective-permute-start(bf16[4,512,128]{2,1,0:T(8,128)(2,1)} %get-tuple-element.13), channel_id=1, source_target_pairs={{0,1},{1,0},{2,3},{3,2},{4,5},{5,4},{6,7},{7,6},{8,9},{9,8},{10,11... | collective-permute-start | bytes 1572872 | tf_op jit(solution)/shard_map/ppermute | solution.py:193
  50.6 0.1 pad_add_fusion.refs_0_
  50.6 0.0 collective-permute-done.3.refs_5_
  50.6 0.0 copy-start.1
  50.6 0.8 copy-done.1
  51.4 0.0 copy-start.2
  51.5 1.0 %copy-done.2 = bf16[4,512,128]{2,1,0:T(8,128)(2,1)S(1)} copy-done((bf16[4,512,128]{2,1,0:T(8,128)(2,1)S(1)}, bf16[4,512,128]{2,1,0:T(8,128)(2,1)}, u32[]{:S(2)}) %copy-start.2) | copy-done | bytes 524312
  52.5 6.8 %shard_map.88 = (bf16[4096,128]{1,0:T(8,128)(2,1)}, bf16[4,512,128]{2,1,0:T(8,128)(2,1)S(1)}, bf16[4,512,128]{2,1,0:T(8,128)(2,1)S(1)}) custom-call(s32[5]{0:T(128)S(1)} %pad_add_fusion.refs_0_, s32[2]{0:T(128)S(1)} %copy-done.5, s32[16,32]{1,0:T(8,128)S(1)} %bitcast.32, bf16[16,272,128]{2,1,0:T(8,128)(2,1)S(1)} %all-to-all-done.refs_3_, ...), custom_call_target="tpu_custom_call" | custom-call | flops 3221225472 | bytes 8388608 | tf_op jit(solution)/shard_map/pallas_call | solution.py:248
  59.3 1.9 %collective-permute-start.7 = (bf16[4,512,128]{2,1,0:T(8,128)(2,1)S(1)}, bf16[4,512,128]{2,1,0:T(8,128)(2,1)S(1)}, u32[]{:S(2)}, u32[]{:S(2)}) collective-permute-start(bf16[4,512,128]{2,1,0:T(8,128)(2,1)S(1)} %get-tuple-element.11), channel_id=1, source_target_pairs={{0,1},{1,0},{2,3},{3,2},{4,5},{5,4},{6,7},{7,6},{8,9},{9,8},{10,11... | collective-permute-start | bytes 1572872 | tf_op jit(solution)/shard_map/ppermute | solution.py:193
  61.2 3.7 %all-to-all-start.1 = ((bf16[16,256,128]{2,1,0:T(8,128)(2,1)}), bf16[16,256,128]{2,1,0:T(8,128)(2,1)S(1)}, u32[]{:S(2)}, u32[]{:S(2)}) async-start(bf16[16,256,128]{2,1,0:T(8,128)(2,1)} %bitcast.8), calls=%async_computation.1 | async-start | bytes 2097152 | tf_op jit(solution)/shard_map/all_to_all | solution.py:189
  64.9 0.0 collective-permute-done.8
  64.9 1.2 %add_convert_fusion = bf16[4,512,128]{2,1,0:T(8,128)(2,1)S(1)} fusion(bf16[4,512,128]{2,1,0:T(8,128)(2,1)} %collective-permute-done.8, bf16[4,512,128]{2,1,0:T(8,128)(2,1)S(1)} %get-tuple-element.12), kind=kLoop, calls=%fused_computation | loop fusion | flops 1048576 | bytes 1572864 | tf_op jit(solution)/shard_map/convert_element_type | solution.py:284
  66.1 0.3 collective-permute-start.11
  66.4 1.5 %collective-permute-start.9 = (bf16[2,512,128]{2,1,0:T(8,128)(2,1)S(1)}, bf16[2,512,128]{2,1,0:T(8,128)(2,1)S(1)}, u32[]{:S(2)}, u32[]{:S(2)}) collective-permute-start(bf16[2,512,128]{2,1,0:T(8,128)(2,1)S(1)} %get-tuple-element.17), channel_id=1, source_target_pairs={{0,8},{8,16},{16,24},{24,32},{32,40},{40,48},{48,56},{56,0},{1,9},... | collective-permute-start | bytes 786440 | tf_op jit(solution)/shard_map/ppermute | solution.py:197
  67.8 0.0 collective-permute-done.7
  67.8 0.1 convert_add_fusion
  68.0 6.4 %collective-permute-done.11 = bf16[2,512,128]{2,1,0:T(8,128)(2,1)S(1)} collective-permute-done((bf16[2,512,128]{2,1,0:T(8,128)(2,1)S(1)}, bf16[2,512,128]{2,1,0:T(8,128)(2,1)S(1)}, u32[]{:S(2)}, u32[]{:S(2)}) %collective-permute-start.11) | collective-permute-done | bytes 262176 | tf_op jit(solution)/shard_map/ppermute | solution.py:197
  74.3 1.3 %collective-permute-done.9 = bf16[2,512,128]{2,1,0:T(8,128)(2,1)S(1)} collective-permute-done((bf16[2,512,128]{2,1,0:T(8,128)(2,1)S(1)}, bf16[2,512,128]{2,1,0:T(8,128)(2,1)S(1)}, u32[]{:S(2)}, u32[]{:S(2)}) %collective-permute-start.9) | collective-permute-done | bytes 262176 | tf_op jit(solution)/shard_map/ppermute | solution.py:197
  75.6 0.1 fusion.9
  75.7 0.1 collective-permute-start.10
  75.8 2.7 %collective-permute-start.12 = (bf16[512,128]{1,0:T(8,128)(2,1)S(1)}, bf16[512,128]{1,0:T(8,128)(2,1)S(1)}, u32[]{:S(2)}, u32[]{:S(2)}) collective-permute-start(bf16[512,128]{1,0:T(8,128)(2,1)S(1)} %get-tuple-element.16), channel_id=1, source_target_pairs={{0,56},{8,0},{16,8},{24,16},{32,24},{40,32},{48,40},{56,48},{1,57}... | collective-permute-start | bytes 393224 | tf_op jit(solution)/shard_map/ppermute | solution.py:197
  78.5 0.0 collective-permute-start.13
  78.5 2.7 %collective-permute-done.10 = bf16[512,128]{1,0:T(8,128)(2,1)S(1)} collective-permute-done((bf16[512,128]{1,0:T(8,128)(2,1)S(1)}, bf16[512,128]{1,0:T(8,128)(2,1)S(1)}, u32[]{:S(2)}, u32[]{:S(2)}) %collective-permute-start.10) | collective-permute-done | bytes 131104 | tf_op jit(solution)/shard_map/ppermute | solution.py:197
  81.3 4.3 %collective-permute-done.12 = bf16[512,128]{1,0:T(8,128)(2,1)S(1)} collective-permute-done((bf16[512,128]{1,0:T(8,128)(2,1)S(1)}, bf16[512,128]{1,0:T(8,128)(2,1)S(1)}, u32[]{:S(2)}, u32[]{:S(2)}) %collective-permute-start.12) | collective-permute-done | bytes 131104 | tf_op jit(solution)/shard_map/ppermute | solution.py:197
  85.6 0.7 collective-permute-done.13
  86.3 0.7 fusion.8
  87.0 0.0 all-to-all-done.1
  87.0 0.8 reduce_sum.12
  (8 shorter events, 0.2 us)
Async XLA Ops:
  0.6 1.0 %copy-start = (bf16[1,1024,128]{2,1,0:T(8,128)(2,1)S(1)}, bf16[1,1024,128]{2,1,0:T(8,128)(2,1)}, u32[]{:S(2)}) copy-start(bf16[1,1024,128]{2,1,0:T(8,128)(2,1)} %param.8) | copy-start | bytes 786436
  1.6 19.6 %collective-permute-start = (bf16[512,128]{1,0:T(8,128)(2,1)S(1)}, bf16[512,128]{1,0:T(8,128)(2,1)S(1)}, u32[]{:S(2)}, u32[]{:S(2)}) collective-permute-start(bf16[512,128]{1,0:T(8,128)(2,1)S(1)} %fusion.15), channel_id=1, source_target_pairs={{0,8},{8,16},{16,24},{24,32},{32,40},{40,48},{48,56},{56,0},{1,9},... | collective-permute-start | bytes 393224 | tf_op jit(solution)/shard_map/ppermute | solution.py:197
  4.1 17.0 %collective-permute-start.1 = (bf16[512,128]{1,0:T(8,128)(2,1)S(1)}, bf16[512,128]{1,0:T(8,128)(2,1)S(1)}, u32[]{:S(2)}, u32[]{:S(2)}) collective-permute-start(bf16[512,128]{1,0:T(8,128)(2,1)S(1)} %fusion.15), channel_id=1, source_target_pairs={{0,56},{8,0},{16,8},{24,16},{32,24},{40,32},{48,40},{56,48},{1,57}... | collective-permute-start | bytes 393224 | tf_op jit(solution)/shard_map/ppermute | solution.py:197
  8.2 13.0 %collective-permute-start.2 = (bf16[512,128]{1,0:T(8,128)(2,1)S(1)}, bf16[512,128]{1,0:T(8,128)(2,1)S(1)}, u32[]{:S(2)}, u32[]{:S(2)}) collective-permute-start(bf16[512,128]{1,0:T(8,128)(2,1)S(1)} %fusion.15), channel_id=1, source_target_pairs={{0,32},{8,40},{16,48},{24,56},{32,0},{40,8},{48,16},{56,24},{1,33}... | collective-permute-start | bytes 393224 | tf_op jit(solution)/shard_map/ppermute | solution.py:197
  14.3 7.1 %copy-start.6 = (s32[8]{0:T(128)S(1)}, s32[8]{0:T(128)}, u32[]{:S(2)}) copy-start(s32[8]{0:T(128)} %constant.44.clone) | copy-start | bytes 100
  14.3 22.7 %all-to-all-start = ((bf16[16,272,128]{2,1,0:T(8,128)(2,1)}), bf16[16,272,128]{2,1,0:T(8,128)(2,1)S(1)}, u32[]{:S(2)}, u32[]{:S(2)}) async-start(bf16[16,272,128]{2,1,0:T(8,128)(2,1)} %shard_map.86), calls=%async_computation | async-start | bytes 2228224 | tf_op jit(solution)/shard_map/all_to_all | solution.py:189
  21.3 7.3 %collective-permute-start.4 = (bf16[2,512,128]{2,1,0:T(8,128)(2,1)S(1)}, bf16[2,512,128]{2,1,0:T(8,128)(2,1)S(1)}, u32[]{:S(2)}, u32[]{:S(2)}) collective-permute-start(bf16[2,512,128]{2,1,0:T(8,128)(2,1)S(1)} %get-tuple-element.20), channel_id=1, source_target_pairs={{0,8},{8,16},{16,24},{24,32},{32,40},{40,48},{48,56},{56,0},{1,9},... | collective-permute-start | bytes 786440 | tf_op jit(solution)/shard_map/ppermute | solution.py:197
  21.4 7.2 %collective-permute-start.5 = (bf16[2,512,128]{2,1,0:T(8,128)(2,1)S(1)}, bf16[2,512,128]{2,1,0:T(8,128)(2,1)S(1)}, u32[]{:S(2)}, u32[]{:S(2)}) collective-permute-start(bf16[2,512,128]{2,1,0:T(8,128)(2,1)S(1)} %get-tuple-element.19), channel_id=1, source_target_pairs={{0,56},{8,0},{16,8},{24,16},{32,24},{40,32},{48,40},{56,48},{1,57}... | collective-permute-start | bytes 786440 | tf_op jit(solution)/shard_map/ppermute | solution.py:197
  24.2 13.6 %copy-start.5 = (s32[2]{0:T(128)S(1)}, s32[2]{0:T(128)}, u32[]{:S(2)}) copy-start(s32[2]{0:T(128)} %refs_1_.3) | copy-start | bytes 28
  28.6 8.3 %collective-permute-start.6 = (bf16[4,512,128]{2,1,0:T(8,128)(2,1)S(1)}, bf16[4,512,128]{2,1,0:T(8,128)(2,1)S(1)}, u32[]{:S(2)}, u32[]{:S(2)}) collective-permute-start(bf16[4,512,128]{2,1,0:T(8,128)(2,1)S(1)} %constant_dynamic-update-slice_fusion.refs_4_), channel_id=1, source_target_pairs={{0,1},{1,0},{2,3},{3,2},{4,5},{5,4},{6,7},{7,6},{8,9},{9,8},{10,11... | collective-permute-start | bytes 1572872 | tf_op jit(solution)/shard_map/ppermute | solution.py:193
  31.6 19.0 %collective-permute-start.3 = (bf16[4,512,128]{2,1,0:T(8,128)(2,1)S(1)}, bf16[4,512,128]{2,1,0:T(8,128)(2,1)S(1)}, u32[]{:S(2)}, u32[]{:S(2)}) collective-permute-start(bf16[4,512,128]{2,1,0:T(8,128)(2,1)S(1)} %pad_maximum_fusion.refs_4_), channel_id=1, source_target_pairs={{0,1},{1,0},{2,3},{3,2},{4,5},{5,4},{6,7},{7,6},{8,9},{9,8},{10,11... | collective-permute-start | bytes 1572872 | tf_op jit(solution)/shard_map/ppermute | solution.py:193
  37.0 0.8 copy-start.3
  37.8 1.0 %copy-start.4 = (bf16[4,512,128]{2,1,0:T(8,128)(2,1)S(1)}, bf16[4,512,128]{2,1,0:T(8,128)(2,1)}, u32[]{:S(2)}) copy-start(bf16[4,512,128]{2,1,0:T(8,128)(2,1)} %copy-done.3) | copy-start | bytes 1572868
  45.4 19.5 %collective-permute-start.8 = (bf16[4,512,128]{2,1,0:T(8,128)(2,1)}, bf16[4,512,128]{2,1,0:T(8,128)(2,1)}, u32[]{:S(2)}, u32[]{:S(2)}) collective-permute-start(bf16[4,512,128]{2,1,0:T(8,128)(2,1)} %get-tuple-element.13), channel_id=1, source_target_pairs={{0,1},{1,0},{2,3},{3,2},{4,5},{5,4},{6,7},{7,6},{8,9},{9,8},{10,11... | collective-permute-start | bytes 1572872 | tf_op jit(solution)/shard_map/ppermute | solution.py:193
  50.6 0.8 copy-start.1
  51.4 1.0 %copy-start.2 = (bf16[4,512,128]{2,1,0:T(8,128)(2,1)S(1)}, bf16[4,512,128]{2,1,0:T(8,128)(2,1)}, u32[]{:S(2)}) copy-start(bf16[4,512,128]{2,1,0:T(8,128)(2,1)} %copy-done.1) | copy-start | bytes 1572868
  59.3 8.5 %collective-permute-start.7 = (bf16[4,512,128]{2,1,0:T(8,128)(2,1)S(1)}, bf16[4,512,128]{2,1,0:T(8,128)(2,1)S(1)}, u32[]{:S(2)}, u32[]{:S(2)}) collective-permute-start(bf16[4,512,128]{2,1,0:T(8,128)(2,1)S(1)} %get-tuple-element.11), channel_id=1, source_target_pairs={{0,1},{1,0},{2,3},{3,2},{4,5},{5,4},{6,7},{7,6},{8,9},{9,8},{10,11... | collective-permute-start | bytes 1572872 | tf_op jit(solution)/shard_map/ppermute | solution.py:193
  61.2 25.8 %all-to-all-start.1 = ((bf16[16,256,128]{2,1,0:T(8,128)(2,1)}), bf16[16,256,128]{2,1,0:T(8,128)(2,1)S(1)}, u32[]{:S(2)}, u32[]{:S(2)}) async-start(bf16[16,256,128]{2,1,0:T(8,128)(2,1)} %bitcast.8), calls=%async_computation.1 | async-start | bytes 2097152 | tf_op jit(solution)/shard_map/all_to_all | solution.py:189
  66.1 8.2 %collective-permute-start.11 = (bf16[2,512,128]{2,1,0:T(8,128)(2,1)S(1)}, bf16[2,512,128]{2,1,0:T(8,128)(2,1)S(1)}, u32[]{:S(2)}, u32[]{:S(2)}) collective-permute-start(bf16[2,512,128]{2,1,0:T(8,128)(2,1)S(1)} %get-tuple-element.18), channel_id=1, source_target_pairs={{0,56},{8,0},{16,8},{24,16},{32,24},{40,32},{48,40},{56,48},{1,57}... | collective-permute-start | bytes 786440 | tf_op jit(solution)/shard_map/ppermute | solution.py:197
  66.4 9.2 %collective-permute-start.9 = (bf16[2,512,128]{2,1,0:T(8,128)(2,1)S(1)}, bf16[2,512,128]{2,1,0:T(8,128)(2,1)S(1)}, u32[]{:S(2)}, u32[]{:S(2)}) collective-permute-start(bf16[2,512,128]{2,1,0:T(8,128)(2,1)S(1)} %get-tuple-element.17), channel_id=1, source_target_pairs={{0,8},{8,16},{16,24},{24,32},{32,40},{40,48},{48,56},{56,0},{1,9},... | collective-permute-start | bytes 786440 | tf_op jit(solution)/shard_map/ppermute | solution.py:197
  75.7 5.5 %collective-permute-start.10 = (bf16[512,128]{1,0:T(8,128)(2,1)S(1)}, bf16[512,128]{1,0:T(8,128)(2,1)S(1)}, u32[]{:S(2)}, u32[]{:S(2)}) collective-permute-start(bf16[512,128]{1,0:T(8,128)(2,1)S(1)} %get-tuple-element.14), channel_id=1, source_target_pairs={{0,8},{8,16},{16,24},{24,32},{32,40},{40,48},{48,56},{56,0},{1,9},... | collective-permute-start | bytes 393224 | tf_op jit(solution)/shard_map/ppermute | solution.py:197
  75.8 9.7 %collective-permute-start.12 = (bf16[512,128]{1,0:T(8,128)(2,1)S(1)}, bf16[512,128]{1,0:T(8,128)(2,1)S(1)}, u32[]{:S(2)}, u32[]{:S(2)}) collective-permute-start(bf16[512,128]{1,0:T(8,128)(2,1)S(1)} %get-tuple-element.16), channel_id=1, source_target_pairs={{0,56},{8,0},{16,8},{24,16},{32,24},{40,32},{48,40},{56,48},{1,57}... | collective-permute-start | bytes 393224 | tf_op jit(solution)/shard_map/ppermute | solution.py:197
  78.5 7.8 %collective-permute-start.13 = (bf16[512,128]{1,0:T(8,128)(2,1)S(1)}, bf16[512,128]{1,0:T(8,128)(2,1)S(1)}, u32[]{:S(2)}, u32[]{:S(2)}) collective-permute-start(bf16[512,128]{1,0:T(8,128)(2,1)S(1)} %get-tuple-element.15), channel_id=1, source_target_pairs={{0,32},{8,40},{16,48},{24,56},{32,0},{40,8},{48,16},{56,24},{1,33}... | collective-permute-start | bytes 393224 | tf_op jit(solution)/shard_map/ppermute | solution.py:197

commit v4 on v3

v4 whole, which is shorter than its diff:
```python
import functools
import math

import jax
import jax.numpy as jnp
from jax import lax
from jax.experimental import pallas as pl
from jax.experimental.pallas import tpu as pltpu
from jax.sharding import Mesh, PartitionSpec as P

SHARPNESS = 4.0
SLOPE_SCALE = 0.5
HOT_SHIFT = 2.0

NX, NZ, NY, NC = 4, 8, 4, 2
PLANE = NX * NY
QT = 32
W = 128
Q_DEV = 8
PAIR_DEV = 64
PATCHES = 1024
HALF = PATCHES // 2
CAP = 2
ROWS = Q_DEV * QT
SEND_ROWS = ROWS + 16
ENTRIES = NZ * CAP
GROUP = 8
BLOCK = 128
LOG2 = 4.0 * math.log2(math.e)
ITEMS = 4
SLOTS = PLANE * CAP
LIST = SLOTS + GROUP
PART = NZ // 2
STEPS = (0, -1, 1, 4, -2, 3, 2, -3)


def pack_kernel(page_ref, query_ref, label_ref, core_ref, rows_ref, whole_ref, out_ref, half_ref):
    half_ref[...] = whole_ref[pl.ds(pl.multiple_of(core_ref[0] * HALF, HALF), HALF), :]
    dest = lax.broadcasted_iota(jnp.int32, (PLANE, W), 0)
    lane = lax.broadcasted_iota(jnp.int32, (PLANE, W), 1)
    entry = lane % ENTRIES
    rank = entry % CAP
    wanted = (dest // NY) * (NZ * NY) + (entry // CAP) * NY + dest % NY
    is_query = lane < ENTRIES
    is_label = jnp.logical_and(lane >= ENTRIES, lane < 2 * ENTRIES)

    def visit(i, carry):
        table, seen = carry
        hit = wanted == page_ref[i]
        value = jnp.where(is_query, query_ref[i] + 1, jnp.where(is_label, label_ref[i], 0))
        table = jnp.where(jnp.logical_and(hit, seen == rank), value, table)
        return table, seen + hit.astype(jnp.int32)

    zeros = jnp.zeros((PLANE, W), jnp.int32)
    table, _ = lax.fori_loop(0, PAIR_DEV, visit, (zeros, zeros), unroll=8)
    table = table.astype(jnp.float32)
    rows = rows_ref[...]
    for d in range(PLANE):
        out_ref[d, :ROWS, :] = rows
        out_ref[d, ROWS:, :] = jnp.broadcast_to(table[d : d + 1, :], (16, W)).astype(jnp.bfloat16)


def score_kernel(
    offset, column_ref, hot_ref, table_ref, got_ref, mine_ref, other_ref,
    query_out, far_mine, far_other, near_mine, near_other,
    slot_query, slot_label, item_page, item_base, item_left, turned, query_acc, page_acc, *work,
):
    rows = GROUP * QT
    token_refs, logit_refs, expo_refs = work[:ITEMS], work[ITEMS : 2 * ITEMS], work[2 * ITEMS :]
    query_acc[...] = jnp.zeros_like(query_acc)
    page_acc[...] = jnp.zeros_like(page_acc)
    first_page = column_ref[NZ]

    def list_page(page, items):
        height = column_ref[page]
        turned[page, :, :HALF] = mine_ref[page].T
        turned[page, :, HALF:] = other_ref[page].T
        start = page * LIST
        count = jnp.int32(0)
        for s in range(PLANE):
            for r in range(CAP):
                code = table_ref[s, height * CAP + r]
                slot_query[start + count] = s * Q_DEV + code - 1
                slot_label[start + count] = table_ref[s, ENTRIES + height * CAP + r]
                count = count + (code > 0).astype(jnp.int32)
        for g in range(GROUP - 1):
            slot_query[start + count + g] = 0
            slot_label[start + count + g] = 0
        for j in range(SLOTS // GROUP):
            item_page[items] = page
            item_base[items] = start + j * GROUP
            item_left[items] = count - j * GROUP
            items = items + (count > j * GROUP).astype(jnp.int32)
        return items

    items = lax.fori_loop(0, NZ, list_page, jnp.int32(0))
    for g in range(GROUP):
        slot_query[NZ * LIST + g] = 0
        slot_label[NZ * LIST + g] = 0
    for u in range(ITEMS):
        item_page[items + u] = 0
        item_base[items + u] = NZ * LIST
        item_left[items + u] = 0

    def per_round(step, _):
        at = [step * ITEMS + u for u in range(ITEMS)]
        page = [item_page[i] for i in at]
        base = [item_base[i] for i in at]
        left = [item_left[i] for i in at]
        query = [[slot_query[b + g] for g in range(GROUP)] for b in base]
        for u in range(ITEMS):
            for g in range(GROUP):
                token_refs[u][g * QT : (g + 1) * QT, :] = got_ref[
                    lax.shift_right_logical(query[u][g], 3),
                    pl.ds(pl.multiple_of(lax.bitwise_and(query[u][g], Q_DEV - 1) * QT, QT), QT),
                    :,
                ]
        dims = (((1,), (1,)), ((), ()))
        peaks, lses, inverses = [], [], []
        blocks = PATCHES // BLOCK
        tops, totals = [None] * ITEMS, [None] * ITEMS

        def multiply(u, c):
            part = (mine_ref, other_ref)[c * BLOCK // HALF]
            first = c * BLOCK % HALF
            block = lax.dot_general(
                part[page[u], first : first + BLOCK, :], token_refs[u][...], dims,
                preferred_element_type=jnp.float32,
            )
            logit_refs[u][c * BLOCK : (c + 1) * BLOCK, :] = block
            top = jnp.max(block.reshape(BLOCK // 8, 8, rows), axis=0)
            tops[u] = top if c == 0 else jnp.maximum(tops[u], top)

        def raise_e(u, c):
            piece = logit_refs[u][c * BLOCK : (c + 1) * BLOCK, :]
            e = jnp.exp2(LOG2 * (piece - peaks[u]))
            expo_refs[u][c * BLOCK : (c + 1) * BLOCK, :] = e.astype(jnp.bfloat16)
            low = jnp.sum(e.reshape(BLOCK // 8, 8, rows), axis=0)
            totals[u] = low if c == 0 else totals[u] + low

        grads = []
        for c in range(blocks):
            multiply(0, c)
        for u in range(ITEMS):
            peaks.append(jnp.max(tops[u], axis=0, keepdims=True))
            for c in range(blocks):
                if u + 1 < ITEMS:
                    multiply(u + 1, c)
                raise_e(u, c)
            total = jnp.sum(totals[u], axis=0, keepdims=True)
            lse = SHARPNESS * peaks[u] + jnp.log(total)
            lses.append(jnp.broadcast_to(lse, (W, rows)).T)
            inverses.append(jnp.broadcast_to(1.0 / total, (W, rows)).T)
            grads.append(
                jnp.dot(turned[page[u]], expo_refs[u][...], preferred_element_type=jnp.float32).T
            )
        scale = []
        for u in range(ITEMS):
            page_id = first_page + column_ref[page[u]] * NY
            hot = jnp.logical_or(hot_ref[0] == page_id, hot_ref[1] == page_id)
            shift = jnp.where(hot, HOT_SHIFT, 0.0).astype(jnp.float32)
            parts = []
            for g in range(GROUP):
                mine = slice(g * QT, (g + 1) * QT)
                score = jnp.sum(lses[u][mine], axis=0, keepdims=True) / SHARPNESS
                logit = SLOPE_SCALE * score + offset - shift
                label = slot_label[base[u] + g].astype(jnp.float32)
                live = jnp.where(g < left[u], SLOPE_SCALE, 0.0)
                slope = live * (1.0 / (1.0 + jnp.exp(-logit)) - label)
                parts.append(slope * inverses[u][mine])
            scale.append(jnp.concatenate(parts, axis=0))
        for u in range(ITEMS):
            scaled = (token_refs[u][...].astype(jnp.float32) * scale[u]).astype(jnp.bfloat16)
            page_acc[page[u]] += jnp.dot(
                expo_refs[u][...], scaled, preferred_element_type=jnp.float32
            )
        for u in range(ITEMS):
            grad = grads[u] * scale[u]
            for g in range(GROUP):
                rows_at = pl.ds(pl.multiple_of(query[u][g] * QT, QT), QT)
                query_acc[rows_at, :] += grad[g * QT : (g + 1) * QT]
        return 0

    lax.fori_loop(0, (items + ITEMS - 1) // ITEMS, per_round, 0)
    for k in range(PART):
        near_mine[k] = page_acc[k, :HALF, :].astype(jnp.bfloat16)
        near_other[k] = page_acc[k, HALF:, :].astype(jnp.bfloat16)
        far_mine[k] = page_acc[PART + k, :HALF, :].astype(jnp.bfloat16)
        far_other[k] = page_acc[PART + k, HALF:, :].astype(jnp.bfloat16)
    query_out[...] = query_acc[...].astype(jnp.bfloat16)


def exchange(array, axes):
    return lax.all_to_all(array, axes, split_axis=0, concat_axis=0, tiled=True)


def swap_cores(array):
    return lax.ppermute(array, "core", [(0, 1), (1, 0)])


def move(array, step):
    return lax.ppermute(array, "z", [(i, (i + step) % NZ) for i in range(NZ)])


def gather_column(half):
    below, above, across = move(half, 1), move(half, -1), move(half, 4)
    far_below = move(jnp.stack([below, across]), 1)
    far_above = move(jnp.stack([above, across]), -1)
    return jnp.concatenate([jnp.stack([half, below, above, across]), far_below, far_above])


def add(mine, other):
    return mine.astype(jnp.float32) + other.astype(jnp.float32)


def reduce_column(mine, other, from_below, from_above):
    up = (add(mine[2], other[2]) + from_below[0].astype(jnp.float32)).astype(jnp.bfloat16)
    down = (add(mine[1], other[1]) + from_above[0].astype(jnp.float32)).astype(jnp.bfloat16)
    over = (add(mine[3], other[3]) + add(from_below[1], from_above[1])).astype(jnp.bfloat16)
    total = add(mine[0], other[0])
    for part in (move(up, 1), move(down, -1), move(over, 4)):
        total = total + part.astype(jnp.float32)
    return total.astype(jnp.bfloat16)


def score(column, hot_pages, table, got, mine, other):
    offset = -SLOPE_SCALE * QT * (math.log(PATCHES) / SHARPNESS + SHARPNESS / 2.0)
    smem = pl.BlockSpec(memory_space=pltpu.SMEM)
    vmem = pl.BlockSpec(memory_space=pltpu.VMEM)
    return pl.pallas_call(
        functools.partial(score_kernel, offset),
        out_shape=(jax.ShapeDtypeStruct((PLANE * ROWS, W), jnp.bfloat16),)
        + (jax.ShapeDtypeStruct((PART, HALF, W), jnp.bfloat16),) * 4,
        in_specs=[smem, smem, smem, vmem, vmem, vmem],
        out_specs=(vmem,) * 5,
        scratch_shapes=[
            pltpu.SMEM((NZ * LIST + GROUP,), jnp.int32),
            pltpu.SMEM((NZ * LIST + GROUP,), jnp.int32),
            pltpu.SMEM((NZ * SLOTS // GROUP + ITEMS,), jnp.int32),
            pltpu.SMEM((NZ * SLOTS // GROUP + ITEMS,), jnp.int32),
            pltpu.SMEM((NZ * SLOTS // GROUP + ITEMS,), jnp.int32),
            pltpu.VMEM((NZ, W, PATCHES), jnp.bfloat16),
            pltpu.VMEM((PLANE * ROWS, W), jnp.float32),
            pltpu.VMEM((NZ, PATCHES, W), jnp.float32),
        ]
        + [pltpu.VMEM((GROUP * QT, W), jnp.bfloat16)] * ITEMS
        + [pltpu.VMEM((PATCHES, GROUP * QT), jnp.float32)] * ITEMS
        + [pltpu.VMEM((PATCHES, GROUP * QT), jnp.bfloat16)] * ITEMS,
        compiler_params=pltpu.CompilerParams(vmem_limit_bytes=26 << 20),
    )(column, hot_pages, table, got, mine, other)


def shards(queries, pages, pair_page, pair_query, pair_label, hot_pages):
    smem = pl.BlockSpec(memory_space=pltpu.SMEM)
    vmem = pl.BlockSpec(memory_space=pltpu.VMEM)
    core = lax.axis_index("core").reshape(1)
    send, half = pl.pallas_call(
        pack_kernel,
        out_shape=(
            jax.ShapeDtypeStruct((PLANE, SEND_ROWS, W), jnp.bfloat16),
            jax.ShapeDtypeStruct((HALF, W), jnp.bfloat16),
        ),
        in_specs=[smem] * 4 + [vmem] * 2,
        out_specs=(vmem, vmem),
    )(pair_page[:, 0], pair_query, pair_label, core, queries.reshape(ROWS, W), pages[0])
    mine = gather_column(half)
    other = swap_cores(mine)
    got = exchange(send, ("x", "y"))
    table = got[:, ROWS, : 2 * ENTRIES].astype(jnp.int32)
    heights = (lax.axis_index("z") + jnp.array(STEPS, jnp.int32)) % NZ
    first_page = lax.axis_index("x") * (NZ * NY) + lax.axis_index("y")
    column = jnp.concatenate([heights, first_page.reshape(1)])
    query_part, far_mine, far_other, near_mine, near_other = score(
        column, hot_pages, table, got, mine, other
    )
    far_other, near_other = swap_cores(far_other), swap_cores(near_other)
    to_above = add(far_mine[2:4], far_other[2:4]).astype(jnp.bfloat16)
    to_below = add(far_mine[0:2], far_other[0:2]).astype(jnp.bfloat16)
    from_below, from_above = move(to_above, 1), move(to_below, -1)
    query_back = exchange(query_part.reshape(PLANE, ROWS, W), ("x", "y"))
    page_grad = reduce_column(near_mine, near_other, from_below, from_above)
    query_grad = jnp.sum(query_back.astype(jnp.float32), axis=0).astype(jnp.bfloat16)
    return query_grad.reshape(Q_DEV, QT, W), page_grad[None]


def solution(mesh):
    torus = Mesh(mesh.devices.reshape(NX, NZ, NY, NC), ("x", "z", "y", "core"))
    owner = ("x", "z", "y")
    device = ("x", "z", "y", "core")
    return jax.shard_map(
        shards,
        mesh=torus,
        in_specs=(P(device), P(owner), P(device), P(device), P(device), P()),
        out_specs=(P(device), P(owner, "core")),
        check_vma=False,
    )
```

time: 88.9 us -> 81 us (0.911)
  the two profiles are of different devices: /device:TPU:1 before, /device:TPU:33 now
where the time goes in v4:
time: 81 us; the launch traced here: 80.5 us
  starting transfers between devices  33.4 us (41%)
  waiting for transfers between devices  28.8 us (36%)
  Pallas kernels  13.8 us (17%)
  other arithmetic  1.97 us (2%)
  local copies, waits for them, and re-layouts  1.77 us (2%)
  between operations  0.81 us (1%)
    ppermute x10, waiting for transfers between devices, move(): return lax.ppermute(array, 'z', [(i, (i + step) % NZ) for i in range(NZ)])  25.1 us
    ppermute x10, starting transfers between devices, move(): return lax.ppermute(array, 'z', [(i, (i + step) % NZ) for i in range(NZ)])  16.2 us
    all_to_all x2, starting transfers between devices, exchange(): return lax.all_to_all(array, axes, split_axis=0, concat_axis=0, tiled=True)  11.9 us
    pallas_call x1, Pallas kernels, score(): pl.pallas_call(functools.partial(score_kernel, offset), out_shape=(jax.Sh...  11.4 us
    ppermute x3, starting transfers between devices, swap_cores(): return lax.ppermute(array, 'core', [(0, 1), (1, 0)])  5.22 us
    all_to_all x2, waiting for transfers between devices, exchange(): return lax.all_to_all(array, axes, split_axis=0, concat_axis=0, tiled=True)  3.68 us
    pallas_call x1, Pallas kernels, shards(): pl.pallas_call(pack_kernel, out_shape=(jax.ShapeDtypeStruct((PLANE, SEND_...  2.35 us
    unnamed x19, local copies, waits for them, and re-layouts  1.73 us
  transfers between devices with their start and end apart: 15, of which 6 were waited for; matrix products, arithmetic and copies ran while one was open for 2% of the time, Pallas kernels for 0%

profile of v4, /device:TPU:33, one launch (start us, length us, event | category | flops | bytes accessed | tf_op | source)
XLA Modules:
  0.0 80.5 jit_solution(2830751192888229997)
XLA Ops:
  0.6 2.3 %shard_map.86 = (bf16[16,272,128]{2,1,0:T(8,128)(2,1)}, bf16[512,128]{1,0:T(8,128)(2,1)}) custom-call(s32[64]{0:T(128)} %bitcast.41, s32[64]{0:T(128)} %query_ref.1, s32[64]{0:T(128)} %label_ref.1, s32[1]{0:T(128)} %bitcast.2.core_ref, bf16[256,128]{1,0:T(8,128)(2,1)} %bitcast.39, bf16[1024,128]{1,0:T(8,128)(2,1)} %bitcast.38), custom_call_target="tpu_custom_call" | custom-call | tf_op jit(solution)/shard_map/pallas_call | solution.py:257
  3.0 6.0 %collective-permute-start.2 = (bf16[512,128]{1,0:T(8,128)(2,1)}, bf16[512,128]{1,0:T(8,128)(2,1)S(1)}, u32[]{:S(2)}, u32[]{:S(2)}) collective-permute-start(bf16[512,128]{1,0:T(8,128)(2,1)} %get-tuple-element.10), channel_id=1, source_target_pairs={{0,32},{8,40},{16,48},{24,56},{32,0},{40,8},{48,16},{56,24},{1,33}... | collective-permute-start | bytes 393224 | tf_op jit(solution)/shard_map/ppermute | solution.py:202
  9.0 0.7 collective-permute-start.1
  9.7 0.7 collective-permute-start
  10.5 0.0 copy-start.5
  10.5 6.9 %all-to-all-start = ((bf16[16,272,128]{2,1,0:T(8,128)(2,1)}), bf16[16,272,128]{2,1,0:T(8,128)(2,1)S(1)}, u32[]{:S(2)}, u32[]{:S(2)}) async-start(bf16[16,272,128]{2,1,0:T(8,128)(2,1)} %get-tuple-element.9), calls=%async_computation | async-start | bytes 2228224 | tf_op jit(solution)/shard_map/all_to_all | solution.py:194
  17.4 0.0 copy-done.5
  17.4 0.0 collective-permute-done.2
  17.4 1.4 %collective-permute-done.1 = bf16[512,128]{1,0:T(8,128)(2,1)S(1)} collective-permute-done((bf16[512,128]{1,0:T(8,128)(2,1)}, bf16[512,128]{1,0:T(8,128)(2,1)S(1)}, u32[]{:S(2)}, u32[]{:S(2)}) %collective-permute-start.1) | collective-permute-done | bytes 131104 | tf_op jit(solution)/shard_map/ppermute | solution.py:202
  18.8 0.0 collective-permute-done
  18.8 0.0 copy-start.6
  18.8 0.0 copy-start.4
  18.9 0.6 collective-permute-start.4
  19.5 0.9 %collective-permute-start.3 = (bf16[2,512,128]{2,1,0:T(8,128)(2,1)S(1)}, bf16[2,512,128]{2,1,0:T(8,128)(2,1)S(1)}, u32[]{:S(2)}, u32[]{:S(2)}) collective-permute-start(bf16[2,512,128]{2,1,0:T(8,128)(2,1)S(1)} %get-tuple-element.22), channel_id=1, source_target_pairs={{0,8},{8,16},{16,24},{24,32},{32,40},{40,48},{48,56},{56,0},{1,9},... | collective-permute-start | bytes 786440 | tf_op jit(solution)/shard_map/ppermute | solution.py:202
  20.5 6.8 %collective-permute-done.3 = bf16[2,512,128]{2,1,0:T(8,128)(2,1)S(1)} collective-permute-done((bf16[2,512,128]{2,1,0:T(8,128)(2,1)S(1)}, bf16[2,512,128]{2,1,0:T(8,128)(2,1)S(1)}, u32[]{:S(2)}, u32[]{:S(2)}) %collective-permute-start.3) | collective-permute-done | bytes 262176 | tf_op jit(solution)/shard_map/ppermute | solution.py:202
  27.4 0.0 collective-permute-done.4
  27.4 1.9 %collective-permute-start.5 = (bf16[8,512,128]{2,1,0:T(8,128)(2,1)S(1)}, bf16[8,512,128]{2,1,0:T(8,128)(2,1)S(1)}, u32[]{:S(2)}, u32[]{:S(2)}) collective-permute-start(bf16[8,512,128]{2,1,0:T(8,128)(2,1)S(1)} %constant_dynamic-update-slice_fusion.mine_ref), channel_id=1, source_target_pairs={{0,1},{1,0},{2,3},{3,2},{4,5},{5,4},{6,7},{7,6},{8,9},{9,8},{10,11... | collective-permute-start | bytes 3145736 | tf_op jit(solution)/shard_map/ppermute | solution.py:198
  29.4 0.0 copy-done.6
  29.4 0.1 pad_add_fusion.column_ref
  29.4 3.7 %all-to-all-done.got_ref = bf16[16,272,128]{2,1,0:T(8,128)(2,1)S(1)} async-done(((bf16[16,272,128]{2,1,0:T(8,128)(2,1)}), bf16[16,272,128]{2,1,0:T(8,128)(2,1)S(1)}, u32[]{:S(2)}, u32[]{:S(2)}) %all-to-all-start) | async-done | bytes 1114144 | tf_op jit(solution)/shard_map/all_to_all | solution.py:194
  33.1 0.0 collective-permute-done.5.other_ref
  33.2 0.0 copy-done.4
  33.2 11.4 %shard_map.87 = (bf16[4096,128]{1,0:T(8,128)(2,1)}, bf16[4,512,128]{2,1,0:T(8,128)(2,1)S(1)}, bf16[4,512,128]{2,1,0:T(8,128)(2,1)}, bf16[4,512,128]{2,1,0:T(8,128)(2,1)S(1)}, bf16[4,512,128]{2,1,0:T(8,128)(2,1)}) custom-call(s32[9]{0:T(128)S(1)} %pad_add_fusion.column_ref, s32[2]{0:T(128)S(1)} %copy-done.4, s32[16,32]{1,0:T(8,128)S(1)} %bitcast.34, ...), custom_call_target="tpu_custom_call" | custom-call | tf_op jit(solution)/shard_map/pallas_call | solution.py:230
  44.6 0.0 copy-start
  44.6 0.8 copy-done
  45.4 0.0 copy-start.2
  45.4 0.8 copy-done.2
  46.2 0.0 copy-start.1
  46.2 3.3 %collective-permute-start.7 = (bf16[4,512,128]{2,1,0:T(8,128)(2,1)}, bf16[4,512,128]{2,1,0:T(8,128)(2,1)S(1)}, u32[]{:S(2)}, u32[]{:S(2)}) collective-permute-start(bf16[4,512,128]{2,1,0:T(8,128)(2,1)} %get-tuple-element.15), channel_id=1, source_target_pairs={{0,1},{1,0},{2,3},{3,2},{4,5},{5,4},{6,7},{7,6},{8,9},{9,8},{10,11... | collective-permute-start | bytes 1572872 | tf_op jit(solution)/shard_map/ppermute | solution.py:198
  49.5 0.0 collective-permute-start.6
  49.5 5.1 %all-to-all-start.1 = ((bf16[16,256,128]{2,1,0:T(8,128)(2,1)}), bf16[16,256,128]{2,1,0:T(8,128)(2,1)S(1)}, u32[]{:S(2)}, u32[]{:S(2)}) async-start(bf16[16,256,128]{2,1,0:T(8,128)(2,1)} %bitcast.10), calls=%async_computation.1 | async-start | bytes 2097152 | tf_op jit(solution)/shard_map/all_to_all | solution.py:194
  54.5 0.0 copy-start.3
  54.5 0.0 collective-permute-done.7
  54.5 0.0 copy-done.1
  54.6 0.1 add_convert_fusion.1
  54.7 0.3 collective-permute-start.8
  55.0 1.8 %collective-permute-start.10 = (bf16[2,512,128]{2,1,0:T(8,128)(2,1)S(1)}, bf16[2,512,128]{2,1,0:T(8,128)(2,1)S(1)}, u32[]{:S(2)}, u32[]{:S(2)}) collective-permute-start(bf16[2,512,128]{2,1,0:T(8,128)(2,1)S(1)} %get-tuple-element.20), channel_id=1, source_target_pairs={{0,56},{8,0},{16,8},{24,16},{32,24},{40,32},{48,40},{56,48},{1,57}... | collective-permute-start | bytes 786440 | tf_op jit(solution)/shard_map/ppermute | solution.py:202
  56.7 0.0 collective-permute-done.6
  56.7 5.8 %collective-permute-done.8 = bf16[2,512,128]{2,1,0:T(8,128)(2,1)S(1)} collective-permute-done((bf16[2,512,128]{2,1,0:T(8,128)(2,1)S(1)}, bf16[2,512,128]{2,1,0:T(8,128)(2,1)S(1)}, u32[]{:S(2)}, u32[]{:S(2)}) %collective-permute-start.8) | collective-permute-done | bytes 262176 | tf_op jit(solution)/shard_map/ppermute | solution.py:202
  62.5 0.0 collective-permute-done.10
  62.6 0.0 copy-done.3
  62.6 0.2 fusion.3
  62.7 1.4 %collective-permute-start.9 = (bf16[512,128]{1,0:T(8,128)(2,1)S(1)}, bf16[512,128]{1,0:T(8,128)(2,1)S(1)}, u32[]{:S(2)}, u32[]{:S(2)}) collective-permute-start(bf16[512,128]{1,0:T(8,128)(2,1)S(1)} %get-tuple-element.16), channel_id=1, source_target_pairs={{0,8},{8,16},{16,24},{24,32},{32,40},{40,48},{48,56},{56,0},{1,9},... | collective-permute-start | bytes 393224 | tf_op jit(solution)/shard_map/ppermute | solution.py:202
  64.1 3.2 %collective-permute-start.12 = (bf16[512,128]{1,0:T(8,128)(2,1)S(1)}, bf16[512,128]{1,0:T(8,128)(2,1)S(1)}, u32[]{:S(2)}, u32[]{:S(2)}) collective-permute-start(bf16[512,128]{1,0:T(8,128)(2,1)S(1)} %get-tuple-element.17), channel_id=1, source_target_pairs={{0,32},{8,40},{16,48},{24,56},{32,0},{40,8},{48,16},{56,24},{1,33}... | collective-permute-start | bytes 393224 | tf_op jit(solution)/shard_map/ppermute | solution.py:202
  67.2 0.6 collective-permute-start.11
  67.9 0.0 collective-permute-done.9
  67.9 4.2 %collective-permute-done.12 = bf16[512,128]{1,0:T(8,128)(2,1)S(1)} collective-permute-done((bf16[512,128]{1,0:T(8,128)(2,1)S(1)}, bf16[512,128]{1,0:T(8,128)(2,1)S(1)}, u32[]{:S(2)}, u32[]{:S(2)}) %collective-permute-start.12) | collective-permute-done | bytes 131104 | tf_op jit(solution)/shard_map/ppermute | solution.py:202
  72.1 6.9 %collective-permute-done.11 = bf16[512,128]{1,0:T(8,128)(2,1)S(1)} collective-permute-done((bf16[512,128]{1,0:T(8,128)(2,1)S(1)}, bf16[512,128]{1,0:T(8,128)(2,1)S(1)}, u32[]{:S(2)}, u32[]{:S(2)}) %collective-permute-start.11) | collective-permute-done | bytes 131104 | tf_op jit(solution)/shard_map/ppermute | solution.py:202
  79.0 0.7 fusion.6
  79.7 0.0 all-to-all-done.1
  79.7 0.8 reduce_sum.12
  (9 shorter events, 0.2 us)
Async XLA Ops:
  3.0 14.4 %collective-permute-start.2 = (bf16[512,128]{1,0:T(8,128)(2,1)}, bf16[512,128]{1,0:T(8,128)(2,1)S(1)}, u32[]{:S(2)}, u32[]{:S(2)}) collective-permute-start(bf16[512,128]{1,0:T(8,128)(2,1)} %get-tuple-element.10), channel_id=1, source_target_pairs={{0,32},{8,40},{16,48},{24,56},{32,0},{40,8},{48,16},{56,24},{1,33}... | collective-permute-start | bytes 393224 | tf_op jit(solution)/shard_map/ppermute | solution.py:202
  9.0 9.8 %collective-permute-start.1 = (bf16[512,128]{1,0:T(8,128)(2,1)}, bf16[512,128]{1,0:T(8,128)(2,1)S(1)}, u32[]{:S(2)}, u32[]{:S(2)}) collective-permute-start(bf16[512,128]{1,0:T(8,128)(2,1)} %get-tuple-element.10), channel_id=1, source_target_pairs={{0,56},{8,0},{16,8},{24,16},{32,24},{40,32},{48,40},{56,48},{1,57}... | collective-permute-start | bytes 393224 | tf_op jit(solution)/shard_map/ppermute | solution.py:202
  9.7 9.1 %collective-permute-start = (bf16[512,128]{1,0:T(8,128)(2,1)}, bf16[512,128]{1,0:T(8,128)(2,1)S(1)}, u32[]{:S(2)}, u32[]{:S(2)}) collective-permute-start(bf16[512,128]{1,0:T(8,128)(2,1)} %get-tuple-element.10), channel_id=1, source_target_pairs={{0,8},{8,16},{16,24},{24,32},{32,40},{40,48},{48,56},{56,0},{1,9},... | collective-permute-start | bytes 393224 | tf_op jit(solution)/shard_map/ppermute | solution.py:202
  10.5 6.9 %copy-start.5 = (bf16[512,128]{1,0:T(8,128)(2,1)S(1)}, bf16[512,128]{1,0:T(8,128)(2,1)}, u32[]{:S(2)}) copy-start(bf16[512,128]{1,0:T(8,128)(2,1)} %get-tuple-element.10) | copy-start | bytes 393220
  10.5 22.7 %all-to-all-start = ((bf16[16,272,128]{2,1,0:T(8,128)(2,1)}), bf16[16,272,128]{2,1,0:T(8,128)(2,1)S(1)}, u32[]{:S(2)}, u32[]{:S(2)}) async-start(bf16[16,272,128]{2,1,0:T(8,128)(2,1)} %get-tuple-element.9), calls=%async_computation | async-start | bytes 2228224 | tf_op jit(solution)/shard_map/all_to_all | solution.py:194
  18.8 10.5 %copy-start.6 = (s32[8]{0:T(128)S(1)}, s32[8]{0:T(128)}, u32[]{:S(2)}) copy-start(s32[8]{0:T(128)} %constant.38.clone) | copy-start | bytes 100
  18.8 14.3 %copy-start.4 = (s32[2]{0:T(128)S(1)}, s32[2]{0:T(128)}, u32[]{:S(2)}) copy-start(s32[2]{0:T(128)} %hot_ref.1) | copy-start | bytes 28
  18.9 8.5 %collective-permute-start.4 = (bf16[2,512,128]{2,1,0:T(8,128)(2,1)S(1)}, bf16[2,512,128]{2,1,0:T(8,128)(2,1)S(1)}, u32[]{:S(2)}, u32[]{:S(2)}) collective-permute-start(bf16[2,512,128]{2,1,0:T(8,128)(2,1)S(1)} %get-tuple-element.21), channel_id=1, source_target_pairs={{0,56},{8,0},{16,8},{24,16},{32,24},{40,32},{48,40},{56,48},{1,57}... | collective-permute-start | bytes 786440 | tf_op jit(solution)/shard_map/ppermute | solution.py:202
  19.5 7.9 %collective-permute-start.3 = (bf16[2,512,128]{2,1,0:T(8,128)(2,1)S(1)}, bf16[2,512,128]{2,1,0:T(8,128)(2,1)S(1)}, u32[]{:S(2)}, u32[]{:S(2)}) collective-permute-start(bf16[2,512,128]{2,1,0:T(8,128)(2,1)S(1)} %get-tuple-element.22), channel_id=1, source_target_pairs={{0,8},{8,16},{16,24},{24,32},{32,40},{40,48},{48,56},{56,0},{1,9},... | collective-permute-start | bytes 786440 | tf_op jit(solution)/shard_map/ppermute | solution.py:202
  27.4 5.7 %collective-permute-start.5 = (bf16[8,512,128]{2,1,0:T(8,128)(2,1)S(1)}, bf16[8,512,128]{2,1,0:T(8,128)(2,1)S(1)}, u32[]{:S(2)}, u32[]{:S(2)}) collective-permute-start(bf16[8,512,128]{2,1,0:T(8,128)(2,1)S(1)} %constant_dynamic-update-slice_fusion.mine_ref), channel_id=1, source_target_pairs={{0,1},{1,0},{2,3},{3,2},{4,5},{5,4},{6,7},{7,6},{8,9},{9,8},{10,11... | collective-permute-start | bytes 3145736 | tf_op jit(solution)/shard_map/ppermute | solution.py:198
  44.6 0.8 copy-start
  45.4 0.8 %copy-start.2 = (bf16[4,512,128]{2,1,0:T(8,128)(2,1)}, bf16[4,512,128]{2,1,0:T(8,128)(2,1)S(1)}, u32[]{:S(2)}) copy-start(bf16[4,512,128]{2,1,0:T(8,128)(2,1)S(1)} %get-tuple-element.12) | copy-start | bytes 1572868
  46.2 8.4 %copy-start.1 = (bf16[4,512,128]{2,1,0:T(8,128)(2,1)S(1)}, bf16[4,512,128]{2,1,0:T(8,128)(2,1)}, u32[]{:S(2)}) copy-start(bf16[4,512,128]{2,1,0:T(8,128)(2,1)} %copy-done) | copy-start | bytes 1572868
  46.2 8.4 %collective-permute-start.7 = (bf16[4,512,128]{2,1,0:T(8,128)(2,1)}, bf16[4,512,128]{2,1,0:T(8,128)(2,1)S(1)}, u32[]{:S(2)}, u32[]{:S(2)}) collective-permute-start(bf16[4,512,128]{2,1,0:T(8,128)(2,1)} %get-tuple-element.15), channel_id=1, source_target_pairs={{0,1},{1,0},{2,3},{3,2},{4,5},{5,4},{6,7},{7,6},{8,9},{9,8},{10,11... | collective-permute-start | bytes 1572872 | tf_op jit(solution)/shard_map/ppermute | solution.py:198
  49.5 7.3 %collective-permute-start.6 = (bf16[4,512,128]{2,1,0:T(8,128)(2,1)}, bf16[4,512,128]{2,1,0:T(8,128)(2,1)S(1)}, u32[]{:S(2)}, u32[]{:S(2)}) collective-permute-start(bf16[4,512,128]{2,1,0:T(8,128)(2,1)} %get-tuple-element.13), channel_id=1, source_target_pairs={{0,1},{1,0},{2,3},{3,2},{4,5},{5,4},{6,7},{7,6},{8,9},{9,8},{10,11... | collective-permute-start | bytes 1572872 | tf_op jit(solution)/shard_map/ppermute | solution.py:198
  49.5 30.3 %all-to-all-start.1 = ((bf16[16,256,128]{2,1,0:T(8,128)(2,1)}), bf16[16,256,128]{2,1,0:T(8,128)(2,1)S(1)}, u32[]{:S(2)}, u32[]{:S(2)}) async-start(bf16[16,256,128]{2,1,0:T(8,128)(2,1)} %bitcast.10), calls=%async_computation.1 | async-start | bytes 2097152 | tf_op jit(solution)/shard_map/all_to_all | solution.py:194
  54.5 8.0 %copy-start.3 = (bf16[4,512,128]{2,1,0:T(8,128)(2,1)S(1)}, bf16[4,512,128]{2,1,0:T(8,128)(2,1)}, u32[]{:S(2)}) copy-start(bf16[4,512,128]{2,1,0:T(8,128)(2,1)} %copy-done.2) | copy-start | bytes 1572868
  54.7 7.8 %collective-permute-start.8 = (bf16[2,512,128]{2,1,0:T(8,128)(2,1)S(1)}, bf16[2,512,128]{2,1,0:T(8,128)(2,1)S(1)}, u32[]{:S(2)}, u32[]{:S(2)}) collective-permute-start(bf16[2,512,128]{2,1,0:T(8,128)(2,1)S(1)} %get-tuple-element.19), channel_id=1, source_target_pairs={{0,8},{8,16},{16,24},{24,32},{32,40},{40,48},{48,56},{56,0},{1,9},... | collective-permute-start | bytes 786440 | tf_op jit(solution)/shard_map/ppermute | solution.py:202
  55.0 7.6 %collective-permute-start.10 = (bf16[2,512,128]{2,1,0:T(8,128)(2,1)S(1)}, bf16[2,512,128]{2,1,0:T(8,128)(2,1)S(1)}, u32[]{:S(2)}, u32[]{:S(2)}) collective-permute-start(bf16[2,512,128]{2,1,0:T(8,128)(2,1)S(1)} %get-tuple-element.20), channel_id=1, source_target_pairs={{0,56},{8,0},{16,8},{24,16},{32,24},{40,32},{48,40},{56,48},{1,57}... | collective-permute-start | bytes 786440 | tf_op jit(solution)/shard_map/ppermute | solution.py:202
  62.7 5.2 %collective-permute-start.9 = (bf16[512,128]{1,0:T(8,128)(2,1)S(1)}, bf16[512,128]{1,0:T(8,128)(2,1)S(1)}, u32[]{:S(2)}, u32[]{:S(2)}) collective-permute-start(bf16[512,128]{1,0:T(8,128)(2,1)S(1)} %get-tuple-element.16), channel_id=1, source_target_pairs={{0,8},{8,16},{16,24},{24,32},{32,40},{40,48},{48,56},{56,0},{1,9},... | collective-permute-start | bytes 393224 | tf_op jit(solution)/shard_map/ppermute | solution.py:202
  64.1 8.0 %collective-permute-start.12 = (bf16[512,128]{1,0:T(8,128)(2,1)S(1)}, bf16[512,128]{1,0:T(8,128)(2,1)S(1)}, u32[]{:S(2)}, u32[]{:S(2)}) collective-permute-start(bf16[512,128]{1,0:T(8,128)(2,1)S(1)} %get-tuple-element.17), channel_id=1, source_target_pairs={{0,32},{8,40},{16,48},{24,56},{32,0},{40,8},{48,16},{56,24},{1,33}... | collective-permute-start | bytes 393224 | tf_op jit(solution)/shard_map/ppermute | solution.py:202
  67.2 11.7 %collective-permute-start.11 = (bf16[512,128]{1,0:T(8,128)(2,1)S(1)}, bf16[512,128]{1,0:T(8,128)(2,1)S(1)}, u32[]{:S(2)}, u32[]{:S(2)}) collective-permute-start(bf16[512,128]{1,0:T(8,128)(2,1)S(1)} %get-tuple-element.18), channel_id=1, source_target_pairs={{0,56},{8,0},{16,8},{24,16},{32,24},{40,32},{48,40},{56,48},{1,57}... | collective-permute-start | bytes 393224 | tf_op jit(solution)/shard_map/ppermute | solution.py:202

commit v5 on v3

--- a/solution.py
+++ b/solution.py
@@ -26,14 +26,16 @@
 ENTRIES = NZ * CAP
 GROUP = 8
 BLOCK = 128
-ITEMS = 3
+LOG2 = 4.0 * math.log2(math.e)
+ITEMS = 2
 SLOTS = PLANE * CAP
 LIST = SLOTS + GROUP
 PART = NZ // 2
 STEPS = (0, -1, 1, 4, -2, 3, 2, -3)
 
 
-def pack_kernel(page_ref, query_ref, label_ref, rows_ref, out_ref):
+def pack_kernel(page_ref, query_ref, label_ref, core_ref, rows_ref, whole_ref, out_ref, half_ref):
+    half_ref[...] = whole_ref[pl.ds(pl.multiple_of(core_ref[0] * HALF, HALF), HALF), :]
     dest = lax.broadcasted_iota(jnp.int32, (PLANE, W), 0)
     lane = lax.broadcasted_iota(jnp.int32, (PLANE, W), 1)
     entry = lane % ENTRIES
@@ -120,36 +122,43 @@
                 ]
         dims = (((1,), (1,)), ((), ()))
         peaks, lses, inverses = [], [], []
-        for u in range(ITEMS):
-            tok = token_refs[u][...]
-            peak = None
-            for c in range(PATCHES // BLOCK):
-                part = (mine_ref, other_ref)[c * BLOCK // HALF]
-                first = c * BLOCK % HALF
-                block = lax.dot_general(
-                    part[page[u], first : first + BLOCK, :], tok, dims,
-                    preferred_element_type=jnp.float32,
-                )
-                logit_refs[u][c * BLOCK : (c + 1) * BLOCK, :] = block
-                top = jnp.max(block.reshape(BLOCK // 8, 8, rows), axis=0)
-                peak = top if peak is None else jnp.maximum(peak, top)
-            peaks.append(jnp.max(peak, axis=0, keepdims=True))
-        for u in range(ITEMS):
-            total = None
-            for c in range(PATCHES // BLOCK):
-                piece = logit_refs[u][c * BLOCK : (c + 1) * BLOCK, :]
-                e = jnp.exp(SHARPNESS * (piece - peaks[u]))
-                expo_refs[u][c * BLOCK : (c + 1) * BLOCK, :] = e.astype(jnp.bfloat16)
-                low = jnp.sum(e.reshape(BLOCK // 8, 8, rows), axis=0)
-                total = low if total is None else total + low
-            total = jnp.sum(total, axis=0, keepdims=True)
+        blocks = PATCHES // BLOCK
+        tops, totals = [None] * ITEMS, [None] * ITEMS
+
+        def multiply(u, c):
+            part = (mine_ref, other_ref)[c * BLOCK // HALF]
+            first = c * BLOCK % HALF
+            block = lax.dot_general(
+                part[page[u], first : first + BLOCK, :], token_refs[u][...], dims,
+                preferred_element_type=jnp.float32,
+            )
+            logit_refs[u][c * BLOCK : (c + 1) * BLOCK, :] = block
+            top = jnp.max(block.reshape(BLOCK // 8, 8, rows), axis=0)
+            tops[u] = top if c == 0 else jnp.maximum(tops[u], top)
+
+        def raise_e(u, c):
+            piece = logit_refs[u][c * BLOCK : (c + 1) * BLOCK, :]
+            e = jnp.exp2(LOG2 * (piece - peaks[u]))
+            expo_refs[u][c * BLOCK : (c + 1) * BLOCK, :] = e.astype(jnp.bfloat16)
+            low = jnp.sum(e.reshape(BLOCK // 8, 8, rows), axis=0)
+            totals[u] = low if c == 0 else totals[u] + low
+
+        grads = []
+        for c in range(blocks):
+            multiply(0, c)
+        for u in range(ITEMS):
+            peaks.append(jnp.max(tops[u], axis=0, keepdims=True))
+            for c in range(blocks):
+                if u + 1 < ITEMS:
+                    multiply(u + 1, c)
+                raise_e(u, c)
+            total = jnp.sum(totals[u], axis=0, keepdims=True)
             lse = SHARPNESS * peaks[u] + jnp.log(total)
             lses.append(jnp.broadcast_to(lse, (W, rows)).T)
             inverses.append(jnp.broadcast_to(1.0 / total, (W, rows)).T)
-        grads = [
-            jnp.dot(turned[page[u]], expo_refs[u][...], preferred_element_type=jnp.float32).T
-            for u in range(ITEMS)
-        ]
+            grads.append(
+                jnp.dot(turned[page[u]], expo_refs[u][...], preferred_element_type=jnp.float32).T
+            )
         scale = []
         for u in range(ITEMS):
             page_id = first_page + column_ref[page[u]] * NY
@@ -204,12 +213,15 @@
     return jnp.stack([half, below, above, across]), jnp.concatenate([far_below, far_above])
 
 
-def reduce_column(near, from_below, from_above):
-    up = (near[2] + from_below[0].astype(jnp.float32)).astype(jnp.bfloat16)
-    down = (near[1] + from_above[0].astype(jnp.float32)).astype(jnp.bfloat16)
-    over = near[3] + from_below[1].astype(jnp.float32) + from_above[1].astype(jnp.float32)
-    over = over.astype(jnp.bfloat16)
-    total = near[0]
+def add(mine, other):
+    return mine.astype(jnp.float32) + other.astype(jnp.float32)
+
+
+def reduce_column(mine, other, from_below, from_above):
+    up = (add(mine[2], other[2]) + from_below[0].astype(jnp.float32)).astype(jnp.bfloat16)
+    down = (add(mine[1], other[1]) + from_above[0].astype(jnp.float32)).astype(jnp.bfloat16)
+    over = (add(mine[3], other[3]) + add(from_below[1], from_above[1])).astype(jnp.bfloat16)
+    total = add(mine[0], other[0])
     for part in (move(up, 1), move(down, -1), move(over, 4)):
         total = total + part.astype(jnp.float32)
     return total.astype(jnp.bfloat16)
@@ -251,7 +263,7 @@
         in_specs=[smem] * 3 + [vmem] * (3 + last),
         out_specs=(vmem, vmem, vmem),
         scratch_shapes=scratch,
-        compiler_params=pltpu.CompilerParams(vmem_limit_bytes=40 << 20),
+        compiler_params=pltpu.CompilerParams(vmem_limit_bytes=18 << 20),
         cost_estimate=pl.CostEstimate(
             flops=6 * PLANE * CAP * 2 * QT * PATCHES * W * 2,
             bytes_accessed=8 << 20,
@@ -263,14 +275,16 @@
 def shards(queries, pages, pair_page, pair_query, pair_label, hot_pages):
     smem = pl.BlockSpec(memory_space=pltpu.SMEM)
     vmem = pl.BlockSpec(memory_space=pltpu.VMEM)
-    core = lax.axis_index("core")
-    half = lax.dynamic_slice(pages[0], (core * HALF, 0), (HALF, W))
-    send = pl.pallas_call(
+    core = lax.axis_index("core").reshape(1)
+    send, half = pl.pallas_call(
         pack_kernel,
-        out_shape=jax.ShapeDtypeStruct((PLANE, SEND_ROWS, W), jnp.bfloat16),
-        in_specs=[smem, smem, smem, vmem],
-        out_specs=vmem,
-    )(pair_page[:, 0], pair_query, pair_label, queries.reshape(ROWS, W))
+        out_shape=(
+            jax.ShapeDtypeStruct((PLANE, SEND_ROWS, W), jnp.bfloat16),
+            jax.ShapeDtypeStruct((HALF, W), jnp.bfloat16),
+        ),
+        in_specs=[smem] * 4 + [vmem] * 2,
+        out_specs=(vmem, vmem),
+    )(pair_page[:, 0], pair_query, pair_label, core, queries.reshape(ROWS, W), pages[0])
     near, far = gather_column(half)
     other_near, other_far = swap_cores(near), swap_cores(far)
     got = exchange(send, ("x", "y"))
@@ -279,16 +293,21 @@
     first_page = (lax.axis_index("x") * (NZ * NY) + lax.axis_index("y")).reshape(1)
     near_column = jnp.concatenate([heights[:PART], first_page])
     far_column = jnp.concatenate([heights[PART:], first_page])
-    sums, mine_terms, other_terms = score(far_column, hot_pages, table, got, far, other_far)
-    far_terms = mine_terms.astype(jnp.float32) + swap_cores(other_terms).astype(jnp.float32)
-    far_terms = far_terms.astype(jnp.bfloat16)
-    query_part, mine_terms, other_terms = score(
+    sums, far_mine, far_other = score(far_column, hot_pages, table, got, far, other_far)
+    far_other = swap_cores(far_other)
+    to_above = add(far_mine[2:4], far_other[2:4]).astype(jnp.bfloat16)
+    to_below = add(far_mine[0:2], far_other[0:2]).astype(jnp.bfloat16)
+    sums, to_above, to_below = lax.optimization_barrier((sums, to_above, to_below))
+    from_below, from_above = move(to_above, 1), move(to_below, -1)
+    query_part, near_mine, near_other = score(
         near_column, hot_pages, table, got, near, other_near, sums
     )
-    near_terms = mine_terms.astype(jnp.float32) + swap_cores(other_terms).astype(jnp.float32)
-    from_below, from_above = move(far_terms[2:4], 1), move(far_terms[0:2], -1)
+    near_other = swap_cores(near_other)
+    query_part, from_below, from_above = lax.optimization_barrier(
+        (query_part, from_below, from_above)
+    )
     query_back = exchange(query_part.reshape(PLANE, ROWS, W), ("x", "y"))
-    page_grad = reduce_column(near_terms, from_below, from_above)
+    page_grad = reduce_column(near_mine, near_other, from_below, from_above)
     query_grad = jnp.sum(query_back.astype(jnp.float32), axis=0).astype(jnp.bfloat16)
     return query_grad.reshape(Q_DEV, QT, W), page_grad[None]
 

time: 88.9 us -> 81.2 us (0.913)
  local copies, waits for them, and re-layouts: 4.83 us -> 0.14 us
  Pallas kernels: 15.6 us -> 14.1 us
  starting transfers between devices: 38.3 us -> 39.4 us
  other arithmetic: 3.17 us -> 2.12 us
  waiting for transfers between devices: 25 us -> 24 us
    ppermute x10, waiting for transfers between devices: 19.8 us -> 13.7 us  [move(): return lax.ppermute(array, 'z', [(i, (i + step) % NZ) for i in range(NZ)])]
    unnamed x15 -> x7, local copies, waits for them, and re-layouts: 4.67 us -> 0.03 us
    all_to_all x2, waiting for transfers between devices: 5.24 us -> 9.06 us  [exchange(): return lax.all_to_all(array, axes, split_axis=0, concat_axis=0, tiled=True)]
    ppermute x10, starting transfers between devices: 17.8 us -> 19.6 us  [move(): return lax.ppermute(array, 'z', [(i, (i + step) % NZ) for i in range(NZ)])]
    pallas_call x2, Pallas kernels: 13.4 us -> 11.7 us  [score(): pl.pallas_call(functools.partial(second_kernel if last else first_kernel,...]
    ppermute x4, waiting for transfers between devices: 0.01 us -> 1.28 us  [swap_cores(): return lax.ppermute(array, 'core', [(0, 1), (1, 0)])]
    convert_element_type x2, other arithmetic: 1.29 us -> 0.32 us  [the longest x1 0.18 us: reduce_column(): (add(mine[2], other[2]) + from_below[0].astype(jnp.float32)).astype(jnp.b...]
  transfers between devices with their start and end apart: 16 -> 16, of which waited for: 7 -> 7; matrix products, arithmetic and copies ran while one was open for 3% -> 2% of each run, Pallas kernels for 18% -> 9%
where the time goes in v5:
time: 81.2 us; the launch traced here: 80.6 us
  starting transfers between devices  39.4 us (49%)
  waiting for transfers between devices  24 us (30%)
  Pallas kernels  14.1 us (17%)
  other arithmetic  2.12 us (3%)
    ppermute x10, starting transfers between devices, move(): return lax.ppermute(array, 'z', [(i, (i + step) % NZ) for i in range(NZ)])  19.6 us
    ppermute x10, waiting for transfers between devices, move(): return lax.ppermute(array, 'z', [(i, (i + step) % NZ) for i in range(NZ)])  13.7 us
    pallas_call x2, Pallas kernels, score(): pl.pallas_call(functools.partial(second_kernel if last else first_kernel,...  11.7 us
    all_to_all x2, starting transfers between devices, exchange(): return lax.all_to_all(array, axes, split_axis=0, concat_axis=0, tiled=True)  10.7 us
    ppermute x4, starting transfers between devices, swap_cores(): return lax.ppermute(array, 'core', [(0, 1), (1, 0)])  9.16 us
    all_to_all x2, waiting for transfers between devices, exchange(): return lax.all_to_all(array, axes, split_axis=0, concat_axis=0, tiled=True)  9.06 us
    pallas_call x1, Pallas kernels, shards(): pl.pallas_call(pack_kernel, out_shape=(jax.ShapeDtypeStruct((PLANE, SEND_...  2.35 us
  transfers between devices with their start and end apart: 16, of which 7 were waited for; matrix products, arithmetic and copies ran while one was open for 2% of the time, Pallas kernels for 9%

profile of v5, /device:TPU:1, one launch (start us, length us, event | category | flops | bytes accessed | tf_op | source)
XLA Modules:
  0.0 80.6 jit_solution(741932514382229988)
XLA Ops:
  0.6 2.4 %shard_map.86 = (bf16[16,272,128]{2,1,0:T(8,128)(2,1)}, bf16[512,128]{1,0:T(8,128)(2,1)}) custom-call(s32[64]{0:T(128)} %bitcast.42, s32[64]{0:T(128)} %query_ref.1, s32[64]{0:T(128)} %label_ref.1, s32[1]{0:T(128)} %bitcast.2.core_ref, bf16[256,128]{1,0:T(8,128)(2,1)} %bitcast.40, bf16[1024,128]{1,0:T(8,128)(2,1)} %bitcast.38), custom_call_target="tpu_custom_call" | custom-call | tf_op jit(solution)/shard_map/pallas_call | solution.py:279
  3.0 7.7 %collective-permute-start.2 = (bf16[512,128]{1,0:T(8,128)(2,1)}, bf16[512,128]{1,0:T(8,128)(2,1)S(1)}, u32[]{:S(2)}, u32[]{:S(2)}) collective-permute-start(bf16[512,128]{1,0:T(8,128)(2,1)} %get-tuple-element.17), channel_id=1, source_target_pairs={{0,32},{8,40},{16,48},{24,56},{32,0},{40,8},{48,16},{56,24},{1,33}... | collective-permute-start | bytes 393224 | tf_op jit(solution)/shard_map/ppermute | solution.py:206
  10.7 0.0 collective-permute-start.1
  10.7 1.5 %collective-permute-start = (bf16[512,128]{1,0:T(8,128)(2,1)}, bf16[512,128]{1,0:T(8,128)(2,1)S(1)}, u32[]{:S(2)}, u32[]{:S(2)}) collective-permute-start(bf16[512,128]{1,0:T(8,128)(2,1)} %get-tuple-element.17), channel_id=1, source_target_pairs={{0,8},{8,16},{16,24},{24,32},{32,40},{40,48},{48,56},{56,0},{1,9},... | collective-permute-start | bytes 393224 | tf_op jit(solution)/shard_map/ppermute | solution.py:206
  12.2 0.0 copy-start.2
  12.2 6.9 %all-to-all-start = ((bf16[16,272,128]{2,1,0:T(8,128)(2,1)}), bf16[16,272,128]{2,1,0:T(8,128)(2,1)S(1)}, u32[]{:S(2)}, u32[]{:S(2)}) async-start(bf16[16,272,128]{2,1,0:T(8,128)(2,1)} %get-tuple-element.16), calls=%async_computation | async-start | bytes 2228224 | tf_op jit(solution)/shard_map/all_to_all | solution.py:198
  19.1 0.0 copy-start
  19.1 0.0 collective-permute-done.2
  19.1 1.2 %collective-permute-done.1 = bf16[512,128]{1,0:T(8,128)(2,1)S(1)} collective-permute-done((bf16[512,128]{1,0:T(8,128)(2,1)}, bf16[512,128]{1,0:T(8,128)(2,1)S(1)}, u32[]{:S(2)}, u32[]{:S(2)}) %collective-permute-start.1) | collective-permute-done | bytes 131104 | tf_op jit(solution)/shard_map/ppermute | solution.py:206
  20.3 0.0 collective-permute-done
  20.4 1.0 %collective-permute-start.4 = (bf16[2,512,128]{2,1,0:T(8,128)(2,1)S(1)}, bf16[2,512,128]{2,1,0:T(8,128)(2,1)S(1)}, u32[]{:S(2)}, u32[]{:S(2)}) collective-permute-start(bf16[2,512,128]{2,1,0:T(8,128)(2,1)S(1)} %get-tuple-element.36), channel_id=1, source_target_pairs={{0,8},{8,16},{16,24},{24,32},{32,40},{40,48},{48,56},{56,0},{1,9},... | collective-permute-start | bytes 786440 | tf_op jit(solution)/shard_map/ppermute | solution.py:206
  21.4 1.7 %collective-permute-start.5 = (bf16[2,512,128]{2,1,0:T(8,128)(2,1)S(1)}, bf16[2,512,128]{2,1,0:T(8,128)(2,1)S(1)}, u32[]{:S(2)}, u32[]{:S(2)}) collective-permute-start(bf16[2,512,128]{2,1,0:T(8,128)(2,1)S(1)} %get-tuple-element.35), channel_id=1, source_target_pairs={{0,56},{8,0},{16,8},{24,16},{32,24},{40,32},{48,40},{56,48},{1,57}... | collective-permute-start | bytes 786440 | tf_op jit(solution)/shard_map/ppermute | solution.py:206
  23.1 0.0 copy-done.2
  23.1 4.8 %collective-permute-done.4 = bf16[2,512,128]{2,1,0:T(8,128)(2,1)S(1)} collective-permute-done((bf16[2,512,128]{2,1,0:T(8,128)(2,1)S(1)}, bf16[2,512,128]{2,1,0:T(8,128)(2,1)S(1)}, u32[]{:S(2)}, u32[]{:S(2)}) %collective-permute-start.4) | collective-permute-done | bytes 262176 | tf_op jit(solution)/shard_map/ppermute | solution.py:206
  28.0 0.5 collective-permute-done.5
  28.5 2.1 %collective-permute-start.6 = (bf16[4,512,128]{2,1,0:T(8,128)(2,1)S(1)}, bf16[4,512,128]{2,1,0:T(8,128)(2,1)S(1)}, u32[]{:S(2)}, u32[]{:S(2)}) collective-permute-start(bf16[4,512,128]{2,1,0:T(8,128)(2,1)S(1)} %constant_dynamic-update-slice_fusion.refs_4_), channel_id=1, source_target_pairs={{0,1},{1,0},{2,3},{3,2},{4,5},{5,4},{6,7},{7,6},{8,9},{9,8},{10,11... | collective-permute-start | bytes 1572872 | tf_op jit(solution)/shard_map/ppermute | solution.py:202
  30.5 0.1 fusion.8
  30.6 0.1 pad_add_fusion.1.refs_0_
  30.7 4.2 %all-to-all-done.refs_3_ = bf16[16,272,128]{2,1,0:T(8,128)(2,1)S(1)} async-done(((bf16[16,272,128]{2,1,0:T(8,128)(2,1)}), bf16[16,272,128]{2,1,0:T(8,128)(2,1)S(1)}, u32[]{:S(2)}, u32[]{:S(2)}) %all-to-all-start) | async-done | bytes 1114144 | tf_op jit(solution)/shard_map/all_to_all | solution.py:198
  34.9 0.0 collective-permute-done.6.refs_5_
  34.9 0.0 copy-done
  34.9 0.0 copy-start.1
  34.9 4.7 %shard_map.87 = (f32[4096,128]{1,0:T(8,128)S(1)}, bf16[4,512,128]{2,1,0:T(8,128)(2,1)S(1)}, bf16[4,512,128]{2,1,0:T(8,128)(2,1)S(1)}) custom-call(s32[5]{0:T(128)S(1)} %pad_add_fusion.1.refs_0_, s32[2]{0:T(128)S(1)} %copy-done, s32[16,32]{1,0:T(8,128)S(1)} %bitcast.30, bf16[16,272,128]{2,1,0:T(8,128)(2,1)S(1)} %all-to-all-done.refs_3_, ...), custom_call_target="tpu_custom_call" | custom-call | flops 3221225472 | bytes 8388608 | tf_op jit(solution)/shard_map/pallas_call | solution.py:260
  39.6 4.7 %collective-permute-start.7 = (bf16[4,512,128]{2,1,0:T(8,128)(2,1)S(1)}, bf16[4,512,128]{2,1,0:T(8,128)(2,1)S(1)}, u32[]{:S(2)}, u32[]{:S(2)}) collective-permute-start(bf16[4,512,128]{2,1,0:T(8,128)(2,1)S(1)} %get-tuple-element.20), channel_id=1, source_target_pairs={{0,1},{1,0},{2,3},{3,2},{4,5},{5,4},{6,7},{7,6},{8,9},{9,8},{10,11... | collective-permute-start | bytes 1572872 | tf_op jit(solution)/shard_map/ppermute | solution.py:202
  44.3 0.0 copy-done.1
  44.3 0.1 pad_maximum_fusion.refs_4_
  44.4 0.1 collective-permute-start.3
  44.5 0.1 pad_add_fusion.refs_0_
  44.6 1.3 %collective-permute-done.7 = bf16[4,512,128]{2,1,0:T(8,128)(2,1)S(1)} collective-permute-done((bf16[4,512,128]{2,1,0:T(8,128)(2,1)S(1)}, bf16[4,512,128]{2,1,0:T(8,128)(2,1)S(1)}, u32[]{:S(2)}, u32[]{:S(2)}) %collective-permute-start.7) | collective-permute-done | bytes 524320 | tf_op jit(solution)/shard_map/ppermute | solution.py:202
  45.8 0.1 add_convert_fusion
  46.0 0.8 %collective-permute-start.8 = (bf16[2,512,128]{2,1,0:T(8,128)(2,1)S(1)}, bf16[2,512,128]{2,1,0:T(8,128)(2,1)S(1)}, u32[]{:S(2)}, u32[]{:S(2)}) collective-permute-start(bf16[2,512,128]{2,1,0:T(8,128)(2,1)S(1)} %get-tuple-element.23), channel_id=1, source_target_pairs={{0,8},{8,16},{16,24},{24,32},{32,40},{40,48},{48,56},{56,0},{1,9},... | collective-permute-start | bytes 786440 | tf_op jit(solution)/shard_map/ppermute | solution.py:206
  46.8 1.9 %collective-permute-start.9 = (bf16[2,512,128]{2,1,0:T(8,128)(2,1)S(1)}, bf16[2,512,128]{2,1,0:T(8,128)(2,1)S(1)}, u32[]{:S(2)}, u32[]{:S(2)}) collective-permute-start(bf16[2,512,128]{2,1,0:T(8,128)(2,1)S(1)} %get-tuple-element.24), channel_id=1, source_target_pairs={{0,56},{8,0},{16,8},{24,16},{32,24},{40,32},{48,40},{56,48},{1,57}... | collective-permute-start | bytes 786440 | tf_op jit(solution)/shard_map/ppermute | solution.py:206
  48.7 0.0 collective-permute-done.3.refs_5_
  48.8 7.1 %shard_map.88 = (bf16[4096,128]{1,0:T(8,128)(2,1)}, bf16[4,512,128]{2,1,0:T(8,128)(2,1)S(1)}, bf16[4,512,128]{2,1,0:T(8,128)(2,1)S(1)}) custom-call(s32[5]{0:T(128)S(1)} %pad_add_fusion.refs_0_, s32[2]{0:T(128)S(1)} %copy-done, s32[16,32]{1,0:T(8,128)S(1)} %bitcast.31, bf16[16,272,128]{2,1,0:T(8,128)(2,1)S(1)} %all-to-all-done.refs_3_, ...), custom_call_target="tpu_custom_call" | custom-call | flops 3221225472 | bytes 8388608 | tf_op jit(solution)/shard_map/pallas_call | solution.py:260
  55.8 2.3 %collective-permute-start.10 = (bf16[4,512,128]{2,1,0:T(8,128)(2,1)S(1)}, bf16[4,512,128]{2,1,0:T(8,128)(2,1)S(1)}, u32[]{:S(2)}, u32[]{:S(2)}) collective-permute-start(bf16[4,512,128]{2,1,0:T(8,128)(2,1)S(1)} %get-tuple-element.27), channel_id=1, source_target_pairs={{0,1},{1,0},{2,3},{3,2},{4,5},{5,4},{6,7},{7,6},{8,9},{9,8},{10,11... | collective-permute-start | bytes 1572872 | tf_op jit(solution)/shard_map/ppermute | solution.py:202
  58.1 0.0 collective-permute-done.8
  58.1 0.0 collective-permute-done.9
  58.1 3.8 %all-to-all-start.1 = ((bf16[16,256,128]{2,1,0:T(8,128)(2,1)}), bf16[16,256,128]{2,1,0:T(8,128)(2,1)S(1)}, u32[]{:S(2)}, u32[]{:S(2)}) async-start(bf16[16,256,128]{2,1,0:T(8,128)(2,1)} %bitcast.10), calls=%async_computation.1 | async-start | bytes 2097152 | tf_op jit(solution)/shard_map/all_to_all | solution.py:198
  61.9 0.0 collective-permute-done.10
  62.0 0.2 fusion.3
  62.1 0.1 collective-permute-start.11
  62.2 2.2 %collective-permute-start.13 = (bf16[512,128]{1,0:T(8,128)(2,1)S(1)}, bf16[512,128]{1,0:T(8,128)(2,1)S(1)}, u32[]{:S(2)}, u32[]{:S(2)}) collective-permute-start(bf16[512,128]{1,0:T(8,128)(2,1)S(1)} %get-tuple-element.31), channel_id=1, source_target_pairs={{0,32},{8,40},{16,48},{24,56},{32,0},{40,8},{48,16},{56,24},{1,33}... | collective-permute-start | bytes 393224 | tf_op jit(solution)/shard_map/ppermute | solution.py:206
  64.4 2.6 %collective-permute-start.12 = (bf16[512,128]{1,0:T(8,128)(2,1)S(1)}, bf16[512,128]{1,0:T(8,128)(2,1)S(1)}, u32[]{:S(2)}, u32[]{:S(2)}) collective-permute-start(bf16[512,128]{1,0:T(8,128)(2,1)S(1)} %get-tuple-element.32), channel_id=1, source_target_pairs={{0,56},{8,0},{16,8},{24,16},{32,24},{40,32},{48,40},{56,48},{1,57}... | collective-permute-start | bytes 393224 | tf_op jit(solution)/shard_map/ppermute | solution.py:206
  67.0 7.2 %collective-permute-done.11 = bf16[512,128]{1,0:T(8,128)(2,1)S(1)} collective-permute-done((bf16[512,128]{1,0:T(8,128)(2,1)S(1)}, bf16[512,128]{1,0:T(8,128)(2,1)S(1)}, u32[]{:S(2)}, u32[]{:S(2)}) %collective-permute-start.11) | collective-permute-done | bytes 131104 | tf_op jit(solution)/shard_map/ppermute | solution.py:206
  74.2 0.0 collective-permute-done.13
  74.2 0.0 collective-permute-done.12
  74.2 0.7 fusion.6
  74.9 4.9 %all-to-all-done.1 = bf16[16,256,128]{2,1,0:T(8,128)(2,1)S(1)} async-done(((bf16[16,256,128]{2,1,0:T(8,128)(2,1)}), bf16[16,256,128]{2,1,0:T(8,128)(2,1)S(1)}, u32[]{:S(2)}, u32[]{:S(2)}) %all-to-all-start.1) | async-done | bytes 1048608 | tf_op jit(solution)/shard_map/all_to_all | solution.py:198
  79.8 0.8 reduce_sum.12
  (5 shorter events, 0.1 us)
Async XLA Ops:
  3.0 16.1 %collective-permute-start.2 = (bf16[512,128]{1,0:T(8,128)(2,1)}, bf16[512,128]{1,0:T(8,128)(2,1)S(1)}, u32[]{:S(2)}, u32[]{:S(2)}) collective-permute-start(bf16[512,128]{1,0:T(8,128)(2,1)} %get-tuple-element.17), channel_id=1, source_target_pairs={{0,32},{8,40},{16,48},{24,56},{32,0},{40,8},{48,16},{56,24},{1,33}... | collective-permute-start | bytes 393224 | tf_op jit(solution)/shard_map/ppermute | solution.py:206
  10.7 9.6 %collective-permute-start.1 = (bf16[512,128]{1,0:T(8,128)(2,1)}, bf16[512,128]{1,0:T(8,128)(2,1)S(1)}, u32[]{:S(2)}, u32[]{:S(2)}) collective-permute-start(bf16[512,128]{1,0:T(8,128)(2,1)} %get-tuple-element.17), channel_id=1, source_target_pairs={{0,56},{8,0},{16,8},{24,16},{32,24},{40,32},{48,40},{56,48},{1,57}... | collective-permute-start | bytes 393224 | tf_op jit(solution)/shard_map/ppermute | solution.py:206
  10.7 9.6 %collective-permute-start = (bf16[512,128]{1,0:T(8,128)(2,1)}, bf16[512,128]{1,0:T(8,128)(2,1)S(1)}, u32[]{:S(2)}, u32[]{:S(2)}) collective-permute-start(bf16[512,128]{1,0:T(8,128)(2,1)} %get-tuple-element.17), channel_id=1, source_target_pairs={{0,8},{8,16},{16,24},{24,32},{32,40},{40,48},{48,56},{56,0},{1,9},... | collective-permute-start | bytes 393224 | tf_op jit(solution)/shard_map/ppermute | solution.py:206
  12.2 10.9 %copy-start.2 = (s32[8]{0:T(128)S(1)}, s32[8]{0:T(128)}, u32[]{:S(2)}) copy-start(s32[8]{0:T(128)} %constant.38.clone) | copy-start | bytes 100
  12.2 22.7 %all-to-all-start = ((bf16[16,272,128]{2,1,0:T(8,128)(2,1)}), bf16[16,272,128]{2,1,0:T(8,128)(2,1)S(1)}, u32[]{:S(2)}, u32[]{:S(2)}) async-start(bf16[16,272,128]{2,1,0:T(8,128)(2,1)} %get-tuple-element.16), calls=%async_computation | async-start | bytes 2228224 | tf_op jit(solution)/shard_map/all_to_all | solution.py:198
  19.1 15.8 %copy-start = (s32[2]{0:T(128)S(1)}, s32[2]{0:T(128)}, u32[]{:S(2)}) copy-start(s32[2]{0:T(128)} %refs_1_.3) | copy-start | bytes 28
  20.4 7.6 %collective-permute-start.4 = (bf16[2,512,128]{2,1,0:T(8,128)(2,1)S(1)}, bf16[2,512,128]{2,1,0:T(8,128)(2,1)S(1)}, u32[]{:S(2)}, u32[]{:S(2)}) collective-permute-start(bf16[2,512,128]{2,1,0:T(8,128)(2,1)S(1)} %get-tuple-element.36), channel_id=1, source_target_pairs={{0,8},{8,16},{16,24},{24,32},{32,40},{40,48},{48,56},{56,0},{1,9},... | collective-permute-start | bytes 786440 | tf_op jit(solution)/shard_map/ppermute | solution.py:206
  21.4 7.1 %collective-permute-start.5 = (bf16[2,512,128]{2,1,0:T(8,128)(2,1)S(1)}, bf16[2,512,128]{2,1,0:T(8,128)(2,1)S(1)}, u32[]{:S(2)}, u32[]{:S(2)}) collective-permute-start(bf16[2,512,128]{2,1,0:T(8,128)(2,1)S(1)} %get-tuple-element.35), channel_id=1, source_target_pairs={{0,56},{8,0},{16,8},{24,16},{32,24},{40,32},{48,40},{56,48},{1,57}... | collective-permute-start | bytes 786440 | tf_op jit(solution)/shard_map/ppermute | solution.py:206
  28.5 6.4 %collective-permute-start.6 = (bf16[4,512,128]{2,1,0:T(8,128)(2,1)S(1)}, bf16[4,512,128]{2,1,0:T(8,128)(2,1)S(1)}, u32[]{:S(2)}, u32[]{:S(2)}) collective-permute-start(bf16[4,512,128]{2,1,0:T(8,128)(2,1)S(1)} %constant_dynamic-update-slice_fusion.refs_4_), channel_id=1, source_target_pairs={{0,1},{1,0},{2,3},{3,2},{4,5},{5,4},{6,7},{7,6},{8,9},{9,8},{10,11... | collective-permute-start | bytes 1572872 | tf_op jit(solution)/shard_map/ppermute | solution.py:202
  34.9 9.4 %copy-start.1 = (bf16[512,128]{1,0:T(8,128)(2,1)S(1)}, bf16[512,128]{1,0:T(8,128)(2,1)}, u32[]{:S(2)}) copy-start(bf16[512,128]{1,0:T(8,128)(2,1)} %get-tuple-element.17) | copy-start | bytes 393220
  39.6 6.2 %collective-permute-start.7 = (bf16[4,512,128]{2,1,0:T(8,128)(2,1)S(1)}, bf16[4,512,128]{2,1,0:T(8,128)(2,1)S(1)}, u32[]{:S(2)}, u32[]{:S(2)}) collective-permute-start(bf16[4,512,128]{2,1,0:T(8,128)(2,1)S(1)} %get-tuple-element.20), channel_id=1, source_target_pairs={{0,1},{1,0},{2,3},{3,2},{4,5},{5,4},{6,7},{7,6},{8,9},{9,8},{10,11... | collective-permute-start | bytes 1572872 | tf_op jit(solution)/shard_map/ppermute | solution.py:202
  44.4 4.4 %collective-permute-start.3 = (bf16[4,512,128]{2,1,0:T(8,128)(2,1)S(1)}, bf16[4,512,128]{2,1,0:T(8,128)(2,1)S(1)}, u32[]{:S(2)}, u32[]{:S(2)}) collective-permute-start(bf16[4,512,128]{2,1,0:T(8,128)(2,1)S(1)} %pad_maximum_fusion.refs_4_), channel_id=1, source_target_pairs={{0,1},{1,0},{2,3},{3,2},{4,5},{5,4},{6,7},{7,6},{8,9},{9,8},{10,11... | collective-permute-start | bytes 1572872 | tf_op jit(solution)/shard_map/ppermute | solution.py:202
  46.0 12.1 %collective-permute-start.8 = (bf16[2,512,128]{2,1,0:T(8,128)(2,1)S(1)}, bf16[2,512,128]{2,1,0:T(8,128)(2,1)S(1)}, u32[]{:S(2)}, u32[]{:S(2)}) collective-permute-start(bf16[2,512,128]{2,1,0:T(8,128)(2,1)S(1)} %get-tuple-element.23), channel_id=1, source_target_pairs={{0,8},{8,16},{16,24},{24,32},{32,40},{40,48},{48,56},{56,0},{1,9},... | collective-permute-start | bytes 786440 | tf_op jit(solution)/shard_map/ppermute | solution.py:206
  46.8 11.3 %collective-permute-start.9 = (bf16[2,512,128]{2,1,0:T(8,128)(2,1)S(1)}, bf16[2,512,128]{2,1,0:T(8,128)(2,1)S(1)}, u32[]{:S(2)}, u32[]{:S(2)}) collective-permute-start(bf16[2,512,128]{2,1,0:T(8,128)(2,1)S(1)} %get-tuple-element.24), channel_id=1, source_target_pairs={{0,56},{8,0},{16,8},{24,16},{32,24},{40,32},{48,40},{56,48},{1,57}... | collective-permute-start | bytes 786440 | tf_op jit(solution)/shard_map/ppermute | solution.py:206
  55.8 6.1 %collective-permute-start.10 = (bf16[4,512,128]{2,1,0:T(8,128)(2,1)S(1)}, bf16[4,512,128]{2,1,0:T(8,128)(2,1)S(1)}, u32[]{:S(2)}, u32[]{:S(2)}) collective-permute-start(bf16[4,512,128]{2,1,0:T(8,128)(2,1)S(1)} %get-tuple-element.27), channel_id=1, source_target_pairs={{0,1},{1,0},{2,3},{3,2},{4,5},{5,4},{6,7},{7,6},{8,9},{9,8},{10,11... | collective-permute-start | bytes 1572872 | tf_op jit(solution)/shard_map/ppermute | solution.py:202
  58.1 21.7 %all-to-all-start.1 = ((bf16[16,256,128]{2,1,0:T(8,128)(2,1)}), bf16[16,256,128]{2,1,0:T(8,128)(2,1)S(1)}, u32[]{:S(2)}, u32[]{:S(2)}) async-start(bf16[16,256,128]{2,1,0:T(8,128)(2,1)} %bitcast.10), calls=%async_computation.1 | async-start | bytes 2097152 | tf_op jit(solution)/shard_map/all_to_all | solution.py:198
  62.1 12.0 %collective-permute-start.11 = (bf16[512,128]{1,0:T(8,128)(2,1)S(1)}, bf16[512,128]{1,0:T(8,128)(2,1)S(1)}, u32[]{:S(2)}, u32[]{:S(2)}) collective-permute-start(bf16[512,128]{1,0:T(8,128)(2,1)S(1)} %get-tuple-element.30), channel_id=1, source_target_pairs={{0,8},{8,16},{16,24},{24,32},{32,40},{40,48},{48,56},{56,0},{1,9},... | collective-permute-start | bytes 393224 | tf_op jit(solution)/shard_map/ppermute | solution.py:206
  62.2 11.9 %collective-permute-start.13 = (bf16[512,128]{1,0:T(8,128)(2,1)S(1)}, bf16[512,128]{1,0:T(8,128)(2,1)S(1)}, u32[]{:S(2)}, u32[]{:S(2)}) collective-permute-start(bf16[512,128]{1,0:T(8,128)(2,1)S(1)} %get-tuple-element.31), channel_id=1, source_target_pairs={{0,32},{8,40},{16,48},{24,56},{32,0},{40,8},{48,16},{56,24},{1,33}... | collective-permute-start | bytes 393224 | tf_op jit(solution)/shard_map/ppermute | solution.py:206
  64.4 9.7 %collective-permute-start.12 = (bf16[512,128]{1,0:T(8,128)(2,1)S(1)}, bf16[512,128]{1,0:T(8,128)(2,1)S(1)}, u32[]{:S(2)}, u32[]{:S(2)}) collective-permute-start(bf16[512,128]{1,0:T(8,128)(2,1)S(1)} %get-tuple-element.32), channel_id=1, source_target_pairs={{0,56},{8,0},{16,8},{24,16},{32,24},{40,32},{48,40},{56,48},{1,57}... | collective-permute-start | bytes 393224 | tf_op jit(solution)/shard_map/ppermute | solution.py:206

commit v6 on v5

--- a/solution.py
+++ b/solution.py
@@ -27,15 +27,23 @@
 GROUP = 8
 BLOCK = 128
 LOG2 = 4.0 * math.log2(math.e)
-ITEMS = 2
 SLOTS = PLANE * CAP
 LIST = SLOTS + GROUP
 PART = NZ // 2
 STEPS = (0, -1, 1, 4, -2, 3, 2, -3)
 
 
-def pack_kernel(page_ref, query_ref, label_ref, core_ref, rows_ref, whole_ref, out_ref, half_ref):
-    half_ref[...] = whole_ref[pl.ds(pl.multiple_of(core_ref[0] * HALF, HALF), HALF), :]
+def pack_kernel(
+    page_ref, query_ref, label_ref, core_ref, rows_ref, whole_ref, out_ref, half_ref, table_ref, done
+):
+    at = pl.ds(pl.multiple_of(core_ref[0] * HALF, HALF), HALF)
+    copies = [pltpu.make_async_copy(whole_ref.at[at, :], half_ref, done.at[PLANE])]
+    for d in range(PLANE):
+        copies.append(
+            pltpu.make_async_copy(rows_ref, out_ref.at[d, pl.ds(0, ROWS), :], done.at[d])
+        )
+    for copy in copies:
+        copy.start()
     dest = lax.broadcasted_iota(jnp.int32, (PLANE, W), 0)
     lane = lax.broadcasted_iota(jnp.int32, (PLANE, W), 1)
     entry = lane % ENTRIES
@@ -54,21 +62,27 @@
     zeros = jnp.zeros((PLANE, W), jnp.int32)
     table, _ = lax.fori_loop(0, PAIR_DEV, visit, (zeros, zeros), unroll=8)
     table = table.astype(jnp.float32)
-    rows = rows_ref[...]
     for d in range(PLANE):
-        out_ref[d, :ROWS, :] = rows
-        out_ref[d, ROWS:, :] = jnp.broadcast_to(table[d : d + 1, :], (16, W)).astype(jnp.bfloat16)
+        table_ref[d] = jnp.broadcast_to(table[d : d + 1, :], (16, W)).astype(jnp.bfloat16)
+    last = pltpu.make_async_copy(
+        table_ref, out_ref.at[:, pl.ds(ROWS, SEND_ROWS - ROWS), :], done.at[PLANE + 1]
+    )
+    last.start()
+    for copy in copies:
+        copy.wait()
+    last.wait()
 
 
 def score_kernel(
-    offset, column_ref, hot_ref, table_ref, got_ref, mine_ref, other_ref, carried_ref,
+    widths, offset, column_ref, hot_ref, table_ref, got_ref, mine_ref, other_ref, carried_ref,
     query_out, mine_out, other_out,
     slot_query, slot_label, item_page, item_base, item_left, turned, query_acc, page_acc, *work,
 ):
     rows = GROUP * QT
     if query_acc is None:
         query_acc = query_out
-    token_refs, logit_refs, expo_refs = work[:ITEMS], work[ITEMS : 2 * ITEMS], work[2 * ITEMS :]
+    most = max(widths)
+    token_refs, logit_refs, expo_refs = work[:most], work[most : 2 * most], work[2 * most :]
     if carried_ref is None:
         query_acc[...] = jnp.zeros_like(query_acc)
     else:
@@ -102,18 +116,18 @@
     for g in range(GROUP):
         slot_query[PART * LIST + g] = 0
         slot_label[PART * LIST + g] = 0
-    for u in range(ITEMS):
+    for u in range(most):
         item_page[items + u] = 0
         item_base[items + u] = PART * LIST
         item_left[items + u] = 0
 
-    def per_round(step, _):
-        at = [step * ITEMS + u for u in range(ITEMS)]
+    def per_round(width, start, step, _):
+        at = [start + step * width + u for u in range(width)]
         page = [item_page[i] for i in at]
         base = [item_base[i] for i in at]
         left = [item_left[i] for i in at]
         query = [[slot_query[b + g] for g in range(GROUP)] for b in base]
-        for u in range(ITEMS):
+        for u in range(width):
             for g in range(GROUP):
                 token_refs[u][g * QT : (g + 1) * QT, :] = got_ref[
                     lax.shift_right_logical(query[u][g], 3),
@@ -123,7 +137,7 @@
         dims = (((1,), (1,)), ((), ()))
         peaks, lses, inverses = [], [], []
         blocks = PATCHES // BLOCK
-        tops, totals = [None] * ITEMS, [None] * ITEMS
+        tops, totals = [None] * width, [None] * width
 
         def multiply(u, c):
             part = (mine_ref, other_ref)[c * BLOCK // HALF]
@@ -146,10 +160,10 @@
         grads = []
         for c in range(blocks):
             multiply(0, c)
-        for u in range(ITEMS):
+        for u in range(width):
             peaks.append(jnp.max(tops[u], axis=0, keepdims=True))
             for c in range(blocks):
-                if u + 1 < ITEMS:
+                if u + 1 < width:
                     multiply(u + 1, c)
                 raise_e(u, c)
             total = jnp.sum(totals[u], axis=0, keepdims=True)
@@ -160,7 +174,7 @@
                 jnp.dot(turned[page[u]], expo_refs[u][...], preferred_element_type=jnp.float32).T
             )
         scale = []
-        for u in range(ITEMS):
+        for u in range(width):
             page_id = first_page + column_ref[page[u]] * NY
             hot = jnp.logical_or(hot_ref[0] == page_id, hot_ref[1] == page_id)
             shift = jnp.where(hot, HOT_SHIFT, 0.0).astype(jnp.float32)
@@ -174,19 +188,26 @@
                 slope = live * (1.0 / (1.0 + jnp.exp(-logit)) - label)
                 parts.append(slope * inverses[u][mine])
             scale.append(jnp.concatenate(parts, axis=0))
-        for u in range(ITEMS):
+        for u in range(width):
             scaled = (token_refs[u][...].astype(jnp.float32) * scale[u]).astype(jnp.bfloat16)
             page_acc[page[u]] += jnp.dot(
                 expo_refs[u][...], scaled, preferred_element_type=jnp.float32
             )
-        for u in range(ITEMS):
+        for u in range(width):
             grad = grads[u] * scale[u]
             for g in range(GROUP):
                 rows_at = pl.ds(pl.multiple_of(query[u][g] * QT, QT), QT)
                 query_acc[rows_at, :] += grad[g * QT : (g + 1) * QT]
         return 0
 
-    lax.fori_loop(0, (items + ITEMS - 1) // ITEMS, per_round, 0)
+    start = jnp.int32(0)
+    for width in widths:
+        if width == widths[-1]:
+            turns = (items - start + width - 1) // width
+        else:
+            turns = (items - start + 1) // width
+        lax.fori_loop(0, turns, functools.partial(per_round, width, start), 0)
+        start = jnp.minimum(start + turns * width, items)
     for k in range(PART):
         mine_out[k] = page_acc[k, :HALF, :].astype(jnp.bfloat16)
         other_out[k] = page_acc[k, HALF:, :].astype(jnp.bfloat16)
@@ -227,12 +248,12 @@
     return total.astype(jnp.bfloat16)
 
 
-def first_kernel(offset, *refs):
-    score_kernel(offset, *refs[:6], None, *refs[6:15], None, *refs[15:])
-
-
-def second_kernel(offset, *refs):
-    score_kernel(offset, *refs)
+def first_kernel(widths, offset, *refs):
+    score_kernel(widths, offset, *refs[:6], None, *refs[6:15], None, *refs[15:])
+
+
+def second_kernel(widths, offset, *refs):
+    score_kernel(widths, offset, *refs)
 
 
 def score(column, hot_pages, table, got, mine, other, carried=None):
@@ -240,9 +261,11 @@
     smem = pl.BlockSpec(memory_space=pltpu.SMEM)
     vmem = pl.BlockSpec(memory_space=pltpu.VMEM)
     last = carried is not None
+    widths = (2,) if last else (4, 2)
+    most = max(widths)
     pages = jax.ShapeDtypeStruct((PART, HALF, W), jnp.bfloat16)
     sums = jax.ShapeDtypeStruct((PLANE * ROWS, W), jnp.bfloat16 if last else jnp.float32)
-    items = PART * SLOTS // GROUP + ITEMS
+    items = PART * SLOTS // GROUP + most
     rows = GROUP * QT
     scratch = [
         pltpu.SMEM((PART * LIST + GROUP,), jnp.int32),
@@ -254,16 +277,16 @@
     ]
     scratch += [pltpu.VMEM((PLANE * ROWS, W), jnp.float32)] * last
     scratch += [pltpu.VMEM((PART, PATCHES, W), jnp.float32)]
-    scratch += [pltpu.VMEM((rows, W), jnp.bfloat16)] * ITEMS
-    scratch += [pltpu.VMEM((PATCHES, rows), jnp.float32)] * ITEMS
-    scratch += [pltpu.VMEM((PATCHES, rows), jnp.bfloat16)] * ITEMS
+    scratch += [pltpu.VMEM((rows, W), jnp.bfloat16)] * most
+    scratch += [pltpu.VMEM((PATCHES, rows), jnp.float32)] * most
+    scratch += [pltpu.VMEM((PATCHES, rows), jnp.bfloat16)] * most
     return pl.pallas_call(
-        functools.partial(second_kernel if last else first_kernel, offset),
+        functools.partial(second_kernel if last else first_kernel, widths, offset),
         out_shape=(sums, pages, pages),
         in_specs=[smem] * 3 + [vmem] * (3 + last),
         out_specs=(vmem, vmem, vmem),
         scratch_shapes=scratch,
-        compiler_params=pltpu.CompilerParams(vmem_limit_bytes=18 << 20),
+        compiler_params=pltpu.CompilerParams(vmem_limit_bytes=20 << 20),
         cost_estimate=pl.CostEstimate(
             flops=6 * PLANE * CAP * 2 * QT * PATCHES * W * 2,
             bytes_accessed=8 << 20,
@@ -282,8 +305,12 @@
             jax.ShapeDtypeStruct((PLANE, SEND_ROWS, W), jnp.bfloat16),
             jax.ShapeDtypeStruct((HALF, W), jnp.bfloat16),
         ),
-        in_specs=[smem] * 4 + [vmem] * 2,
-        out_specs=(vmem, vmem),
+        in_specs=[smem] * 4 + [pl.BlockSpec(memory_space=pl.ANY)] * 2,
+        out_specs=(pl.BlockSpec(memory_space=pl.ANY),) * 2,
+        scratch_shapes=[
+            pltpu.VMEM((PLANE, SEND_ROWS - ROWS, W), jnp.bfloat16),
+            pltpu.SemaphoreType.DMA((PLANE + 2,)),
+        ],
     )(pair_page[:, 0], pair_query, pair_label, core, queries.reshape(ROWS, W), pages[0])
     near, far = gather_column(half)
     other_near, other_far = swap_cores(near), swap_cores(far)

time: 81.2 us -> 114 us (1.40)
  Pallas kernels: 14.1 us -> 52 us
  starting transfers between devices: 39.4 us -> 37.3 us
  waiting for transfers between devices: 24 us -> 22 us
    pallas_call x1, Pallas kernels: 2.35 us -> 37.7 us  [shards(): pl.pallas_call(pack_kernel, out_shape=(jax.ShapeDtypeStruct((PLANE, SEND_...]
    ppermute x4, starting transfers between devices: 9.16 us -> 5.51 us  [swap_cores(): return lax.ppermute(array, 'core', [(0, 1), (1, 0)])]
    pallas_call x2, Pallas kernels: 11.7 us -> 14.3 us  [score(): pl.pallas_call(functools.partial(second_kernel if last else first_kernel,...]
    ppermute x10, waiting for transfers between devices: 13.7 us -> 11.6 us  [move(): return lax.ppermute(array, 'z', [(i, (i + step) % NZ) for i in range(NZ)])]
    ppermute x10, starting transfers between devices: 19.6 us -> 20.9 us  [move(): return lax.ppermute(array, 'z', [(i, (i + step) % NZ) for i in range(NZ)])]
  transfers between devices with their start and end apart: 16 -> 16, of which waited for: 7 -> 9; matrix products, arithmetic and copies ran while one was open for 2% -> 1% of each run, Pallas kernels for 9% -> 7%
where the time goes in v6:
time: 114 us
  Pallas kernels  52 us (46%)
  starting transfers between devices  37.3 us (33%)
  waiting for transfers between devices  22 us (19%)
  other arithmetic  2.11 us (2%)
    pallas_call x1, Pallas kernels, shards(): pl.pallas_call(pack_kernel, out_shape=(jax.ShapeDtypeStruct((PLANE, SEND_...  37.7 us
    ppermute x10, starting transfers between devices, move(): return lax.ppermute(array, 'z', [(i, (i + step) % NZ) for i in range(NZ)])  20.9 us
    pallas_call x2, Pallas kernels, score(): pl.pallas_call(functools.partial(second_kernel if last else first_kernel,...  14.3 us
    ppermute x10, waiting for transfers between devices, move(): return lax.ppermute(array, 'z', [(i, (i + step) % NZ) for i in range(NZ)])  11.6 us
    all_to_all x2, starting transfers between devices, exchange(): return lax.all_to_all(array, axes, split_axis=0, concat_axis=0, tiled=True)  10.9 us
    all_to_all x2, waiting for transfers between devices, exchange(): return lax.all_to_all(array, axes, split_axis=0, concat_axis=0, tiled=True)  9.09 us
    ppermute x4, starting transfers between devices, swap_cores(): return lax.ppermute(array, 'core', [(0, 1), (1, 0)])  5.51 us
  transfers between devices with their start and end apart: 16, of which 9 were waited for; matrix products, arithmetic and copies ran while one was open for 1% of the time, Pallas kernels for 7%

profile of v6, /device:TPU:1, one launch (start us, length us, event | category | flops | bytes accessed | tf_op | source)
XLA Modules:
  0.0 114.3 jit_solution(8238400613985471469)
XLA Ops:
  0.6 37.7 %shard_map.86 = (bf16[16,272,128]{2,1,0:T(8,128)(2,1)}, bf16[512,128]{1,0:T(8,128)(2,1)}) custom-call(s32[64]{0:T(128)} %bitcast.42, s32[64]{0:T(128)} %query_ref.1, s32[64]{0:T(128)} %label_ref.1, s32[1]{0:T(128)} %bitcast.2.core_ref, bf16[256,128]{1,0:T(8,128)(2,1)} %bitcast.40, bf16[1024,128]{1,0:T(8,128)(2,1)} %bitcast.38), custom_call_target="tpu_custom_call" | custom-call | tf_op jit(solution)/shard_map/pallas_call | solution.py:302
  38.3 7.8 %collective-permute-start.2 = (bf16[512,128]{1,0:T(8,128)(2,1)}, bf16[512,128]{1,0:T(8,128)(2,1)S(1)}, u32[]{:S(2)}, u32[]{:S(2)}) collective-permute-start(bf16[512,128]{1,0:T(8,128)(2,1)} %get-tuple-element.17), channel_id=1, source_target_pairs={{0,32},{8,40},{16,48},{24,56},{32,0},{40,8},{48,16},{56,24},{1,33}... | collective-permute-start | bytes 393224 | tf_op jit(solution)/shard_map/ppermute | solution.py:227
  46.1 0.0 collective-permute-start.1
  46.1 1.5 %collective-permute-start = (bf16[512,128]{1,0:T(8,128)(2,1)}, bf16[512,128]{1,0:T(8,128)(2,1)S(1)}, u32[]{:S(2)}, u32[]{:S(2)}) collective-permute-start(bf16[512,128]{1,0:T(8,128)(2,1)} %get-tuple-element.17), channel_id=1, source_target_pairs={{0,8},{8,16},{16,24},{24,32},{32,40},{40,48},{48,56},{56,0},{1,9},... | collective-permute-start | bytes 393224 | tf_op jit(solution)/shard_map/ppermute | solution.py:227
  47.6 0.0 copy-start.2
  47.6 6.9 %all-to-all-start = ((bf16[16,272,128]{2,1,0:T(8,128)(2,1)}), bf16[16,272,128]{2,1,0:T(8,128)(2,1)S(1)}, u32[]{:S(2)}, u32[]{:S(2)}) async-start(bf16[16,272,128]{2,1,0:T(8,128)(2,1)} %get-tuple-element.16), calls=%async_computation | async-start | bytes 2228224 | tf_op jit(solution)/shard_map/all_to_all | solution.py:219
  54.5 0.0 copy-start
  54.5 0.0 collective-permute-done.2
  54.5 1.2 %collective-permute-done.1 = bf16[512,128]{1,0:T(8,128)(2,1)S(1)} collective-permute-done((bf16[512,128]{1,0:T(8,128)(2,1)}, bf16[512,128]{1,0:T(8,128)(2,1)S(1)}, u32[]{:S(2)}, u32[]{:S(2)}) %collective-permute-start.1) | collective-permute-done | bytes 131104 | tf_op jit(solution)/shard_map/ppermute | solution.py:227
  55.7 0.0 collective-permute-done
  55.8 1.0 collective-permute-start.4
  56.8 1.7 %collective-permute-start.5 = (bf16[2,512,128]{2,1,0:T(8,128)(2,1)S(1)}, bf16[2,512,128]{2,1,0:T(8,128)(2,1)S(1)}, u32[]{:S(2)}, u32[]{:S(2)}) collective-permute-start(bf16[2,512,128]{2,1,0:T(8,128)(2,1)S(1)} %get-tuple-element.35), channel_id=1, source_target_pairs={{0,56},{8,0},{16,8},{24,16},{32,24},{40,32},{48,40},{56,48},{1,57}... | collective-permute-start | bytes 786440 | tf_op jit(solution)/shard_map/ppermute | solution.py:227
  58.5 0.0 copy-done.2
  58.5 4.8 %collective-permute-done.4 = bf16[2,512,128]{2,1,0:T(8,128)(2,1)S(1)} collective-permute-done((bf16[2,512,128]{2,1,0:T(8,128)(2,1)S(1)}, bf16[2,512,128]{2,1,0:T(8,128)(2,1)S(1)}, u32[]{:S(2)}, u32[]{:S(2)}) %collective-permute-start.4) | collective-permute-done | bytes 262176 | tf_op jit(solution)/shard_map/ppermute | solution.py:227
  63.4 0.5 collective-permute-done.5
  63.9 2.1 %collective-permute-start.6 = (bf16[4,512,128]{2,1,0:T(8,128)(2,1)S(1)}, bf16[4,512,128]{2,1,0:T(8,128)(2,1)S(1)}, u32[]{:S(2)}, u32[]{:S(2)}) collective-permute-start(bf16[4,512,128]{2,1,0:T(8,128)(2,1)S(1)} %constant_dynamic-update-slice_fusion.refs_4_), channel_id=1, source_target_pairs={{0,1},{1,0},{2,3},{3,2},{4,5},{5,4},{6,7},{7,6},{8,9},{9,8},{10,11... | collective-permute-start | bytes 1572872 | tf_op jit(solution)/shard_map/ppermute | solution.py:223
  65.9 0.1 fusion.8
  66.0 0.1 pad_add_fusion.1.refs_0_
  66.1 4.2 %all-to-all-done.refs_3_ = bf16[16,272,128]{2,1,0:T(8,128)(2,1)S(1)} async-done(((bf16[16,272,128]{2,1,0:T(8,128)(2,1)}), bf16[16,272,128]{2,1,0:T(8,128)(2,1)S(1)}, u32[]{:S(2)}, u32[]{:S(2)}) %all-to-all-start) | async-done | bytes 1114144 | tf_op jit(solution)/shard_map/all_to_all | solution.py:219
  70.3 0.0 collective-permute-done.6.refs_5_
  70.3 0.0 copy-done
  70.3 0.0 copy-start.1
  70.3 5.9 %shard_map.87 = (f32[4096,128]{1,0:T(8,128)S(1)}, bf16[4,512,128]{2,1,0:T(8,128)(2,1)S(1)}, bf16[4,512,128]{2,1,0:T(8,128)(2,1)S(1)}) custom-call(s32[5]{0:T(128)S(1)} %pad_add_fusion.1.refs_0_, s32[2]{0:T(128)S(1)} %copy-done, s32[16,32]{1,0:T(8,128)S(1)} %bitcast.30, bf16[16,272,128]{2,1,0:T(8,128)(2,1)S(1)} %all-to-all-done.refs_3_, ...), custom_call_target="tpu_custom_call" | custom-call | flops 3221225472 | bytes 8388608 | tf_op jit(solution)/shard_map/pallas_call | solution.py:283
  76.3 3.3 %collective-permute-start.7 = (bf16[4,512,128]{2,1,0:T(8,128)(2,1)S(1)}, bf16[4,512,128]{2,1,0:T(8,128)(2,1)S(1)}, u32[]{:S(2)}, u32[]{:S(2)}) collective-permute-start(bf16[4,512,128]{2,1,0:T(8,128)(2,1)S(1)} %get-tuple-element.20), channel_id=1, source_target_pairs={{0,1},{1,0},{2,3},{3,2},{4,5},{5,4},{6,7},{7,6},{8,9},{9,8},{10,11... | collective-permute-start | bytes 1572872 | tf_op jit(solution)/shard_map/ppermute | solution.py:223
  79.6 0.0 copy-done.1
  79.6 0.1 pad_maximum_fusion.refs_4_
  79.7 0.1 collective-permute-start.3
  79.8 0.1 pad_add_fusion.refs_0_
  79.9 1.3 %collective-permute-done.7 = bf16[4,512,128]{2,1,0:T(8,128)(2,1)S(1)} collective-permute-done((bf16[4,512,128]{2,1,0:T(8,128)(2,1)S(1)}, bf16[4,512,128]{2,1,0:T(8,128)(2,1)S(1)}, u32[]{:S(2)}, u32[]{:S(2)}) %collective-permute-start.7) | collective-permute-done | bytes 524320 | tf_op jit(solution)/shard_map/ppermute | solution.py:223
  81.2 0.1 add_convert_fusion
  81.3 0.8 collective-permute-start.8
  82.1 2.0 %collective-permute-start.9 = (bf16[2,512,128]{2,1,0:T(8,128)(2,1)S(1)}, bf16[2,512,128]{2,1,0:T(8,128)(2,1)S(1)}, u32[]{:S(2)}, u32[]{:S(2)}) collective-permute-start(bf16[2,512,128]{2,1,0:T(8,128)(2,1)S(1)} %get-tuple-element.24), channel_id=1, source_target_pairs={{0,56},{8,0},{16,8},{24,16},{32,24},{40,32},{48,40},{56,48},{1,57}... | collective-permute-start | bytes 786440 | tf_op jit(solution)/shard_map/ppermute | solution.py:227
  84.1 0.0 collective-permute-done.3.refs_5_
  84.1 8.4 %shard_map.88 = (bf16[4096,128]{1,0:T(8,128)(2,1)}, bf16[4,512,128]{2,1,0:T(8,128)(2,1)S(1)}, bf16[4,512,128]{2,1,0:T(8,128)(2,1)S(1)}) custom-call(s32[5]{0:T(128)S(1)} %pad_add_fusion.refs_0_, s32[2]{0:T(128)S(1)} %copy-done, s32[16,32]{1,0:T(8,128)S(1)} %bitcast.31, bf16[16,272,128]{2,1,0:T(8,128)(2,1)S(1)} %all-to-all-done.refs_3_, ...), custom_call_target="tpu_custom_call" | custom-call | flops 3221225472 | bytes 8388608 | tf_op jit(solution)/shard_map/pallas_call | solution.py:283
  92.5 0.0 collective-permute-start.10
  92.5 0.0 collective-permute-done.8
  92.5 0.0 collective-permute-done.9
  92.5 4.0 %all-to-all-start.1 = ((bf16[16,256,128]{2,1,0:T(8,128)(2,1)}), bf16[16,256,128]{2,1,0:T(8,128)(2,1)S(1)}, u32[]{:S(2)}, u32[]{:S(2)}) async-start(bf16[16,256,128]{2,1,0:T(8,128)(2,1)} %bitcast.10), calls=%async_computation.1 | async-start | bytes 2097152 | tf_op jit(solution)/shard_map/all_to_all | solution.py:219
  96.6 0.0 collective-permute-done.10
  96.6 0.2 fusion.3
  96.8 0.3 collective-permute-start.11
  97.0 3.2 %collective-permute-start.13 = (bf16[512,128]{1,0:T(8,128)(2,1)S(1)}, bf16[512,128]{1,0:T(8,128)(2,1)S(1)}, u32[]{:S(2)}, u32[]{:S(2)}) collective-permute-start(bf16[512,128]{1,0:T(8,128)(2,1)S(1)} %get-tuple-element.31), channel_id=1, source_target_pairs={{0,32},{8,40},{16,48},{24,56},{32,0},{40,8},{48,16},{56,24},{1,33}... | collective-permute-start | bytes 393224 | tf_op jit(solution)/shard_map/ppermute | solution.py:227
  100.2 2.6 %collective-permute-start.12 = (bf16[512,128]{1,0:T(8,128)(2,1)S(1)}, bf16[512,128]{1,0:T(8,128)(2,1)S(1)}, u32[]{:S(2)}, u32[]{:S(2)}) collective-permute-start(bf16[512,128]{1,0:T(8,128)(2,1)S(1)} %get-tuple-element.32), channel_id=1, source_target_pairs={{0,56},{8,0},{16,8},{24,16},{32,24},{40,32},{48,40},{56,48},{1,57}... | collective-permute-start | bytes 393224 | tf_op jit(solution)/shard_map/ppermute | solution.py:227
  102.8 0.1 collective-permute-done.11
  102.8 4.4 %collective-permute-done.13 = bf16[512,128]{1,0:T(8,128)(2,1)S(1)} collective-permute-done((bf16[512,128]{1,0:T(8,128)(2,1)S(1)}, bf16[512,128]{1,0:T(8,128)(2,1)S(1)}, u32[]{:S(2)}, u32[]{:S(2)}) %collective-permute-start.13) | collective-permute-done | bytes 131104 | tf_op jit(solution)/shard_map/ppermute | solution.py:227
  107.3 0.6 collective-permute-done.12
  107.9 0.7 fusion.6
  108.6 4.9 %all-to-all-done.1 = bf16[16,256,128]{2,1,0:T(8,128)(2,1)S(1)} async-done(((bf16[16,256,128]{2,1,0:T(8,128)(2,1)}), bf16[16,256,128]{2,1,0:T(8,128)(2,1)S(1)}, u32[]{:S(2)}, u32[]{:S(2)}) %all-to-all-start.1) | async-done | bytes 1048608 | tf_op jit(solution)/shard_map/all_to_all | solution.py:219
  113.5 0.8 reduce_sum.12
  (5 shorter events, 0.1 us)
Async XLA Ops:
  38.3 16.2 %collective-permute-start.2 = (bf16[512,128]{1,0:T(8,128)(2,1)}, bf16[512,128]{1,0:T(8,128)(2,1)S(1)}, u32[]{:S(2)}, u32[]{:S(2)}) collective-permute-start(bf16[512,128]{1,0:T(8,128)(2,1)} %get-tuple-element.17), channel_id=1, source_target_pairs={{0,32},{8,40},{16,48},{24,56},{32,0},{40,8},{48,16},{56,24},{1,33}... | collective-permute-start | bytes 393224 | tf_op jit(solution)/shard_map/ppermute | solution.py:227
  46.1 9.6 %collective-permute-start.1 = (bf16[512,128]{1,0:T(8,128)(2,1)}, bf16[512,128]{1,0:T(8,128)(2,1)S(1)}, u32[]{:S(2)}, u32[]{:S(2)}) collective-permute-start(bf16[512,128]{1,0:T(8,128)(2,1)} %get-tuple-element.17), channel_id=1, source_target_pairs={{0,56},{8,0},{16,8},{24,16},{32,24},{40,32},{48,40},{56,48},{1,57}... | collective-permute-start | bytes 393224 | tf_op jit(solution)/shard_map/ppermute | solution.py:227
  46.1 9.6 %collective-permute-start = (bf16[512,128]{1,0:T(8,128)(2,1)}, bf16[512,128]{1,0:T(8,128)(2,1)S(1)}, u32[]{:S(2)}, u32[]{:S(2)}) collective-permute-start(bf16[512,128]{1,0:T(8,128)(2,1)} %get-tuple-element.17), channel_id=1, source_target_pairs={{0,8},{8,16},{16,24},{24,32},{32,40},{40,48},{48,56},{56,0},{1,9},... | collective-permute-start | bytes 393224 | tf_op jit(solution)/shard_map/ppermute | solution.py:227
  47.6 10.9 %copy-start.2 = (s32[8]{0:T(128)S(1)}, s32[8]{0:T(128)}, u32[]{:S(2)}) copy-start(s32[8]{0:T(128)} %constant.38.clone) | copy-start | bytes 100
  47.6 22.7 %all-to-all-start = ((bf16[16,272,128]{2,1,0:T(8,128)(2,1)}), bf16[16,272,128]{2,1,0:T(8,128)(2,1)S(1)}, u32[]{:S(2)}, u32[]{:S(2)}) async-start(bf16[16,272,128]{2,1,0:T(8,128)(2,1)} %get-tuple-element.16), calls=%async_computation | async-start | bytes 2228224 | tf_op jit(solution)/shard_map/all_to_all | solution.py:219
  54.5 15.8 %copy-start = (s32[2]{0:T(128)S(1)}, s32[2]{0:T(128)}, u32[]{:S(2)}) copy-start(s32[2]{0:T(128)} %refs_1_.3) | copy-start | bytes 28
  55.8 7.6 %collective-permute-start.4 = (bf16[2,512,128]{2,1,0:T(8,128)(2,1)S(1)}, bf16[2,512,128]{2,1,0:T(8,128)(2,1)S(1)}, u32[]{:S(2)}, u32[]{:S(2)}) collective-permute-start(bf16[2,512,128]{2,1,0:T(8,128)(2,1)S(1)} %get-tuple-element.36), channel_id=1, source_target_pairs={{0,8},{8,16},{16,24},{24,32},{32,40},{40,48},{48,56},{56,0},{1,9},... | collective-permute-start | bytes 786440 | tf_op jit(solution)/shard_map/ppermute | solution.py:227
  56.8 7.1 %collective-permute-start.5 = (bf16[2,512,128]{2,1,0:T(8,128)(2,1)S(1)}, bf16[2,512,128]{2,1,0:T(8,128)(2,1)S(1)}, u32[]{:S(2)}, u32[]{:S(2)}) collective-permute-start(bf16[2,512,128]{2,1,0:T(8,128)(2,1)S(1)} %get-tuple-element.35), channel_id=1, source_target_pairs={{0,56},{8,0},{16,8},{24,16},{32,24},{40,32},{48,40},{56,48},{1,57}... | collective-permute-start | bytes 786440 | tf_op jit(solution)/shard_map/ppermute | solution.py:227
  63.9 6.4 %collective-permute-start.6 = (bf16[4,512,128]{2,1,0:T(8,128)(2,1)S(1)}, bf16[4,512,128]{2,1,0:T(8,128)(2,1)S(1)}, u32[]{:S(2)}, u32[]{:S(2)}) collective-permute-start(bf16[4,512,128]{2,1,0:T(8,128)(2,1)S(1)} %constant_dynamic-update-slice_fusion.refs_4_), channel_id=1, source_target_pairs={{0,1},{1,0},{2,3},{3,2},{4,5},{5,4},{6,7},{7,6},{8,9},{9,8},{10,11... | collective-permute-start | bytes 1572872 | tf_op jit(solution)/shard_map/ppermute | solution.py:223
  70.3 9.3 %copy-start.1 = (bf16[512,128]{1,0:T(8,128)(2,1)S(1)}, bf16[512,128]{1,0:T(8,128)(2,1)}, u32[]{:S(2)}) copy-start(bf16[512,128]{1,0:T(8,128)(2,1)} %get-tuple-element.17) | copy-start | bytes 393220
  76.3 4.9 %collective-permute-start.7 = (bf16[4,512,128]{2,1,0:T(8,128)(2,1)S(1)}, bf16[4,512,128]{2,1,0:T(8,128)(2,1)S(1)}, u32[]{:S(2)}, u32[]{:S(2)}) collective-permute-start(bf16[4,512,128]{2,1,0:T(8,128)(2,1)S(1)} %get-tuple-element.20), channel_id=1, source_target_pairs={{0,1},{1,0},{2,3},{3,2},{4,5},{5,4},{6,7},{7,6},{8,9},{9,8},{10,11... | collective-permute-start | bytes 1572872 | tf_op jit(solution)/shard_map/ppermute | solution.py:223
  79.7 4.4 %collective-permute-start.3 = (bf16[4,512,128]{2,1,0:T(8,128)(2,1)S(1)}, bf16[4,512,128]{2,1,0:T(8,128)(2,1)S(1)}, u32[]{:S(2)}, u32[]{:S(2)}) collective-permute-start(bf16[4,512,128]{2,1,0:T(8,128)(2,1)S(1)} %pad_maximum_fusion.refs_4_), channel_id=1, source_target_pairs={{0,1},{1,0},{2,3},{3,2},{4,5},{5,4},{6,7},{7,6},{8,9},{9,8},{10,11... | collective-permute-start | bytes 1572872 | tf_op jit(solution)/shard_map/ppermute | solution.py:223
  81.3 11.2 %collective-permute-start.8 = (bf16[2,512,128]{2,1,0:T(8,128)(2,1)S(1)}, bf16[2,512,128]{2,1,0:T(8,128)(2,1)S(1)}, u32[]{:S(2)}, u32[]{:S(2)}) collective-permute-start(bf16[2,512,128]{2,1,0:T(8,128)(2,1)S(1)} %get-tuple-element.23), channel_id=1, source_target_pairs={{0,8},{8,16},{16,24},{24,32},{32,40},{40,48},{48,56},{56,0},{1,9},... | collective-permute-start | bytes 786440 | tf_op jit(solution)/shard_map/ppermute | solution.py:227
  82.1 10.4 %collective-permute-start.9 = (bf16[2,512,128]{2,1,0:T(8,128)(2,1)S(1)}, bf16[2,512,128]{2,1,0:T(8,128)(2,1)S(1)}, u32[]{:S(2)}, u32[]{:S(2)}) collective-permute-start(bf16[2,512,128]{2,1,0:T(8,128)(2,1)S(1)} %get-tuple-element.24), channel_id=1, source_target_pairs={{0,56},{8,0},{16,8},{24,16},{32,24},{40,32},{48,40},{56,48},{1,57}... | collective-permute-start | bytes 786440 | tf_op jit(solution)/shard_map/ppermute | solution.py:227
  92.5 4.0 %collective-permute-start.10 = (bf16[4,512,128]{2,1,0:T(8,128)(2,1)S(1)}, bf16[4,512,128]{2,1,0:T(8,128)(2,1)S(1)}, u32[]{:S(2)}, u32[]{:S(2)}) collective-permute-start(bf16[4,512,128]{2,1,0:T(8,128)(2,1)S(1)} %get-tuple-element.27), channel_id=1, source_target_pairs={{0,1},{1,0},{2,3},{3,2},{4,5},{5,4},{6,7},{7,6},{8,9},{9,8},{10,11... | collective-permute-start | bytes 1572872 | tf_op jit(solution)/shard_map/ppermute | solution.py:223
  92.5 21.0 %all-to-all-start.1 = ((bf16[16,256,128]{2,1,0:T(8,128)(2,1)}), bf16[16,256,128]{2,1,0:T(8,128)(2,1)S(1)}, u32[]{:S(2)}, u32[]{:S(2)}) async-start(bf16[16,256,128]{2,1,0:T(8,128)(2,1)} %bitcast.10), calls=%async_computation.1 | async-start | bytes 2097152 | tf_op jit(solution)/shard_map/all_to_all | solution.py:219
  96.8 6.1 %collective-permute-start.11 = (bf16[512,128]{1,0:T(8,128)(2,1)S(1)}, bf16[512,128]{1,0:T(8,128)(2,1)S(1)}, u32[]{:S(2)}, u32[]{:S(2)}) collective-permute-start(bf16[512,128]{1,0:T(8,128)(2,1)S(1)} %get-tuple-element.30), channel_id=1, source_target_pairs={{0,8},{8,16},{16,24},{24,32},{32,40},{40,48},{48,56},{56,0},{1,9},... | collective-permute-start | bytes 393224 | tf_op jit(solution)/shard_map/ppermute | solution.py:227
  97.0 10.3 %collective-permute-start.13 = (bf16[512,128]{1,0:T(8,128)(2,1)S(1)}, bf16[512,128]{1,0:T(8,128)(2,1)S(1)}, u32[]{:S(2)}, u32[]{:S(2)}) collective-permute-start(bf16[512,128]{1,0:T(8,128)(2,1)S(1)} %get-tuple-element.31), channel_id=1, source_target_pairs={{0,32},{8,40},{16,48},{24,56},{32,0},{40,8},{48,16},{56,24},{1,33}... | collective-permute-start | bytes 393224 | tf_op jit(solution)/shard_map/ppermute | solution.py:227
  100.2 7.7 %collective-permute-start.12 = (bf16[512,128]{1,0:T(8,128)(2,1)S(1)}, bf16[512,128]{1,0:T(8,128)(2,1)S(1)}, u32[]{:S(2)}, u32[]{:S(2)}) collective-permute-start(bf16[512,128]{1,0:T(8,128)(2,1)S(1)} %get-tuple-element.32), channel_id=1, source_target_pairs={{0,56},{8,0},{16,8},{24,16},{32,24},{40,32},{48,40},{56,48},{1,57}... | collective-permute-start | bytes 393224 | tf_op jit(solution)/shard_map/ppermute | solution.py:227

commit v7 on v6

--- a/solution.py
+++ b/solution.py
@@ -305,7 +305,7 @@
             jax.ShapeDtypeStruct((PLANE, SEND_ROWS, W), jnp.bfloat16),
             jax.ShapeDtypeStruct((HALF, W), jnp.bfloat16),
         ),
-        in_specs=[smem] * 4 + [pl.BlockSpec(memory_space=pl.ANY)] * 2,
+        in_specs=[smem] * 4 + [vmem] * 2,
         out_specs=(pl.BlockSpec(memory_space=pl.ANY),) * 2,
         scratch_shapes=[
             pltpu.VMEM((PLANE, SEND_ROWS - ROWS, W), jnp.bfloat16),

time: 114 us -> 79.3 us (0.70)
  Pallas kernels: 52 us -> 15.2 us
  starting transfers between devices: 37.3 us -> 39.5 us
    pallas_call x1, Pallas kernels: 37.7 us -> 2.21 us  [shards(): pl.pallas_call(pack_kernel, out_shape=(jax.ShapeDtypeStruct((PLANE, SEND_...]
    pallas_call x2, Pallas kernels: 14.3 us -> 13 us  [score(): pl.pallas_call(functools.partial(second_kernel if last else first_kernel,...]
  transfers between devices with their start and end apart: 16 -> 16, of which waited for: 9 -> 8; matrix products, arithmetic and copies ran while one was open for 1% -> 2% of each run, Pallas kernels for 7% -> 9%
where the time goes in v7:
time: 79.3 us; the launch traced here: 79 us
  starting transfers between devices  39.5 us (50%)
  waiting for transfers between devices  21.3 us (27%)
  Pallas kernels  15.2 us (19%)
  other arithmetic  2.11 us (3%)
    ppermute x10, starting transfers between devices, move(): return lax.ppermute(array, 'z', [(i, (i + step) % NZ) for i in range(NZ)])  21.5 us
    pallas_call x2, Pallas kernels, score(): pl.pallas_call(functools.partial(second_kernel if last else first_kernel,...  13 us
    ppermute x10, waiting for transfers between devices, move(): return lax.ppermute(array, 'z', [(i, (i + step) % NZ) for i in range(NZ)])  11.8 us
    all_to_all x2, starting transfers between devices, exchange(): return lax.all_to_all(array, axes, split_axis=0, concat_axis=0, tiled=True)  11.5 us
    all_to_all x2, waiting for transfers between devices, exchange(): return lax.all_to_all(array, axes, split_axis=0, concat_axis=0, tiled=True)  8.21 us
    ppermute x4, starting transfers between devices, swap_cores(): return lax.ppermute(array, 'core', [(0, 1), (1, 0)])  6.44 us
    pallas_call x1, Pallas kernels, shards(): pl.pallas_call(pack_kernel, out_shape=(jax.ShapeDtypeStruct((PLANE, SEND_...  2.21 us
  transfers between devices with their start and end apart: 16, of which 8 were waited for; matrix products, arithmetic and copies ran while one was open for 2% of the time, Pallas kernels for 9%

profile of v7, /device:TPU:1, one launch (start us, length us, event | category | flops | bytes accessed | tf_op | source)
XLA Modules:
  0.0 79.0 jit_solution(13922383303067736304)
XLA Ops:
  0.6 2.2 %shard_map.86 = (bf16[16,272,128]{2,1,0:T(8,128)(2,1)}, bf16[512,128]{1,0:T(8,128)(2,1)}) custom-call(s32[64]{0:T(128)} %bitcast.42, s32[64]{0:T(128)} %query_ref.1, s32[64]{0:T(128)} %label_ref.1, s32[1]{0:T(128)} %bitcast.2.core_ref, bf16[256,128]{1,0:T(8,128)(2,1)} %bitcast.40, bf16[1024,128]{1,0:T(8,128)(2,1)} %bitcast.38), custom_call_target="tpu_custom_call" | custom-call | tf_op jit(solution)/shard_map/pallas_call | solution.py:302
  2.9 7.8 %collective-permute-start.2 = (bf16[512,128]{1,0:T(8,128)(2,1)}, bf16[512,128]{1,0:T(8,128)(2,1)S(1)}, u32[]{:S(2)}, u32[]{:S(2)}) collective-permute-start(bf16[512,128]{1,0:T(8,128)(2,1)} %get-tuple-element.17), channel_id=1, source_target_pairs={{0,32},{8,40},{16,48},{24,56},{32,0},{40,8},{48,16},{56,24},{1,33}... | collective-permute-start | bytes 393224 | tf_op jit(solution)/shard_map/ppermute | solution.py:227
  10.7 0.0 collective-permute-start.1
  10.7 1.5 %collective-permute-start = (bf16[512,128]{1,0:T(8,128)(2,1)}, bf16[512,128]{1,0:T(8,128)(2,1)S(1)}, u32[]{:S(2)}, u32[]{:S(2)}) collective-permute-start(bf16[512,128]{1,0:T(8,128)(2,1)} %get-tuple-element.17), channel_id=1, source_target_pairs={{0,8},{8,16},{16,24},{24,32},{32,40},{40,48},{48,56},{56,0},{1,9},... | collective-permute-start | bytes 393224 | tf_op jit(solution)/shard_map/ppermute | solution.py:227
  12.1 0.0 copy-start.2
  12.1 6.9 %all-to-all-start = ((bf16[16,272,128]{2,1,0:T(8,128)(2,1)}), bf16[16,272,128]{2,1,0:T(8,128)(2,1)S(1)}, u32[]{:S(2)}, u32[]{:S(2)}) async-start(bf16[16,272,128]{2,1,0:T(8,128)(2,1)} %get-tuple-element.16), calls=%async_computation | async-start | bytes 2228224 | tf_op jit(solution)/shard_map/all_to_all | solution.py:219
  19.0 0.0 copy-start
  19.1 0.0 collective-permute-done.2
  19.1 1.2 %collective-permute-done.1 = bf16[512,128]{1,0:T(8,128)(2,1)S(1)} collective-permute-done((bf16[512,128]{1,0:T(8,128)(2,1)}, bf16[512,128]{1,0:T(8,128)(2,1)S(1)}, u32[]{:S(2)}, u32[]{:S(2)}) %collective-permute-start.1) | collective-permute-done | bytes 131104 | tf_op jit(solution)/shard_map/ppermute | solution.py:227
  20.3 0.0 collective-permute-done
  20.3 1.0 %collective-permute-start.4 = (bf16[2,512,128]{2,1,0:T(8,128)(2,1)S(1)}, bf16[2,512,128]{2,1,0:T(8,128)(2,1)S(1)}, u32[]{:S(2)}, u32[]{:S(2)}) collective-permute-start(bf16[2,512,128]{2,1,0:T(8,128)(2,1)S(1)} %get-tuple-element.36), channel_id=1, source_target_pairs={{0,8},{8,16},{16,24},{24,32},{32,40},{40,48},{48,56},{56,0},{1,9},... | collective-permute-start | bytes 786440 | tf_op jit(solution)/shard_map/ppermute | solution.py:227
  21.3 1.7 %collective-permute-start.5 = (bf16[2,512,128]{2,1,0:T(8,128)(2,1)S(1)}, bf16[2,512,128]{2,1,0:T(8,128)(2,1)S(1)}, u32[]{:S(2)}, u32[]{:S(2)}) collective-permute-start(bf16[2,512,128]{2,1,0:T(8,128)(2,1)S(1)} %get-tuple-element.35), channel_id=1, source_target_pairs={{0,56},{8,0},{16,8},{24,16},{32,24},{40,32},{48,40},{56,48},{1,57}... | collective-permute-start | bytes 786440 | tf_op jit(solution)/shard_map/ppermute | solution.py:227
  23.1 0.0 copy-done.2
  23.1 4.8 %collective-permute-done.4 = bf16[2,512,128]{2,1,0:T(8,128)(2,1)S(1)} collective-permute-done((bf16[2,512,128]{2,1,0:T(8,128)(2,1)S(1)}, bf16[2,512,128]{2,1,0:T(8,128)(2,1)S(1)}, u32[]{:S(2)}, u32[]{:S(2)}) %collective-permute-start.4) | collective-permute-done | bytes 262176 | tf_op jit(solution)/shard_map/ppermute | solution.py:227
  27.9 0.5 collective-permute-done.5
  28.4 2.1 %collective-permute-start.6 = (bf16[4,512,128]{2,1,0:T(8,128)(2,1)S(1)}, bf16[4,512,128]{2,1,0:T(8,128)(2,1)S(1)}, u32[]{:S(2)}, u32[]{:S(2)}) collective-permute-start(bf16[4,512,128]{2,1,0:T(8,128)(2,1)S(1)} %constant_dynamic-update-slice_fusion.refs_4_), channel_id=1, source_target_pairs={{0,1},{1,0},{2,3},{3,2},{4,5},{5,4},{6,7},{7,6},{8,9},{9,8},{10,11... | collective-permute-start | bytes 1572872 | tf_op jit(solution)/shard_map/ppermute | solution.py:223
  30.5 0.1 fusion.8
  30.6 0.1 pad_add_fusion.1.refs_0_
  30.6 4.2 %all-to-all-done.refs_3_ = bf16[16,272,128]{2,1,0:T(8,128)(2,1)S(1)} async-done(((bf16[16,272,128]{2,1,0:T(8,128)(2,1)}), bf16[16,272,128]{2,1,0:T(8,128)(2,1)S(1)}, u32[]{:S(2)}, u32[]{:S(2)}) %all-to-all-start) | async-done | bytes 1114144 | tf_op jit(solution)/shard_map/all_to_all | solution.py:219
  34.8 0.0 collective-permute-done.6.refs_5_
  34.8 0.0 copy-done
  34.8 0.0 copy-start.1
  34.9 5.9 %shard_map.87 = (f32[4096,128]{1,0:T(8,128)S(1)}, bf16[4,512,128]{2,1,0:T(8,128)(2,1)S(1)}, bf16[4,512,128]{2,1,0:T(8,128)(2,1)S(1)}) custom-call(s32[5]{0:T(128)S(1)} %pad_add_fusion.1.refs_0_, s32[2]{0:T(128)S(1)} %copy-done, s32[16,32]{1,0:T(8,128)S(1)} %bitcast.30, bf16[16,272,128]{2,1,0:T(8,128)(2,1)S(1)} %all-to-all-done.refs_3_, ...), custom_call_target="tpu_custom_call" | custom-call | flops 3221225472 | bytes 8388608 | tf_op jit(solution)/shard_map/pallas_call | solution.py:283
  40.8 3.3 %collective-permute-start.7 = (bf16[4,512,128]{2,1,0:T(8,128)(2,1)S(1)}, bf16[4,512,128]{2,1,0:T(8,128)(2,1)S(1)}, u32[]{:S(2)}, u32[]{:S(2)}) collective-permute-start(bf16[4,512,128]{2,1,0:T(8,128)(2,1)S(1)} %get-tuple-element.20), channel_id=1, source_target_pairs={{0,1},{1,0},{2,3},{3,2},{4,5},{5,4},{6,7},{7,6},{8,9},{9,8},{10,11... | collective-permute-start | bytes 1572872 | tf_op jit(solution)/shard_map/ppermute | solution.py:223
  44.1 0.0 copy-done.1
  44.1 0.1 pad_maximum_fusion.refs_4_
  44.2 0.1 collective-permute-start.3
  44.3 0.1 pad_add_fusion.refs_0_
  44.4 1.3 %collective-permute-done.7 = bf16[4,512,128]{2,1,0:T(8,128)(2,1)S(1)} collective-permute-done((bf16[4,512,128]{2,1,0:T(8,128)(2,1)S(1)}, bf16[4,512,128]{2,1,0:T(8,128)(2,1)S(1)}, u32[]{:S(2)}, u32[]{:S(2)}) %collective-permute-start.7) | collective-permute-done | bytes 524320 | tf_op jit(solution)/shard_map/ppermute | solution.py:223
  45.7 0.1 add_convert_fusion
  45.8 0.8 %collective-permute-start.8 = (bf16[2,512,128]{2,1,0:T(8,128)(2,1)S(1)}, bf16[2,512,128]{2,1,0:T(8,128)(2,1)S(1)}, u32[]{:S(2)}, u32[]{:S(2)}) collective-permute-start(bf16[2,512,128]{2,1,0:T(8,128)(2,1)S(1)} %get-tuple-element.23), channel_id=1, source_target_pairs={{0,8},{8,16},{16,24},{24,32},{32,40},{40,48},{48,56},{56,0},{1,9},... | collective-permute-start | bytes 786440 | tf_op jit(solution)/shard_map/ppermute | solution.py:227
  46.6 1.9 %collective-permute-start.9 = (bf16[2,512,128]{2,1,0:T(8,128)(2,1)S(1)}, bf16[2,512,128]{2,1,0:T(8,128)(2,1)S(1)}, u32[]{:S(2)}, u32[]{:S(2)}) collective-permute-start(bf16[2,512,128]{2,1,0:T(8,128)(2,1)S(1)} %get-tuple-element.24), channel_id=1, source_target_pairs={{0,56},{8,0},{16,8},{24,16},{32,24},{40,32},{48,40},{56,48},{1,57}... | collective-permute-start | bytes 786440 | tf_op jit(solution)/shard_map/ppermute | solution.py:227
  48.6 0.0 collective-permute-done.3.refs_5_
  48.6 7.1 %shard_map.88 = (bf16[4096,128]{1,0:T(8,128)(2,1)}, bf16[4,512,128]{2,1,0:T(8,128)(2,1)S(1)}, bf16[4,512,128]{2,1,0:T(8,128)(2,1)S(1)}) custom-call(s32[5]{0:T(128)S(1)} %pad_add_fusion.refs_0_, s32[2]{0:T(128)S(1)} %copy-done, s32[16,32]{1,0:T(8,128)S(1)} %bitcast.31, bf16[16,272,128]{2,1,0:T(8,128)(2,1)S(1)} %all-to-all-done.refs_3_, ...), custom_call_target="tpu_custom_call" | custom-call | flops 3221225472 | bytes 8388608 | tf_op jit(solution)/shard_map/pallas_call | solution.py:283
  55.6 0.9 %collective-permute-start.10 = (bf16[4,512,128]{2,1,0:T(8,128)(2,1)S(1)}, bf16[4,512,128]{2,1,0:T(8,128)(2,1)S(1)}, u32[]{:S(2)}, u32[]{:S(2)}) collective-permute-start(bf16[4,512,128]{2,1,0:T(8,128)(2,1)S(1)} %get-tuple-element.27), channel_id=1, source_target_pairs={{0,1},{1,0},{2,3},{3,2},{4,5},{5,4},{6,7},{7,6},{8,9},{9,8},{10,11... | collective-permute-start | bytes 1572872 | tf_op jit(solution)/shard_map/ppermute | solution.py:223
  56.6 0.0 collective-permute-done.8
  56.6 0.0 collective-permute-done.9
  56.6 4.7 %all-to-all-start.1 = ((bf16[16,256,128]{2,1,0:T(8,128)(2,1)}), bf16[16,256,128]{2,1,0:T(8,128)(2,1)S(1)}, u32[]{:S(2)}, u32[]{:S(2)}) async-start(bf16[16,256,128]{2,1,0:T(8,128)(2,1)} %bitcast.10), calls=%async_computation.1 | async-start | bytes 2097152 | tf_op jit(solution)/shard_map/all_to_all | solution.py:219
  61.3 0.0 collective-permute-done.10
  61.3 0.2 fusion.3
  61.4 0.1 collective-permute-start.11
  61.5 4.0 %collective-permute-start.13 = (bf16[512,128]{1,0:T(8,128)(2,1)S(1)}, bf16[512,128]{1,0:T(8,128)(2,1)S(1)}, u32[]{:S(2)}, u32[]{:S(2)}) collective-permute-start(bf16[512,128]{1,0:T(8,128)(2,1)S(1)} %get-tuple-element.31), channel_id=1, source_target_pairs={{0,32},{8,40},{16,48},{24,56},{32,0},{40,8},{48,16},{56,24},{1,33}... | collective-permute-start | bytes 393224 | tf_op jit(solution)/shard_map/ppermute | solution.py:227
  65.6 2.6 %collective-permute-start.12 = (bf16[512,128]{1,0:T(8,128)(2,1)S(1)}, bf16[512,128]{1,0:T(8,128)(2,1)S(1)}, u32[]{:S(2)}, u32[]{:S(2)}) collective-permute-start(bf16[512,128]{1,0:T(8,128)(2,1)S(1)} %get-tuple-element.32), channel_id=1, source_target_pairs={{0,56},{8,0},{16,8},{24,16},{32,24},{40,32},{48,40},{56,48},{1,57}... | collective-permute-start | bytes 393224 | tf_op jit(solution)/shard_map/ppermute | solution.py:227
  68.2 0.0 collective-permute-done.11
  68.2 4.2 %collective-permute-done.13 = bf16[512,128]{1,0:T(8,128)(2,1)S(1)} collective-permute-done((bf16[512,128]{1,0:T(8,128)(2,1)S(1)}, bf16[512,128]{1,0:T(8,128)(2,1)S(1)}, u32[]{:S(2)}, u32[]{:S(2)}) %collective-permute-start.13) | collective-permute-done | bytes 131104 | tf_op jit(solution)/shard_map/ppermute | solution.py:227
  72.4 1.1 %collective-permute-done.12 = bf16[512,128]{1,0:T(8,128)(2,1)S(1)} collective-permute-done((bf16[512,128]{1,0:T(8,128)(2,1)S(1)}, bf16[512,128]{1,0:T(8,128)(2,1)S(1)}, u32[]{:S(2)}, u32[]{:S(2)}) %collective-permute-start.12) | collective-permute-done | bytes 131104 | tf_op jit(solution)/shard_map/ppermute | solution.py:227
  73.5 0.7 fusion.6
  74.2 4.0 %all-to-all-done.1 = bf16[16,256,128]{2,1,0:T(8,128)(2,1)S(1)} async-done(((bf16[16,256,128]{2,1,0:T(8,128)(2,1)}), bf16[16,256,128]{2,1,0:T(8,128)(2,1)S(1)}, u32[]{:S(2)}, u32[]{:S(2)}) %all-to-all-start.1) | async-done | bytes 1048608 | tf_op jit(solution)/shard_map/all_to_all | solution.py:219
  78.2 0.8 reduce_sum.12
  (5 shorter events, 0.1 us)
Async XLA Ops:
  2.9 16.2 %collective-permute-start.2 = (bf16[512,128]{1,0:T(8,128)(2,1)}, bf16[512,128]{1,0:T(8,128)(2,1)S(1)}, u32[]{:S(2)}, u32[]{:S(2)}) collective-permute-start(bf16[512,128]{1,0:T(8,128)(2,1)} %get-tuple-element.17), channel_id=1, source_target_pairs={{0,32},{8,40},{16,48},{24,56},{32,0},{40,8},{48,16},{56,24},{1,33}... | collective-permute-start | bytes 393224 | tf_op jit(solution)/shard_map/ppermute | solution.py:227
  10.7 9.6 %collective-permute-start.1 = (bf16[512,128]{1,0:T(8,128)(2,1)}, bf16[512,128]{1,0:T(8,128)(2,1)S(1)}, u32[]{:S(2)}, u32[]{:S(2)}) collective-permute-start(bf16[512,128]{1,0:T(8,128)(2,1)} %get-tuple-element.17), channel_id=1, source_target_pairs={{0,56},{8,0},{16,8},{24,16},{32,24},{40,32},{48,40},{56,48},{1,57}... | collective-permute-start | bytes 393224 | tf_op jit(solution)/shard_map/ppermute | solution.py:227
  10.7 9.6 %collective-permute-start = (bf16[512,128]{1,0:T(8,128)(2,1)}, bf16[512,128]{1,0:T(8,128)(2,1)S(1)}, u32[]{:S(2)}, u32[]{:S(2)}) collective-permute-start(bf16[512,128]{1,0:T(8,128)(2,1)} %get-tuple-element.17), channel_id=1, source_target_pairs={{0,8},{8,16},{16,24},{24,32},{32,40},{40,48},{48,56},{56,0},{1,9},... | collective-permute-start | bytes 393224 | tf_op jit(solution)/shard_map/ppermute | solution.py:227
  12.1 10.9 %copy-start.2 = (s32[8]{0:T(128)S(1)}, s32[8]{0:T(128)}, u32[]{:S(2)}) copy-start(s32[8]{0:T(128)} %constant.38.clone) | copy-start | bytes 100
  12.1 22.7 %all-to-all-start = ((bf16[16,272,128]{2,1,0:T(8,128)(2,1)}), bf16[16,272,128]{2,1,0:T(8,128)(2,1)S(1)}, u32[]{:S(2)}, u32[]{:S(2)}) async-start(bf16[16,272,128]{2,1,0:T(8,128)(2,1)} %get-tuple-element.16), calls=%async_computation | async-start | bytes 2228224 | tf_op jit(solution)/shard_map/all_to_all | solution.py:219
  19.0 15.8 %copy-start = (s32[2]{0:T(128)S(1)}, s32[2]{0:T(128)}, u32[]{:S(2)}) copy-start(s32[2]{0:T(128)} %refs_1_.3) | copy-start | bytes 28
  20.3 7.6 %collective-permute-start.4 = (bf16[2,512,128]{2,1,0:T(8,128)(2,1)S(1)}, bf16[2,512,128]{2,1,0:T(8,128)(2,1)S(1)}, u32[]{:S(2)}, u32[]{:S(2)}) collective-permute-start(bf16[2,512,128]{2,1,0:T(8,128)(2,1)S(1)} %get-tuple-element.36), channel_id=1, source_target_pairs={{0,8},{8,16},{16,24},{24,32},{32,40},{40,48},{48,56},{56,0},{1,9},... | collective-permute-start | bytes 786440 | tf_op jit(solution)/shard_map/ppermute | solution.py:227
  21.3 7.1 %collective-permute-start.5 = (bf16[2,512,128]{2,1,0:T(8,128)(2,1)S(1)}, bf16[2,512,128]{2,1,0:T(8,128)(2,1)S(1)}, u32[]{:S(2)}, u32[]{:S(2)}) collective-permute-start(bf16[2,512,128]{2,1,0:T(8,128)(2,1)S(1)} %get-tuple-element.35), channel_id=1, source_target_pairs={{0,56},{8,0},{16,8},{24,16},{32,24},{40,32},{48,40},{56,48},{1,57}... | collective-permute-start | bytes 786440 | tf_op jit(solution)/shard_map/ppermute | solution.py:227
  28.4 6.4 %collective-permute-start.6 = (bf16[4,512,128]{2,1,0:T(8,128)(2,1)S(1)}, bf16[4,512,128]{2,1,0:T(8,128)(2,1)S(1)}, u32[]{:S(2)}, u32[]{:S(2)}) collective-permute-start(bf16[4,512,128]{2,1,0:T(8,128)(2,1)S(1)} %constant_dynamic-update-slice_fusion.refs_4_), channel_id=1, source_target_pairs={{0,1},{1,0},{2,3},{3,2},{4,5},{5,4},{6,7},{7,6},{8,9},{9,8},{10,11... | collective-permute-start | bytes 1572872 | tf_op jit(solution)/shard_map/ppermute | solution.py:223
  34.8 9.3 %copy-start.1 = (bf16[512,128]{1,0:T(8,128)(2,1)S(1)}, bf16[512,128]{1,0:T(8,128)(2,1)}, u32[]{:S(2)}) copy-start(bf16[512,128]{1,0:T(8,128)(2,1)} %get-tuple-element.17) | copy-start | bytes 393220
  40.8 4.9 %collective-permute-start.7 = (bf16[4,512,128]{2,1,0:T(8,128)(2,1)S(1)}, bf16[4,512,128]{2,1,0:T(8,128)(2,1)S(1)}, u32[]{:S(2)}, u32[]{:S(2)}) collective-permute-start(bf16[4,512,128]{2,1,0:T(8,128)(2,1)S(1)} %get-tuple-element.20), channel_id=1, source_target_pairs={{0,1},{1,0},{2,3},{3,2},{4,5},{5,4},{6,7},{7,6},{8,9},{9,8},{10,11... | collective-permute-start | bytes 1572872 | tf_op jit(solution)/shard_map/ppermute | solution.py:223
  44.2 4.4 %collective-permute-start.3 = (bf16[4,512,128]{2,1,0:T(8,128)(2,1)S(1)}, bf16[4,512,128]{2,1,0:T(8,128)(2,1)S(1)}, u32[]{:S(2)}, u32[]{:S(2)}) collective-permute-start(bf16[4,512,128]{2,1,0:T(8,128)(2,1)S(1)} %pad_maximum_fusion.refs_4_), channel_id=1, source_target_pairs={{0,1},{1,0},{2,3},{3,2},{4,5},{5,4},{6,7},{7,6},{8,9},{9,8},{10,11... | collective-permute-start | bytes 1572872 | tf_op jit(solution)/shard_map/ppermute | solution.py:223
  45.8 10.8 %collective-permute-start.8 = (bf16[2,512,128]{2,1,0:T(8,128)(2,1)S(1)}, bf16[2,512,128]{2,1,0:T(8,128)(2,1)S(1)}, u32[]{:S(2)}, u32[]{:S(2)}) collective-permute-start(bf16[2,512,128]{2,1,0:T(8,128)(2,1)S(1)} %get-tuple-element.23), channel_id=1, source_target_pairs={{0,8},{8,16},{16,24},{24,32},{32,40},{40,48},{48,56},{56,0},{1,9},... | collective-permute-start | bytes 786440 | tf_op jit(solution)/shard_map/ppermute | solution.py:227
  46.6 9.9 %collective-permute-start.9 = (bf16[2,512,128]{2,1,0:T(8,128)(2,1)S(1)}, bf16[2,512,128]{2,1,0:T(8,128)(2,1)S(1)}, u32[]{:S(2)}, u32[]{:S(2)}) collective-permute-start(bf16[2,512,128]{2,1,0:T(8,128)(2,1)S(1)} %get-tuple-element.24), channel_id=1, source_target_pairs={{0,56},{8,0},{16,8},{24,16},{32,24},{40,32},{48,40},{56,48},{1,57}... | collective-permute-start | bytes 786440 | tf_op jit(solution)/shard_map/ppermute | solution.py:227
  55.6 5.6 %collective-permute-start.10 = (bf16[4,512,128]{2,1,0:T(8,128)(2,1)S(1)}, bf16[4,512,128]{2,1,0:T(8,128)(2,1)S(1)}, u32[]{:S(2)}, u32[]{:S(2)}) collective-permute-start(bf16[4,512,128]{2,1,0:T(8,128)(2,1)S(1)} %get-tuple-element.27), channel_id=1, source_target_pairs={{0,1},{1,0},{2,3},{3,2},{4,5},{5,4},{6,7},{7,6},{8,9},{9,8},{10,11... | collective-permute-start | bytes 1572872 | tf_op jit(solution)/shard_map/ppermute | solution.py:223
  56.6 21.6 %all-to-all-start.1 = ((bf16[16,256,128]{2,1,0:T(8,128)(2,1)}), bf16[16,256,128]{2,1,0:T(8,128)(2,1)S(1)}, u32[]{:S(2)}, u32[]{:S(2)}) async-start(bf16[16,256,128]{2,1,0:T(8,128)(2,1)} %bitcast.10), calls=%async_computation.1 | async-start | bytes 2097152 | tf_op jit(solution)/shard_map/all_to_all | solution.py:219
  61.4 6.7 %collective-permute-start.11 = (bf16[512,128]{1,0:T(8,128)(2,1)S(1)}, bf16[512,128]{1,0:T(8,128)(2,1)S(1)}, u32[]{:S(2)}, u32[]{:S(2)}) collective-permute-start(bf16[512,128]{1,0:T(8,128)(2,1)S(1)} %get-tuple-element.30), channel_id=1, source_target_pairs={{0,8},{8,16},{16,24},{24,32},{32,40},{40,48},{48,56},{56,0},{1,9},... | collective-permute-start | bytes 393224 | tf_op jit(solution)/shard_map/ppermute | solution.py:227
  61.5 10.8 %collective-permute-start.13 = (bf16[512,128]{1,0:T(8,128)(2,1)S(1)}, bf16[512,128]{1,0:T(8,128)(2,1)S(1)}, u32[]{:S(2)}, u32[]{:S(2)}) collective-permute-start(bf16[512,128]{1,0:T(8,128)(2,1)S(1)} %get-tuple-element.31), channel_id=1, source_target_pairs={{0,32},{8,40},{16,48},{24,56},{32,0},{40,8},{48,16},{56,24},{1,33}... | collective-permute-start | bytes 393224 | tf_op jit(solution)/shard_map/ppermute | solution.py:227
  65.6 7.9 %collective-permute-start.12 = (bf16[512,128]{1,0:T(8,128)(2,1)S(1)}, bf16[512,128]{1,0:T(8,128)(2,1)S(1)}, u32[]{:S(2)}, u32[]{:S(2)}) collective-permute-start(bf16[512,128]{1,0:T(8,128)(2,1)S(1)} %get-tuple-element.32), channel_id=1, source_target_pairs={{0,56},{8,0},{16,8},{24,16},{32,24},{40,32},{48,40},{56,48},{1,57}... | collective-permute-start | bytes 393224 | tf_op jit(solution)/shard_map/ppermute | solution.py:227

commit v8 on v7

--- a/solution.py
+++ b/solution.py
@@ -30,6 +30,7 @@
 SLOTS = PLANE * CAP
 LIST = SLOTS + GROUP
 PART = NZ // 2
+COMBINE_FLOPS = 40 * 10**9
 STEPS = (0, -1, 1, 4, -2, 3, 2, -3)
 
 
@@ -238,10 +239,25 @@
     return mine.astype(jnp.float32) + other.astype(jnp.float32)
 
 
+def combine_kernel(mine_ref, other_ref, below_ref, above_ref, up_ref, down_ref, over_ref):
+    below, above = below_ref[...].astype(jnp.float32), above_ref[...].astype(jnp.float32)
+    up_ref[...] = (add(mine_ref[2], other_ref[2]) + below[0]).astype(jnp.bfloat16)
+    down_ref[...] = (add(mine_ref[1], other_ref[1]) + above[0]).astype(jnp.bfloat16)
+    over_ref[...] = (add(mine_ref[3], other_ref[3]) + below[1] + above[1]).astype(jnp.bfloat16)
+
+
 def reduce_column(mine, other, from_below, from_above):
-    up = (add(mine[2], other[2]) + from_below[0].astype(jnp.float32)).astype(jnp.bfloat16)
-    down = (add(mine[1], other[1]) + from_above[0].astype(jnp.float32)).astype(jnp.bfloat16)
-    over = (add(mine[3], other[3]) + add(from_below[1], from_above[1])).astype(jnp.bfloat16)
+    vmem = pl.BlockSpec(memory_space=pltpu.VMEM)
+    up, down, over = pl.pallas_call(
+        combine_kernel,
+        out_shape=(jax.ShapeDtypeStruct((HALF, W), jnp.bfloat16),) * 3,
+        in_specs=[vmem] * 4,
+        out_specs=(vmem,) * 3,
+        compiler_params=pltpu.CompilerParams(vmem_limit_bytes=6 << 20),
+        cost_estimate=pl.CostEstimate(
+            flops=COMBINE_FLOPS, bytes_accessed=4 << 20, transcendentals=0
+        ),
+    )(mine, other, from_below, from_above)
     total = add(mine[0], other[0])
     for part in (move(up, 1), move(down, -1), move(over, 4)):
         total = total + part.astype(jnp.float32)
@@ -261,7 +277,7 @@
     smem = pl.BlockSpec(memory_space=pltpu.SMEM)
     vmem = pl.BlockSpec(memory_space=pltpu.VMEM)
     last = carried is not None
-    widths = (2,) if last else (4, 2)
+    widths = (4, 2)
     most = max(widths)
     pages = jax.ShapeDtypeStruct((PART, HALF, W), jnp.bfloat16)
     sums = jax.ShapeDtypeStruct((PLANE * ROWS, W), jnp.bfloat16 if last else jnp.float32)
@@ -324,15 +340,11 @@
     far_other = swap_cores(far_other)
     to_above = add(far_mine[2:4], far_other[2:4]).astype(jnp.bfloat16)
     to_below = add(far_mine[0:2], far_other[0:2]).astype(jnp.bfloat16)
-    sums, to_above, to_below = lax.optimization_barrier((sums, to_above, to_below))
     from_below, from_above = move(to_above, 1), move(to_below, -1)
     query_part, near_mine, near_other = score(
         near_column, hot_pages, table, got, near, other_near, sums
     )
     near_other = swap_cores(near_other)
-    query_part, from_below, from_above = lax.optimization_barrier(
-        (query_part, from_below, from_above)
-    )
     query_back = exchange(query_part.reshape(PLANE, ROWS, W), ("x", "y"))
     page_grad = reduce_column(near_mine, near_other, from_below, from_above)
     query_grad = jnp.sum(query_back.astype(jnp.float32), axis=0).astype(jnp.bfloat16)

time: 79.3 us -> 78.4 us (0.989)
  Pallas kernels: 15.2 us -> 13.8 us
  starting transfers between devices: 39.5 us -> 38.3 us
  other arithmetic: 2.11 us -> 3.18 us
  waiting for transfers between devices: 21.3 us -> 22.3 us
    ppermute x10, waiting for transfers between devices: 11.8 us -> 17.2 us  [move(): return lax.ppermute(array, 'z', [(i, (i + step) % NZ) for i in range(NZ)])]
    all_to_all x2, waiting for transfers between devices: 8.21 us -> 5.17 us  [exchange(): return lax.all_to_all(array, axes, split_axis=0, concat_axis=0, tiled=True)]
    ppermute x10, starting transfers between devices: 21.5 us -> 19.4 us  [move(): return lax.ppermute(array, 'z', [(i, (i + step) % NZ) for i in range(NZ)])]
    pallas_call x2, Pallas kernels: 13 us -> 11.4 us  [score(): pl.pallas_call(functools.partial(second_kernel if last else first_kernel,...]
    ppermute x4, starting transfers between devices: 6.44 us -> 7.71 us  [swap_cores(): return lax.ppermute(array, 'core', [(0, 1), (1, 0)])]
    ppermute x4, waiting for transfers between devices: 1.28 us -> 0.01 us  [swap_cores(): return lax.ppermute(array, 'core', [(0, 1), (1, 0)])]
    reduce_sum x1, other arithmetic: 0.77 us -> 2.01 us  [shards(): jnp.sum(query_back.astype(jnp.float32), axis=0).astype(jnp.bfloat16)]
  transfers between devices with their start and end apart: 16 -> 16, of which waited for: 8 -> 7; matrix products, arithmetic and copies ran while one was open for 2% -> 2% of each run, Pallas kernels for 9% -> 15%
where the time goes in v8:
time: 78.4 us; the launch traced here: 78.6 us
  starting transfers between devices  38.3 us (49%)
  waiting for transfers between devices  22.3 us (28%)
  Pallas kernels  13.8 us (18%)
  other arithmetic  3.18 us (4%)
  between operations  0.82 us (1%)
    ppermute x10, starting transfers between devices, move(): return lax.ppermute(array, 'z', [(i, (i + step) % NZ) for i in range(NZ)])  19.4 us
    ppermute x10, waiting for transfers between devices, move(): return lax.ppermute(array, 'z', [(i, (i + step) % NZ) for i in range(NZ)])  17.2 us
    pallas_call x2, Pallas kernels, score(): pl.pallas_call(functools.partial(second_kernel if last else first_kernel,...  11.4 us
    all_to_all x2, starting transfers between devices, exchange(): return lax.all_to_all(array, axes, split_axis=0, concat_axis=0, tiled=True)  11.2 us
    ppermute x4, starting transfers between devices, swap_cores(): return lax.ppermute(array, 'core', [(0, 1), (1, 0)])  7.71 us
    all_to_all x2, waiting for transfers between devices, exchange(): return lax.all_to_all(array, axes, split_axis=0, concat_axis=0, tiled=True)  5.17 us
    pallas_call x1, Pallas kernels, shards(): pl.pallas_call(pack_kernel, out_shape=(jax.ShapeDtypeStruct((PLANE, SEND_...  2.21 us
    reduce_sum x1, other arithmetic, shards(): jnp.sum(query_back.astype(jnp.float32), axis=0).astype(jnp.bfloat16)  2.01 us
  transfers between devices with their start and end apart: 16, of which 7 were waited for; matrix products, arithmetic and copies ran while one was open for 2% of the time, Pallas kernels for 15%

profile of v8, /device:TPU:1, one launch (start us, length us, event | category | flops | bytes accessed | tf_op | source)
XLA Modules:
  0.0 78.6 jit_solution(16944601252026067967)
XLA Ops:
  0.6 2.2 %shard_map.86 = (bf16[16,272,128]{2,1,0:T(8,128)(2,1)}, bf16[512,128]{1,0:T(8,128)(2,1)}) custom-call(s32[64]{0:T(128)} %bitcast.36, s32[64]{0:T(128)} %query_ref.1, s32[64]{0:T(128)} %label_ref.1, s32[1]{0:T(128)} %bitcast.2.core_ref, bf16[256,128]{1,0:T(8,128)(2,1)} %bitcast.34, bf16[1024,128]{1,0:T(8,128)(2,1)} %bitcast.32), custom_call_target="tpu_custom_call" | custom-call | tf_op jit(solution)/shard_map/pallas_call | solution.py:318
  2.9 2.5 %collective-permute-start = (bf16[512,128]{1,0:T(8,128)(2,1)}, bf16[512,128]{1,0:T(8,128)(2,1)S(1)}, u32[]{:S(2)}, u32[]{:S(2)}) collective-permute-start(bf16[512,128]{1,0:T(8,128)(2,1)} %get-tuple-element.14), channel_id=1, source_target_pairs={{0,8},{8,16},{16,24},{24,32},{32,40},{40,48},{48,56},{56,0},{1,9},... | collective-permute-start | bytes 393224 | tf_op jit(solution)/shard_map/ppermute | solution.py:228
  5.4 4.0 %collective-permute-start.1 = (bf16[512,128]{1,0:T(8,128)(2,1)}, bf16[512,128]{1,0:T(8,128)(2,1)S(1)}, u32[]{:S(2)}, u32[]{:S(2)}) collective-permute-start(bf16[512,128]{1,0:T(8,128)(2,1)} %get-tuple-element.14), channel_id=1, source_target_pairs={{0,56},{8,0},{16,8},{24,16},{32,24},{40,32},{48,40},{56,48},{1,57}... | collective-permute-start | bytes 393224 | tf_op jit(solution)/shard_map/ppermute | solution.py:228
  9.4 3.9 %collective-permute-start.2 = (bf16[512,128]{1,0:T(8,128)(2,1)}, bf16[512,128]{1,0:T(8,128)(2,1)S(1)}, u32[]{:S(2)}, u32[]{:S(2)}) collective-permute-start(bf16[512,128]{1,0:T(8,128)(2,1)} %get-tuple-element.14), channel_id=1, source_target_pairs={{0,32},{8,40},{16,48},{24,56},{32,0},{40,8},{48,16},{56,24},{1,33}... | collective-permute-start | bytes 393224 | tf_op jit(solution)/shard_map/ppermute | solution.py:228
  13.3 0.0 copy-start.2
  13.3 6.9 %all-to-all-start = ((bf16[16,272,128]{2,1,0:T(8,128)(2,1)}), bf16[16,272,128]{2,1,0:T(8,128)(2,1)S(1)}, u32[]{:S(2)}, u32[]{:S(2)}) async-start(bf16[16,272,128]{2,1,0:T(8,128)(2,1)} %get-tuple-element.13), calls=%async_computation | async-start | bytes 2228224 | tf_op jit(solution)/shard_map/all_to_all | solution.py:220
  20.2 0.0 copy-start.1
  20.3 0.0 collective-permute-done
  20.3 0.0 collective-permute-done.1
  20.3 0.0 collective-permute-done.2
  20.3 0.0 copy-start
  20.3 0.1 collective-permute-start.4
  20.4 2.7 %collective-permute-start.5 = (bf16[2,512,128]{2,1,0:T(8,128)(2,1)S(1)}, bf16[2,512,128]{2,1,0:T(8,128)(2,1)S(1)}, u32[]{:S(2)}, u32[]{:S(2)}) collective-permute-start(bf16[2,512,128]{2,1,0:T(8,128)(2,1)S(1)} %get-tuple-element.26), channel_id=1, source_target_pairs={{0,56},{8,0},{16,8},{24,16},{32,24},{40,32},{48,40},{56,48},{1,57}... | collective-permute-start | bytes 786440 | tf_op jit(solution)/shard_map/ppermute | solution.py:228
  23.1 0.0 copy-done.2
  23.1 4.4 %collective-permute-done.4 = bf16[2,512,128]{2,1,0:T(8,128)(2,1)S(1)} collective-permute-done((bf16[2,512,128]{2,1,0:T(8,128)(2,1)S(1)}, bf16[2,512,128]{2,1,0:T(8,128)(2,1)S(1)}, u32[]{:S(2)}, u32[]{:S(2)}) %collective-permute-start.4) | collective-permute-done | bytes 262176 | tf_op jit(solution)/shard_map/ppermute | solution.py:228
  27.6 0.0 collective-permute-done.5
  27.6 2.9 %collective-permute-start.6 = (bf16[4,512,128]{2,1,0:T(8,128)(2,1)S(1)}, bf16[4,512,128]{2,1,0:T(8,128)(2,1)S(1)}, u32[]{:S(2)}, u32[]{:S(2)}) collective-permute-start(bf16[4,512,128]{2,1,0:T(8,128)(2,1)S(1)} %constant_dynamic-update-slice_fusion.refs_4_), channel_id=1, source_target_pairs={{0,1},{1,0},{2,3},{3,2},{4,5},{5,4},{6,7},{7,6},{8,9},{9,8},{10,11... | collective-permute-start | bytes 1572872 | tf_op jit(solution)/shard_map/ppermute | solution.py:224
  30.5 0.1 fusion.5
  30.6 0.1 pad_add_fusion.1.refs_0_
  30.7 0.0 copy-done.1
  30.7 0.1 pad_maximum_fusion.refs_4_
  30.7 0.1 collective-permute-start.3
  30.9 5.2 %all-to-all-done.refs_3_ = bf16[16,272,128]{2,1,0:T(8,128)(2,1)S(1)} async-done(((bf16[16,272,128]{2,1,0:T(8,128)(2,1)}), bf16[16,272,128]{2,1,0:T(8,128)(2,1)S(1)}, u32[]{:S(2)}, u32[]{:S(2)}) %all-to-all-start) | async-done | bytes 1114144 | tf_op jit(solution)/shard_map/all_to_all | solution.py:220
  36.0 0.0 collective-permute-done.6.refs_5_
  36.0 0.0 copy-done
  36.0 5.8 %shard_map.87 = (f32[4096,128]{1,0:T(8,128)S(1)}, bf16[4,512,128]{2,1,0:T(8,128)(2,1)S(1)}, bf16[4,512,128]{2,1,0:T(8,128)(2,1)S(1)}) custom-call(s32[5]{0:T(128)S(1)} %pad_add_fusion.1.refs_0_, s32[2]{0:T(128)S(1)} %copy-done, s32[16,32]{1,0:T(8,128)S(1)} %bitcast.24, bf16[16,272,128]{2,1,0:T(8,128)(2,1)S(1)} %all-to-all-done.refs_3_, ...), custom_call_target="tpu_custom_call" | custom-call | flops 3221225472 | bytes 8388608 | tf_op jit(solution)/shard_map/pallas_call | solution.py:299
  41.9 3.3 %collective-permute-start.8 = (bf16[4,512,128]{2,1,0:T(8,128)(2,1)S(1)}, bf16[4,512,128]{2,1,0:T(8,128)(2,1)S(1)}, u32[]{:S(2)}, u32[]{:S(2)}) collective-permute-start(bf16[4,512,128]{2,1,0:T(8,128)(2,1)S(1)} %get-tuple-element.20), channel_id=1, source_target_pairs={{0,1},{1,0},{2,3},{3,2},{4,5},{5,4},{6,7},{7,6},{8,9},{9,8},{10,11... | collective-permute-start | bytes 1572872 | tf_op jit(solution)/shard_map/ppermute | solution.py:224
  45.2 0.1 pad_add_fusion.refs_0_
  45.3 0.0 collective-permute-done.3.refs_5_
  45.3 5.6 %shard_map.88 = (bf16[4096,128]{1,0:T(8,128)(2,1)}, bf16[4,512,128]{2,1,0:T(8,128)(2,1)S(1)}, bf16[4,512,128]{2,1,0:T(8,128)(2,1)S(1)}) custom-call(s32[5]{0:T(128)S(1)} %pad_add_fusion.refs_0_, s32[2]{0:T(128)S(1)} %copy-done, s32[16,32]{1,0:T(8,128)S(1)} %bitcast.25, bf16[16,272,128]{2,1,0:T(8,128)(2,1)S(1)} %all-to-all-done.refs_3_, ...), custom_call_target="tpu_custom_call" | custom-call | flops 3221225472 | bytes 8388608 | tf_op jit(solution)/shard_map/pallas_call | solution.py:299
  50.9 1.4 %collective-permute-start.7 = (bf16[4,512,128]{2,1,0:T(8,128)(2,1)S(1)}, bf16[4,512,128]{2,1,0:T(8,128)(2,1)S(1)}, u32[]{:S(2)}, u32[]{:S(2)}) collective-permute-start(bf16[4,512,128]{2,1,0:T(8,128)(2,1)S(1)} %get-tuple-element.18), channel_id=1, source_target_pairs={{0,1},{1,0},{2,3},{3,2},{4,5},{5,4},{6,7},{7,6},{8,9},{9,8},{10,11... | collective-permute-start | bytes 1572872 | tf_op jit(solution)/shard_map/ppermute | solution.py:224
  52.3 0.0 collective-permute-done.8
  52.3 0.1 add_convert_fusion
  52.5 0.1 collective-permute-start.10
  52.6 1.5 %collective-permute-start.9 = (bf16[2,512,128]{2,1,0:T(8,128)(2,1)S(1)}, bf16[2,512,128]{2,1,0:T(8,128)(2,1)S(1)}, u32[]{:S(2)}, u32[]{:S(2)}) collective-permute-start(bf16[2,512,128]{2,1,0:T(8,128)(2,1)S(1)} %get-tuple-element.25), channel_id=1, source_target_pairs={{0,8},{8,16},{16,24},{24,32},{32,40},{40,48},{48,56},{56,0},{1,9},... | collective-permute-start | bytes 786440 | tf_op jit(solution)/shard_map/ppermute | solution.py:228
  54.0 4.3 %all-to-all-start.1 = ((bf16[16,256,128]{2,1,0:T(8,128)(2,1)}), bf16[16,256,128]{2,1,0:T(8,128)(2,1)}, u32[]{:S(2)}, u32[]{:S(2)}) async-start(bf16[16,256,128]{2,1,0:T(8,128)(2,1)} %bitcast.10), calls=%async_computation.1 | async-start | bytes 2097152 | tf_op jit(solution)/shard_map/all_to_all | solution.py:220
  58.3 0.0 collective-permute-done.7.other_ref
  58.4 2.1 %collective-permute-done.10.above_ref = bf16[2,512,128]{2,1,0:T(8,128)(2,1)S(1)} collective-permute-done((bf16[2,512,128]{2,1,0:T(8,128)(2,1)S(1)}, bf16[2,512,128]{2,1,0:T(8,128)(2,1)S(1)}, u32[]{:S(2)}, u32[]{:S(2)}) %collective-permute-start.10) | collective-permute-done | bytes 262176 | tf_op jit(solution)/shard_map/ppermute | solution.py:228
  60.5 1.3 %collective-permute-done.9.below_ref = bf16[2,512,128]{2,1,0:T(8,128)(2,1)S(1)} collective-permute-done((bf16[2,512,128]{2,1,0:T(8,128)(2,1)S(1)}, bf16[2,512,128]{2,1,0:T(8,128)(2,1)S(1)}, u32[]{:S(2)}, u32[]{:S(2)}) %collective-permute-start.9) | collective-permute-done | bytes 262176 | tf_op jit(solution)/shard_map/ppermute | solution.py:228
  61.8 0.2 shard_map.89
  61.9 0.1 collective-permute-start.11
  62.0 2.7 %collective-permute-start.12 = (bf16[512,128]{1,0:T(8,128)(2,1)S(1)}, bf16[512,128]{1,0:T(8,128)(2,1)S(1)}, u32[]{:S(2)}, u32[]{:S(2)}) collective-permute-start(bf16[512,128]{1,0:T(8,128)(2,1)S(1)} %get-tuple-element.22), channel_id=1, source_target_pairs={{0,56},{8,0},{16,8},{24,16},{32,24},{40,32},{48,40},{56,48},{1,57}... | collective-permute-start | bytes 393224 | tf_op jit(solution)/shard_map/ppermute | solution.py:228
  64.7 1.9 %collective-permute-start.13 = (bf16[512,128]{1,0:T(8,128)(2,1)S(1)}, bf16[512,128]{1,0:T(8,128)(2,1)S(1)}, u32[]{:S(2)}, u32[]{:S(2)}) collective-permute-start(bf16[512,128]{1,0:T(8,128)(2,1)S(1)} %get-tuple-element.23), channel_id=1, source_target_pairs={{0,32},{8,40},{16,48},{24,56},{32,0},{40,8},{48,16},{56,24},{1,33}... | collective-permute-start | bytes 393224 | tf_op jit(solution)/shard_map/ppermute | solution.py:228
  66.6 1.0 %collective-permute-done.11 = bf16[512,128]{1,0:T(8,128)(2,1)S(1)} collective-permute-done((bf16[512,128]{1,0:T(8,128)(2,1)S(1)}, bf16[512,128]{1,0:T(8,128)(2,1)S(1)}, u32[]{:S(2)}, u32[]{:S(2)}) %collective-permute-start.11) | collective-permute-done | bytes 131104 | tf_op jit(solution)/shard_map/ppermute | solution.py:228
  67.6 0.1 collective-permute-done.12
  67.7 8.1 %collective-permute-done.13 = bf16[512,128]{1,0:T(8,128)(2,1)S(1)} collective-permute-done((bf16[512,128]{1,0:T(8,128)(2,1)S(1)}, bf16[512,128]{1,0:T(8,128)(2,1)S(1)}, u32[]{:S(2)}, u32[]{:S(2)}) %collective-permute-start.13) | collective-permute-done | bytes 131104 | tf_op jit(solution)/shard_map/ppermute | solution.py:228
  75.8 0.7 fusion.3
  76.6 0.0 all-to-all-done.1
  76.6 2.0 %reduce_sum.12 = bf16[256,128]{1,0:T(8,128)(2,1)} reduce(bf16[16,256,128]{2,1,0:T(8,128)(2,1)} %all-to-all-done.1, bf16[]{:T(256)} %constant.37.clone.1), dimensions={0}, to_apply=%region_0.1 | reduce | flops 491520 | bytes 1114114 | tf_op jit(solution)/shard_map/reduce_sum | solution.py:350
  (5 shorter events, 0.1 us)
Async XLA Ops:
  2.9 17.4 %collective-permute-start = (bf16[512,128]{1,0:T(8,128)(2,1)}, bf16[512,128]{1,0:T(8,128)(2,1)S(1)}, u32[]{:S(2)}, u32[]{:S(2)}) collective-permute-start(bf16[512,128]{1,0:T(8,128)(2,1)} %get-tuple-element.14), channel_id=1, source_target_pairs={{0,8},{8,16},{16,24},{24,32},{32,40},{40,48},{48,56},{56,0},{1,9},... | collective-permute-start | bytes 393224 | tf_op jit(solution)/shard_map/ppermute | solution.py:228
  5.4 14.9 %collective-permute-start.1 = (bf16[512,128]{1,0:T(8,128)(2,1)}, bf16[512,128]{1,0:T(8,128)(2,1)S(1)}, u32[]{:S(2)}, u32[]{:S(2)}) collective-permute-start(bf16[512,128]{1,0:T(8,128)(2,1)} %get-tuple-element.14), channel_id=1, source_target_pairs={{0,56},{8,0},{16,8},{24,16},{32,24},{40,32},{48,40},{56,48},{1,57}... | collective-permute-start | bytes 393224 | tf_op jit(solution)/shard_map/ppermute | solution.py:228
  9.4 10.9 %collective-permute-start.2 = (bf16[512,128]{1,0:T(8,128)(2,1)}, bf16[512,128]{1,0:T(8,128)(2,1)S(1)}, u32[]{:S(2)}, u32[]{:S(2)}) collective-permute-start(bf16[512,128]{1,0:T(8,128)(2,1)} %get-tuple-element.14), channel_id=1, source_target_pairs={{0,32},{8,40},{16,48},{24,56},{32,0},{40,8},{48,16},{56,24},{1,33}... | collective-permute-start | bytes 393224 | tf_op jit(solution)/shard_map/ppermute | solution.py:228
  13.3 9.8 %copy-start.2 = (s32[8]{0:T(128)S(1)}, s32[8]{0:T(128)}, u32[]{:S(2)}) copy-start(s32[8]{0:T(128)} %constant.38.clone) | copy-start | bytes 100
  13.3 22.7 %all-to-all-start = ((bf16[16,272,128]{2,1,0:T(8,128)(2,1)}), bf16[16,272,128]{2,1,0:T(8,128)(2,1)S(1)}, u32[]{:S(2)}, u32[]{:S(2)}) async-start(bf16[16,272,128]{2,1,0:T(8,128)(2,1)} %get-tuple-element.13), calls=%async_computation | async-start | bytes 2228224 | tf_op jit(solution)/shard_map/all_to_all | solution.py:220
  20.2 10.4 %copy-start.1 = (bf16[512,128]{1,0:T(8,128)(2,1)S(1)}, bf16[512,128]{1,0:T(8,128)(2,1)}, u32[]{:S(2)}) copy-start(bf16[512,128]{1,0:T(8,128)(2,1)} %get-tuple-element.14) | copy-start | bytes 393220
  20.3 15.7 %copy-start = (s32[2]{0:T(128)S(1)}, s32[2]{0:T(128)}, u32[]{:S(2)}) copy-start(s32[2]{0:T(128)} %refs_1_.3) | copy-start | bytes 28
  20.3 7.2 %collective-permute-start.4 = (bf16[2,512,128]{2,1,0:T(8,128)(2,1)S(1)}, bf16[2,512,128]{2,1,0:T(8,128)(2,1)S(1)}, u32[]{:S(2)}, u32[]{:S(2)}) collective-permute-start(bf16[2,512,128]{2,1,0:T(8,128)(2,1)S(1)} %get-tuple-element.27), channel_id=1, source_target_pairs={{0,8},{8,16},{16,24},{24,32},{32,40},{40,48},{48,56},{56,0},{1,9},... | collective-permute-start | bytes 786440 | tf_op jit(solution)/shard_map/ppermute | solution.py:228
  20.4 7.1 %collective-permute-start.5 = (bf16[2,512,128]{2,1,0:T(8,128)(2,1)S(1)}, bf16[2,512,128]{2,1,0:T(8,128)(2,1)S(1)}, u32[]{:S(2)}, u32[]{:S(2)}) collective-permute-start(bf16[2,512,128]{2,1,0:T(8,128)(2,1)S(1)} %get-tuple-element.26), channel_id=1, source_target_pairs={{0,56},{8,0},{16,8},{24,16},{32,24},{40,32},{48,40},{56,48},{1,57}... | collective-permute-start | bytes 786440 | tf_op jit(solution)/shard_map/ppermute | solution.py:228
  27.6 8.4 %collective-permute-start.6 = (bf16[4,512,128]{2,1,0:T(8,128)(2,1)S(1)}, bf16[4,512,128]{2,1,0:T(8,128)(2,1)S(1)}, u32[]{:S(2)}, u32[]{:S(2)}) collective-permute-start(bf16[4,512,128]{2,1,0:T(8,128)(2,1)S(1)} %constant_dynamic-update-slice_fusion.refs_4_), channel_id=1, source_target_pairs={{0,1},{1,0},{2,3},{3,2},{4,5},{5,4},{6,7},{7,6},{8,9},{9,8},{10,11... | collective-permute-start | bytes 1572872 | tf_op jit(solution)/shard_map/ppermute | solution.py:224
  30.7 14.6 %collective-permute-start.3 = (bf16[4,512,128]{2,1,0:T(8,128)(2,1)S(1)}, bf16[4,512,128]{2,1,0:T(8,128)(2,1)S(1)}, u32[]{:S(2)}, u32[]{:S(2)}) collective-permute-start(bf16[4,512,128]{2,1,0:T(8,128)(2,1)S(1)} %pad_maximum_fusion.refs_4_), channel_id=1, source_target_pairs={{0,1},{1,0},{2,3},{3,2},{4,5},{5,4},{6,7},{7,6},{8,9},{9,8},{10,11... | collective-permute-start | bytes 1572872 | tf_op jit(solution)/shard_map/ppermute | solution.py:224
  41.9 10.4 %collective-permute-start.8 = (bf16[4,512,128]{2,1,0:T(8,128)(2,1)S(1)}, bf16[4,512,128]{2,1,0:T(8,128)(2,1)S(1)}, u32[]{:S(2)}, u32[]{:S(2)}) collective-permute-start(bf16[4,512,128]{2,1,0:T(8,128)(2,1)S(1)} %get-tuple-element.20), channel_id=1, source_target_pairs={{0,1},{1,0},{2,3},{3,2},{4,5},{5,4},{6,7},{7,6},{8,9},{9,8},{10,11... | collective-permute-start | bytes 1572872 | tf_op jit(solution)/shard_map/ppermute | solution.py:224
  50.9 7.4 %collective-permute-start.7 = (bf16[4,512,128]{2,1,0:T(8,128)(2,1)S(1)}, bf16[4,512,128]{2,1,0:T(8,128)(2,1)S(1)}, u32[]{:S(2)}, u32[]{:S(2)}) collective-permute-start(bf16[4,512,128]{2,1,0:T(8,128)(2,1)S(1)} %get-tuple-element.18), channel_id=1, source_target_pairs={{0,1},{1,0},{2,3},{3,2},{4,5},{5,4},{6,7},{7,6},{8,9},{9,8},{10,11... | collective-permute-start | bytes 1572872 | tf_op jit(solution)/shard_map/ppermute | solution.py:224
  52.5 8.0 %collective-permute-start.10 = (bf16[2,512,128]{2,1,0:T(8,128)(2,1)S(1)}, bf16[2,512,128]{2,1,0:T(8,128)(2,1)S(1)}, u32[]{:S(2)}, u32[]{:S(2)}) collective-permute-start(bf16[2,512,128]{2,1,0:T(8,128)(2,1)S(1)} %get-tuple-element.24), channel_id=1, source_target_pairs={{0,56},{8,0},{16,8},{24,16},{32,24},{40,32},{48,40},{56,48},{1,57}... | collective-permute-start | bytes 786440 | tf_op jit(solution)/shard_map/ppermute | solution.py:228
  52.6 9.2 %collective-permute-start.9 = (bf16[2,512,128]{2,1,0:T(8,128)(2,1)S(1)}, bf16[2,512,128]{2,1,0:T(8,128)(2,1)S(1)}, u32[]{:S(2)}, u32[]{:S(2)}) collective-permute-start(bf16[2,512,128]{2,1,0:T(8,128)(2,1)S(1)} %get-tuple-element.25), channel_id=1, source_target_pairs={{0,8},{8,16},{16,24},{24,32},{32,40},{40,48},{48,56},{56,0},{1,9},... | collective-permute-start | bytes 786440 | tf_op jit(solution)/shard_map/ppermute | solution.py:228
  54.0 22.6 %all-to-all-start.1 = ((bf16[16,256,128]{2,1,0:T(8,128)(2,1)}), bf16[16,256,128]{2,1,0:T(8,128)(2,1)}, u32[]{:S(2)}, u32[]{:S(2)}) async-start(bf16[16,256,128]{2,1,0:T(8,128)(2,1)} %bitcast.10), calls=%async_computation.1 | async-start | bytes 2097152 | tf_op jit(solution)/shard_map/all_to_all | solution.py:220
  61.9 5.6 %collective-permute-start.11 = (bf16[512,128]{1,0:T(8,128)(2,1)S(1)}, bf16[512,128]{1,0:T(8,128)(2,1)S(1)}, u32[]{:S(2)}, u32[]{:S(2)}) collective-permute-start(bf16[512,128]{1,0:T(8,128)(2,1)S(1)} %get-tuple-element.21), channel_id=1, source_target_pairs={{0,8},{8,16},{16,24},{24,32},{32,40},{40,48},{48,56},{56,0},{1,9},... | collective-permute-start | bytes 393224 | tf_op jit(solution)/shard_map/ppermute | solution.py:228
  62.0 5.7 %collective-permute-start.12 = (bf16[512,128]{1,0:T(8,128)(2,1)S(1)}, bf16[512,128]{1,0:T(8,128)(2,1)S(1)}, u32[]{:S(2)}, u32[]{:S(2)}) collective-permute-start(bf16[512,128]{1,0:T(8,128)(2,1)S(1)} %get-tuple-element.22), channel_id=1, source_target_pairs={{0,56},{8,0},{16,8},{24,16},{32,24},{40,32},{48,40},{56,48},{1,57}... | collective-permute-start | bytes 393224 | tf_op jit(solution)/shard_map/ppermute | solution.py:228
  64.7 11.1 %collective-permute-start.13 = (bf16[512,128]{1,0:T(8,128)(2,1)S(1)}, bf16[512,128]{1,0:T(8,128)(2,1)S(1)}, u32[]{:S(2)}, u32[]{:S(2)}) collective-permute-start(bf16[512,128]{1,0:T(8,128)(2,1)S(1)} %get-tuple-element.23), channel_id=1, source_target_pairs={{0,32},{8,40},{16,48},{24,56},{32,0},{40,8},{48,16},{56,24},{1,33}... | collective-permute-start | bytes 393224 | tf_op jit(solution)/shard_map/ppermute | solution.py:228

commit v9 on v8

--- a/solution.py
+++ b/solution.py
@@ -237,6 +237,13 @@
 
 def add(mine, other):
     return mine.astype(jnp.float32) + other.astype(jnp.float32)
+
+
+def sum_kernel(parts_ref, out_ref):
+    total = parts_ref[0].astype(jnp.float32)
+    for s in range(1, PLANE):
+        total = total + parts_ref[s].astype(jnp.float32)
+    out_ref[...] = total.astype(jnp.bfloat16)
 
 
 def combine_kernel(mine_ref, other_ref, below_ref, above_ref, up_ref, down_ref, over_ref):
@@ -347,7 +354,13 @@
     near_other = swap_cores(near_other)
     query_back = exchange(query_part.reshape(PLANE, ROWS, W), ("x", "y"))
     page_grad = reduce_column(near_mine, near_other, from_below, from_above)
-    query_grad = jnp.sum(query_back.astype(jnp.float32), axis=0).astype(jnp.bfloat16)
+    query_grad = pl.pallas_call(
+        sum_kernel,
+        out_shape=jax.ShapeDtypeStruct((ROWS, W), jnp.bfloat16),
+        in_specs=[vmem],
+        out_specs=vmem,
+        compiler_params=pltpu.CompilerParams(vmem_limit_bytes=4 << 20),
+    )(query_back)
     return query_grad.reshape(Q_DEV, QT, W), page_grad[None]
 
 

time: 78.4 us -> 78.1 us (level); the launches traced: 78.6 us -> 77 us
  waiting for transfers between devices: 22.3 us -> 19.8 us
  Pallas kernels: 13.8 us -> 15.9 us
  other arithmetic: 3.18 us -> 1.87 us
    ppermute x10, waiting for transfers between devices: 17.2 us -> 14.6 us  [move(): return lax.ppermute(array, 'z', [(i, (i + step) % NZ) for i in range(NZ)])]
    reduce_sum x1 -> x0, other arithmetic: 2.01 us -> none  [shards(): jnp.sum(query_back.astype(jnp.float32), axis=0).astype(jnp.bfloat16)]
    ppermute x4, starting transfers between devices: 7.71 us -> 6.35 us  [swap_cores(): return lax.ppermute(array, 'core', [(0, 1), (1, 0)])]
    pallas_call x2, Pallas kernels: 11.4 us -> 12.8 us  [score(): pl.pallas_call(functools.partial(second_kernel if last else first_kernel,...]
    all_to_all x2, starting transfers between devices: 11.2 us -> 12 us  [exchange(): return lax.all_to_all(array, axes, split_axis=0, concat_axis=0, tiled=True)]
  transfers between devices with their start and end apart: 16 -> 16, of which waited for: 7 -> 5; matrix products, arithmetic and copies ran while one was open for 2% -> 3% of each run, Pallas kernels for 15% -> 17%
where the time goes in v9:
time: 78.1 us; the launch traced here: 77 us
  starting transfers between devices  38.5 us (49%)
  waiting for transfers between devices  19.8 us (25%)
  Pallas kernels  15.9 us (20%)
  other arithmetic  1.87 us (2%)
  between operations  0.8 us (1%)
    ppermute x10, starting transfers between devices, move(): return lax.ppermute(array, 'z', [(i, (i + step) % NZ) for i in range(NZ)])  20.1 us
    ppermute x10, waiting for transfers between devices, move(): return lax.ppermute(array, 'z', [(i, (i + step) % NZ) for i in range(NZ)])  14.6 us
    pallas_call x2, Pallas kernels, score(): pl.pallas_call(functools.partial(second_kernel if last else first_kernel,...  12.8 us
    all_to_all x2, starting transfers between devices, exchange(): return lax.all_to_all(array, axes, split_axis=0, concat_axis=0, tiled=True)  12 us
    ppermute x4, starting transfers between devices, swap_cores(): return lax.ppermute(array, 'core', [(0, 1), (1, 0)])  6.35 us
    all_to_all x2, waiting for transfers between devices, exchange(): return lax.all_to_all(array, axes, split_axis=0, concat_axis=0, tiled=True)  5.17 us
    pallas_call x1, Pallas kernels, shards(): pl.pallas_call(pack_kernel, out_shape=(jax.ShapeDtypeStruct((PLANE, SEND_...  2.18 us
  transfers between devices with their start and end apart: 16, of which 5 were waited for; matrix products, arithmetic and copies ran while one was open for 3% of the time, Pallas kernels for 17%

profile of v9, /device:TPU:1, one launch (start us, length us, event | category | flops | bytes accessed | tf_op | source)
XLA Modules:
  0.0 77.0 jit_solution(7856522821309107923)
XLA Ops:
  0.6 2.2 %shard_map.86 = (bf16[16,272,128]{2,1,0:T(8,128)(2,1)}, bf16[512,128]{1,0:T(8,128)(2,1)}) custom-call(s32[64]{0:T(128)} %bitcast.36, s32[64]{0:T(128)} %query_ref.1, s32[64]{0:T(128)} %label_ref.1, s32[1]{0:T(128)} %bitcast.2.core_ref, bf16[256,128]{1,0:T(8,128)(2,1)} %bitcast.34, bf16[1024,128]{1,0:T(8,128)(2,1)} %bitcast.32), custom_call_target="tpu_custom_call" | custom-call | tf_op jit(solution)/shard_map/pallas_call | solution.py:325
  2.8 2.5 %collective-permute-start = (bf16[512,128]{1,0:T(8,128)(2,1)}, bf16[512,128]{1,0:T(8,128)(2,1)S(1)}, u32[]{:S(2)}, u32[]{:S(2)}) collective-permute-start(bf16[512,128]{1,0:T(8,128)(2,1)} %get-tuple-element.14), channel_id=1, source_target_pairs={{0,8},{8,16},{16,24},{24,32},{32,40},{40,48},{48,56},{56,0},{1,9},... | collective-permute-start | bytes 393224 | tf_op jit(solution)/shard_map/ppermute | solution.py:228
  5.4 4.0 %collective-permute-start.1 = (bf16[512,128]{1,0:T(8,128)(2,1)}, bf16[512,128]{1,0:T(8,128)(2,1)S(1)}, u32[]{:S(2)}, u32[]{:S(2)}) collective-permute-start(bf16[512,128]{1,0:T(8,128)(2,1)} %get-tuple-element.14), channel_id=1, source_target_pairs={{0,56},{8,0},{16,8},{24,16},{32,24},{40,32},{48,40},{56,48},{1,57}... | collective-permute-start | bytes 393224 | tf_op jit(solution)/shard_map/ppermute | solution.py:228
  9.4 3.9 %collective-permute-start.2 = (bf16[512,128]{1,0:T(8,128)(2,1)}, bf16[512,128]{1,0:T(8,128)(2,1)S(1)}, u32[]{:S(2)}, u32[]{:S(2)}) collective-permute-start(bf16[512,128]{1,0:T(8,128)(2,1)} %get-tuple-element.14), channel_id=1, source_target_pairs={{0,32},{8,40},{16,48},{24,56},{32,0},{40,8},{48,16},{56,24},{1,33}... | collective-permute-start | bytes 393224 | tf_op jit(solution)/shard_map/ppermute | solution.py:228
  13.3 0.0 copy-start.2
  13.3 6.9 %all-to-all-start = ((bf16[16,272,128]{2,1,0:T(8,128)(2,1)}), bf16[16,272,128]{2,1,0:T(8,128)(2,1)S(1)}, u32[]{:S(2)}, u32[]{:S(2)}) async-start(bf16[16,272,128]{2,1,0:T(8,128)(2,1)} %get-tuple-element.13), calls=%async_computation | async-start | bytes 2228224 | tf_op jit(solution)/shard_map/all_to_all | solution.py:220
  20.2 0.0 copy-start.1
  20.2 0.0 collective-permute-done
  20.2 0.0 collective-permute-done.1
  20.2 0.0 collective-permute-done.2
  20.3 0.0 copy-start
  20.3 0.1 collective-permute-start.4
  20.4 2.7 %collective-permute-start.5 = (bf16[2,512,128]{2,1,0:T(8,128)(2,1)S(1)}, bf16[2,512,128]{2,1,0:T(8,128)(2,1)S(1)}, u32[]{:S(2)}, u32[]{:S(2)}) collective-permute-start(bf16[2,512,128]{2,1,0:T(8,128)(2,1)S(1)} %get-tuple-element.26), channel_id=1, source_target_pairs={{0,56},{8,0},{16,8},{24,16},{32,24},{40,32},{48,40},{56,48},{1,57}... | collective-permute-start | bytes 786440 | tf_op jit(solution)/shard_map/ppermute | solution.py:228
  23.1 0.0 copy-done.2
  23.1 4.4 %collective-permute-done.4 = bf16[2,512,128]{2,1,0:T(8,128)(2,1)S(1)} collective-permute-done((bf16[2,512,128]{2,1,0:T(8,128)(2,1)S(1)}, bf16[2,512,128]{2,1,0:T(8,128)(2,1)S(1)}, u32[]{:S(2)}, u32[]{:S(2)}) %collective-permute-start.4) | collective-permute-done | bytes 262176 | tf_op jit(solution)/shard_map/ppermute | solution.py:228
  27.6 0.0 collective-permute-done.5
  27.6 2.9 %collective-permute-start.6 = (bf16[4,512,128]{2,1,0:T(8,128)(2,1)S(1)}, bf16[4,512,128]{2,1,0:T(8,128)(2,1)S(1)}, u32[]{:S(2)}, u32[]{:S(2)}) collective-permute-start(bf16[4,512,128]{2,1,0:T(8,128)(2,1)S(1)} %constant_dynamic-update-slice_fusion.refs_4_), channel_id=1, source_target_pairs={{0,1},{1,0},{2,3},{3,2},{4,5},{5,4},{6,7},{7,6},{8,9},{9,8},{10,11... | collective-permute-start | bytes 1572872 | tf_op jit(solution)/shard_map/ppermute | solution.py:224
  30.5 0.1 fusion.5
  30.6 0.1 pad_add_fusion.1.refs_0_
  30.6 0.0 copy-done.1
  30.6 0.1 pad_maximum_fusion.refs_4_
  30.7 0.1 collective-permute-start.3
  30.8 5.2 %all-to-all-done.refs_3_ = bf16[16,272,128]{2,1,0:T(8,128)(2,1)S(1)} async-done(((bf16[16,272,128]{2,1,0:T(8,128)(2,1)}), bf16[16,272,128]{2,1,0:T(8,128)(2,1)S(1)}, u32[]{:S(2)}, u32[]{:S(2)}) %all-to-all-start) | async-done | bytes 1114144 | tf_op jit(solution)/shard_map/all_to_all | solution.py:220
  36.0 0.0 collective-permute-done.6.refs_5_
  36.0 0.0 copy-done
  36.0 5.8 %shard_map.87 = (f32[4096,128]{1,0:T(8,128)S(1)}, bf16[4,512,128]{2,1,0:T(8,128)(2,1)S(1)}, bf16[4,512,128]{2,1,0:T(8,128)(2,1)S(1)}) custom-call(s32[5]{0:T(128)S(1)} %pad_add_fusion.1.refs_0_, s32[2]{0:T(128)S(1)} %copy-done, s32[16,32]{1,0:T(8,128)S(1)} %bitcast.24, bf16[16,272,128]{2,1,0:T(8,128)(2,1)S(1)} %all-to-all-done.refs_3_, ...), custom_call_target="tpu_custom_call" | custom-call | flops 3221225472 | bytes 8388608 | tf_op jit(solution)/shard_map/pallas_call | solution.py:306
  41.8 3.3 %collective-permute-start.8 = (bf16[4,512,128]{2,1,0:T(8,128)(2,1)S(1)}, bf16[4,512,128]{2,1,0:T(8,128)(2,1)S(1)}, u32[]{:S(2)}, u32[]{:S(2)}) collective-permute-start(bf16[4,512,128]{2,1,0:T(8,128)(2,1)S(1)} %get-tuple-element.20), channel_id=1, source_target_pairs={{0,1},{1,0},{2,3},{3,2},{4,5},{5,4},{6,7},{7,6},{8,9},{9,8},{10,11... | collective-permute-start | bytes 1572872 | tf_op jit(solution)/shard_map/ppermute | solution.py:224
  45.2 0.1 pad_add_fusion.refs_0_
  45.2 0.0 collective-permute-done.3.refs_5_
  45.2 7.0 %shard_map.88 = (bf16[4096,128]{1,0:T(8,128)(2,1)}, bf16[4,512,128]{2,1,0:T(8,128)(2,1)S(1)}, bf16[4,512,128]{2,1,0:T(8,128)(2,1)S(1)}) custom-call(s32[5]{0:T(128)S(1)} %pad_add_fusion.refs_0_, s32[2]{0:T(128)S(1)} %copy-done, s32[16,32]{1,0:T(8,128)S(1)} %bitcast.25, bf16[16,272,128]{2,1,0:T(8,128)(2,1)S(1)} %all-to-all-done.refs_3_, ...), custom_call_target="tpu_custom_call" | custom-call | flops 3221225472 | bytes 8388608 | tf_op jit(solution)/shard_map/pallas_call | solution.py:306
  52.2 0.0 collective-permute-start.7
  52.3 0.0 collective-permute-done.8
  52.3 0.8 %add_convert_fusion = (bf16[2,512,128]{2,1,0:T(8,128)(2,1)}, bf16[2,512,128]{2,1,0:T(8,128)(2,1)S(1)}) fusion(bf16[4,512,128]{2,1,0:T(8,128)(2,1)S(1)} %collective-permute-done.8, bf16[4,512,128]{2,1,0:T(8,128)(2,1)S(1)} %get-tuple-element.19), kind=kLoop, calls=%fused_computation.1 | loop fusion | flops 1048576 | bytes 1572864 | tf_op jit(solution)/shard_map/convert_element_type | solution.py:349
  53.1 0.2 collective-permute-start.10
  53.3 1.3 %collective-permute-start.9 = (bf16[2,512,128]{2,1,0:T(8,128)(2,1)S(1)}, bf16[2,512,128]{2,1,0:T(8,128)(2,1)S(1)}, u32[]{:S(2)}, u32[]{:S(2)}) collective-permute-start(bf16[2,512,128]{2,1,0:T(8,128)(2,1)S(1)} %get-tuple-element.25), channel_id=1, source_target_pairs={{0,8},{8,16},{16,24},{24,32},{32,40},{40,48},{48,56},{56,0},{1,9},... | collective-permute-start | bytes 786440 | tf_op jit(solution)/shard_map/ppermute | solution.py:228
  54.6 5.2 %all-to-all-start.1 = ((bf16[16,256,128]{2,1,0:T(8,128)(2,1)}), bf16[16,256,128]{2,1,0:T(8,128)(2,1)S(1)}, u32[]{:S(2)}, u32[]{:S(2)}) async-start(bf16[16,256,128]{2,1,0:T(8,128)(2,1)} %bitcast.10), calls=%async_computation.1 | async-start | bytes 2097152 | tf_op jit(solution)/shard_map/all_to_all | solution.py:220
  59.7 0.0 collective-permute-done.7.other_ref
  59.8 1.0 %collective-permute-done.10.above_ref = bf16[2,512,128]{2,1,0:T(8,128)(2,1)S(1)} collective-permute-done((bf16[2,512,128]{2,1,0:T(8,128)(2,1)}, bf16[2,512,128]{2,1,0:T(8,128)(2,1)S(1)}, u32[]{:S(2)}, u32[]{:S(2)}) %collective-permute-start.10) | collective-permute-done | bytes 262176 | tf_op jit(solution)/shard_map/ppermute | solution.py:228
  60.7 0.8 %collective-permute-done.9.below_ref = bf16[2,512,128]{2,1,0:T(8,128)(2,1)S(1)} collective-permute-done((bf16[2,512,128]{2,1,0:T(8,128)(2,1)S(1)}, bf16[2,512,128]{2,1,0:T(8,128)(2,1)S(1)}, u32[]{:S(2)}, u32[]{:S(2)}) %collective-permute-start.9) | collective-permute-done | bytes 262176 | tf_op jit(solution)/shard_map/ppermute | solution.py:228
  61.6 0.2 shard_map.90
  61.7 0.2 collective-permute-start.11
  61.9 2.6 %collective-permute-start.12 = (bf16[512,128]{1,0:T(8,128)(2,1)S(1)}, bf16[512,128]{1,0:T(8,128)(2,1)S(1)}, u32[]{:S(2)}, u32[]{:S(2)}) collective-permute-start(bf16[512,128]{1,0:T(8,128)(2,1)S(1)} %get-tuple-element.22), channel_id=1, source_target_pairs={{0,56},{8,0},{16,8},{24,16},{32,24},{40,32},{48,40},{56,48},{1,57}... | collective-permute-start | bytes 393224 | tf_op jit(solution)/shard_map/ppermute | solution.py:228
  64.5 2.7 %collective-permute-start.13 = (bf16[512,128]{1,0:T(8,128)(2,1)S(1)}, bf16[512,128]{1,0:T(8,128)(2,1)S(1)}, u32[]{:S(2)}, u32[]{:S(2)}) collective-permute-start(bf16[512,128]{1,0:T(8,128)(2,1)S(1)} %get-tuple-element.23), channel_id=1, source_target_pairs={{0,32},{8,40},{16,48},{24,56},{32,0},{40,8},{48,16},{56,24},{1,33}... | collective-permute-start | bytes 393224 | tf_op jit(solution)/shard_map/ppermute | solution.py:228
  67.1 0.0 collective-permute-done.11
  67.1 0.0 collective-permute-done.12
  67.1 8.3 %collective-permute-done.13 = bf16[512,128]{1,0:T(8,128)(2,1)S(1)} collective-permute-done((bf16[512,128]{1,0:T(8,128)(2,1)S(1)}, bf16[512,128]{1,0:T(8,128)(2,1)S(1)}, u32[]{:S(2)}, u32[]{:S(2)}) %collective-permute-start.13) | collective-permute-done | bytes 131104 | tf_op jit(solution)/shard_map/ppermute | solution.py:228
  75.5 0.8 fusion.3
  76.2 0.0 all-to-all-done.1.parts_ref
  76.2 0.8 shard_map.89
  (5 shorter events, 0.1 us)
Async XLA Ops:
  2.8 17.4 %collective-permute-start = (bf16[512,128]{1,0:T(8,128)(2,1)}, bf16[512,128]{1,0:T(8,128)(2,1)S(1)}, u32[]{:S(2)}, u32[]{:S(2)}) collective-permute-start(bf16[512,128]{1,0:T(8,128)(2,1)} %get-tuple-element.14), channel_id=1, source_target_pairs={{0,8},{8,16},{16,24},{24,32},{32,40},{40,48},{48,56},{56,0},{1,9},... | collective-permute-start | bytes 393224 | tf_op jit(solution)/shard_map/ppermute | solution.py:228
  5.4 14.9 %collective-permute-start.1 = (bf16[512,128]{1,0:T(8,128)(2,1)}, bf16[512,128]{1,0:T(8,128)(2,1)S(1)}, u32[]{:S(2)}, u32[]{:S(2)}) collective-permute-start(bf16[512,128]{1,0:T(8,128)(2,1)} %get-tuple-element.14), channel_id=1, source_target_pairs={{0,56},{8,0},{16,8},{24,16},{32,24},{40,32},{48,40},{56,48},{1,57}... | collective-permute-start | bytes 393224 | tf_op jit(solution)/shard_map/ppermute | solution.py:228
  9.4 10.9 %collective-permute-start.2 = (bf16[512,128]{1,0:T(8,128)(2,1)}, bf16[512,128]{1,0:T(8,128)(2,1)S(1)}, u32[]{:S(2)}, u32[]{:S(2)}) collective-permute-start(bf16[512,128]{1,0:T(8,128)(2,1)} %get-tuple-element.14), channel_id=1, source_target_pairs={{0,32},{8,40},{16,48},{24,56},{32,0},{40,8},{48,16},{56,24},{1,33}... | collective-permute-start | bytes 393224 | tf_op jit(solution)/shard_map/ppermute | solution.py:228
  13.3 9.8 %copy-start.2 = (s32[8]{0:T(128)S(1)}, s32[8]{0:T(128)}, u32[]{:S(2)}) copy-start(s32[8]{0:T(128)} %constant.35.clone) | copy-start | bytes 100
  13.3 22.7 %all-to-all-start = ((bf16[16,272,128]{2,1,0:T(8,128)(2,1)}), bf16[16,272,128]{2,1,0:T(8,128)(2,1)S(1)}, u32[]{:S(2)}, u32[]{:S(2)}) async-start(bf16[16,272,128]{2,1,0:T(8,128)(2,1)} %get-tuple-element.13), calls=%async_computation | async-start | bytes 2228224 | tf_op jit(solution)/shard_map/all_to_all | solution.py:220
  20.2 10.4 %copy-start.1 = (bf16[512,128]{1,0:T(8,128)(2,1)S(1)}, bf16[512,128]{1,0:T(8,128)(2,1)}, u32[]{:S(2)}) copy-start(bf16[512,128]{1,0:T(8,128)(2,1)} %get-tuple-element.14) | copy-start | bytes 393220
  20.3 15.7 %copy-start = (s32[2]{0:T(128)S(1)}, s32[2]{0:T(128)}, u32[]{:S(2)}) copy-start(s32[2]{0:T(128)} %refs_1_.3) | copy-start | bytes 28
  20.3 7.2 %collective-permute-start.4 = (bf16[2,512,128]{2,1,0:T(8,128)(2,1)S(1)}, bf16[2,512,128]{2,1,0:T(8,128)(2,1)S(1)}, u32[]{:S(2)}, u32[]{:S(2)}) collective-permute-start(bf16[2,512,128]{2,1,0:T(8,128)(2,1)S(1)} %get-tuple-element.27), channel_id=1, source_target_pairs={{0,8},{8,16},{16,24},{24,32},{32,40},{40,48},{48,56},{56,0},{1,9},... | collective-permute-start | bytes 786440 | tf_op jit(solution)/shard_map/ppermute | solution.py:228
  20.4 7.1 %collective-permute-start.5 = (bf16[2,512,128]{2,1,0:T(8,128)(2,1)S(1)}, bf16[2,512,128]{2,1,0:T(8,128)(2,1)S(1)}, u32[]{:S(2)}, u32[]{:S(2)}) collective-permute-start(bf16[2,512,128]{2,1,0:T(8,128)(2,1)S(1)} %get-tuple-element.26), channel_id=1, source_target_pairs={{0,56},{8,0},{16,8},{24,16},{32,24},{40,32},{48,40},{56,48},{1,57}... | collective-permute-start | bytes 786440 | tf_op jit(solution)/shard_map/ppermute | solution.py:228
  27.6 8.4 %collective-permute-start.6 = (bf16[4,512,128]{2,1,0:T(8,128)(2,1)S(1)}, bf16[4,512,128]{2,1,0:T(8,128)(2,1)S(1)}, u32[]{:S(2)}, u32[]{:S(2)}) collective-permute-start(bf16[4,512,128]{2,1,0:T(8,128)(2,1)S(1)} %constant_dynamic-update-slice_fusion.refs_4_), channel_id=1, source_target_pairs={{0,1},{1,0},{2,3},{3,2},{4,5},{5,4},{6,7},{7,6},{8,9},{9,8},{10,11... | collective-permute-start | bytes 1572872 | tf_op jit(solution)/shard_map/ppermute | solution.py:224
  30.7 14.5 %collective-permute-start.3 = (bf16[4,512,128]{2,1,0:T(8,128)(2,1)S(1)}, bf16[4,512,128]{2,1,0:T(8,128)(2,1)S(1)}, u32[]{:S(2)}, u32[]{:S(2)}) collective-permute-start(bf16[4,512,128]{2,1,0:T(8,128)(2,1)S(1)} %pad_maximum_fusion.refs_4_), channel_id=1, source_target_pairs={{0,1},{1,0},{2,3},{3,2},{4,5},{5,4},{6,7},{7,6},{8,9},{9,8},{10,11... | collective-permute-start | bytes 1572872 | tf_op jit(solution)/shard_map/ppermute | solution.py:224
  41.8 10.5 %collective-permute-start.8 = (bf16[4,512,128]{2,1,0:T(8,128)(2,1)S(1)}, bf16[4,512,128]{2,1,0:T(8,128)(2,1)S(1)}, u32[]{:S(2)}, u32[]{:S(2)}) collective-permute-start(bf16[4,512,128]{2,1,0:T(8,128)(2,1)S(1)} %get-tuple-element.20), channel_id=1, source_target_pairs={{0,1},{1,0},{2,3},{3,2},{4,5},{5,4},{6,7},{7,6},{8,9},{9,8},{10,11... | collective-permute-start | bytes 1572872 | tf_op jit(solution)/shard_map/ppermute | solution.py:224
  52.2 7.5 %collective-permute-start.7 = (bf16[4,512,128]{2,1,0:T(8,128)(2,1)S(1)}, bf16[4,512,128]{2,1,0:T(8,128)(2,1)S(1)}, u32[]{:S(2)}, u32[]{:S(2)}) collective-permute-start(bf16[4,512,128]{2,1,0:T(8,128)(2,1)S(1)} %get-tuple-element.18), channel_id=1, source_target_pairs={{0,1},{1,0},{2,3},{3,2},{4,5},{5,4},{6,7},{7,6},{8,9},{9,8},{10,11... | collective-permute-start | bytes 1572872 | tf_op jit(solution)/shard_map/ppermute | solution.py:224
  53.1 7.6 %collective-permute-start.10 = (bf16[2,512,128]{2,1,0:T(8,128)(2,1)}, bf16[2,512,128]{2,1,0:T(8,128)(2,1)S(1)}, u32[]{:S(2)}, u32[]{:S(2)}) collective-permute-start(bf16[2,512,128]{2,1,0:T(8,128)(2,1)} %get-tuple-element.24), channel_id=1, source_target_pairs={{0,56},{8,0},{16,8},{24,16},{32,24},{40,32},{48,40},{56,48},{1,57}... | collective-permute-start | bytes 786440 | tf_op jit(solution)/shard_map/ppermute | solution.py:228
  53.3 8.3 %collective-permute-start.9 = (bf16[2,512,128]{2,1,0:T(8,128)(2,1)S(1)}, bf16[2,512,128]{2,1,0:T(8,128)(2,1)S(1)}, u32[]{:S(2)}, u32[]{:S(2)}) collective-permute-start(bf16[2,512,128]{2,1,0:T(8,128)(2,1)S(1)} %get-tuple-element.25), channel_id=1, source_target_pairs={{0,8},{8,16},{16,24},{24,32},{32,40},{40,48},{48,56},{56,0},{1,9},... | collective-permute-start | bytes 786440 | tf_op jit(solution)/shard_map/ppermute | solution.py:228
  54.6 21.7 %all-to-all-start.1 = ((bf16[16,256,128]{2,1,0:T(8,128)(2,1)}), bf16[16,256,128]{2,1,0:T(8,128)(2,1)S(1)}, u32[]{:S(2)}, u32[]{:S(2)}) async-start(bf16[16,256,128]{2,1,0:T(8,128)(2,1)} %bitcast.10), calls=%async_computation.1 | async-start | bytes 2097152 | tf_op jit(solution)/shard_map/all_to_all | solution.py:220
  61.7 5.4 %collective-permute-start.11 = (bf16[512,128]{1,0:T(8,128)(2,1)S(1)}, bf16[512,128]{1,0:T(8,128)(2,1)S(1)}, u32[]{:S(2)}, u32[]{:S(2)}) collective-permute-start(bf16[512,128]{1,0:T(8,128)(2,1)S(1)} %get-tuple-element.21), channel_id=1, source_target_pairs={{0,8},{8,16},{16,24},{24,32},{32,40},{40,48},{48,56},{56,0},{1,9},... | collective-permute-start | bytes 393224 | tf_op jit(solution)/shard_map/ppermute | solution.py:228
  61.9 5.2 %collective-permute-start.12 = (bf16[512,128]{1,0:T(8,128)(2,1)S(1)}, bf16[512,128]{1,0:T(8,128)(2,1)S(1)}, u32[]{:S(2)}, u32[]{:S(2)}) collective-permute-start(bf16[512,128]{1,0:T(8,128)(2,1)S(1)} %get-tuple-element.22), channel_id=1, source_target_pairs={{0,56},{8,0},{16,8},{24,16},{32,24},{40,32},{48,40},{56,48},{1,57}... | collective-permute-start | bytes 393224 | tf_op jit(solution)/shard_map/ppermute | solution.py:228
  64.5 11.0 %collective-permute-start.13 = (bf16[512,128]{1,0:T(8,128)(2,1)S(1)}, bf16[512,128]{1,0:T(8,128)(2,1)S(1)}, u32[]{:S(2)}, u32[]{:S(2)}) collective-permute-start(bf16[512,128]{1,0:T(8,128)(2,1)S(1)} %get-tuple-element.23), channel_id=1, source_target_pairs={{0,32},{8,40},{16,48},{24,56},{32,0},{40,8},{48,16},{56,24},{1,33}... | collective-permute-start | bytes 393224 | tf_op jit(solution)/shard_map/ppermute | solution.py:228

commit v10 on v9

--- a/solution.py
+++ b/solution.py
@@ -229,7 +229,7 @@
 
 
 def gather_column(half):
-    below, above, across = move(half, 1), move(half, -1), move(half, 4)
+    across, below, above = move(half, 4), move(half, 1), move(half, -1)
     far_below = move(jnp.stack([below, across]), 1)
     far_above = move(jnp.stack([above, across]), -1)
     return jnp.stack([half, below, above, across]), jnp.concatenate([far_below, far_above])
@@ -266,7 +266,7 @@
         ),
     )(mine, other, from_below, from_above)
     total = add(mine[0], other[0])
-    for part in (move(up, 1), move(down, -1), move(over, 4)):
+    for part in (move(over, 4), move(up, 1), move(down, -1)):
         total = total + part.astype(jnp.float32)
     return total.astype(jnp.bfloat16)
 

time: 78.1 us -> 77.2 us (0.988)
  Pallas kernels: 15.9 us -> 14.5 us
  starting transfers between devices: 38.5 us -> 39.9 us
    pallas_call x2, Pallas kernels: 12.8 us -> 11.4 us  [score(): pl.pallas_call(functools.partial(second_kernel if last else first_kernel,...]
    ppermute x4, starting transfers between devices: 6.35 us -> 7.71 us  [swap_cores(): return lax.ppermute(array, 'core', [(0, 1), (1, 0)])]
  transfers between devices with their start and end apart: 16 -> 16, of which waited for: 5 -> 6; matrix products, arithmetic and copies ran while one was open for 3% -> 3% of each run, Pallas kernels for 17% -> 15%
where the time goes in v10:
time: 77.2 us; the launch traced here: 76.9 us
  starting transfers between devices  39.9 us (52%)
  waiting for transfers between devices  19.6 us (25%)
  Pallas kernels  14.5 us (19%)
  other arithmetic  1.87 us (2%)
  between operations  0.8 us (1%)
    ppermute x10, starting transfers between devices, move(): return lax.ppermute(array, 'z', [(i, (i + step) % NZ) for i in range(NZ)])  20.7 us
    ppermute x10, waiting for transfers between devices, move(): return lax.ppermute(array, 'z', [(i, (i + step) % NZ) for i in range(NZ)])  14.4 us
    all_to_all x2, starting transfers between devices, exchange(): return lax.all_to_all(array, axes, split_axis=0, concat_axis=0, tiled=True)  11.5 us
    pallas_call x2, Pallas kernels, score(): pl.pallas_call(functools.partial(second_kernel if last else first_kernel,...  11.4 us
    ppermute x4, starting transfers between devices, swap_cores(): return lax.ppermute(array, 'core', [(0, 1), (1, 0)])  7.71 us
    all_to_all x2, waiting for transfers between devices, exchange(): return lax.all_to_all(array, axes, split_axis=0, concat_axis=0, tiled=True)  5.17 us
    pallas_call x1, Pallas kernels, shards(): pl.pallas_call(pack_kernel, out_shape=(jax.ShapeDtypeStruct((PLANE, SEND_...  2.18 us
  transfers between devices with their start and end apart: 16, of which 6 were waited for; matrix products, arithmetic and copies ran while one was open for 3% of the time, Pallas kernels for 15%

profile of v10, /device:TPU:1, one launch (start us, length us, event | category | flops | bytes accessed | tf_op | source)
XLA Modules:
  0.0 76.9 jit_solution(2745715341512290178)
XLA Ops:
  0.6 2.2 %shard_map.86 = (bf16[16,272,128]{2,1,0:T(8,128)(2,1)}, bf16[512,128]{1,0:T(8,128)(2,1)}) custom-call(s32[64]{0:T(128)} %bitcast.36, s32[64]{0:T(128)} %query_ref.1, s32[64]{0:T(128)} %label_ref.1, s32[1]{0:T(128)} %bitcast.2.core_ref, bf16[256,128]{1,0:T(8,128)(2,1)} %bitcast.34, bf16[1024,128]{1,0:T(8,128)(2,1)} %bitcast.32), custom_call_target="tpu_custom_call" | custom-call | tf_op jit(solution)/shard_map/pallas_call | solution.py:325
  2.8 2.5 %collective-permute-start = (bf16[512,128]{1,0:T(8,128)(2,1)}, bf16[512,128]{1,0:T(8,128)(2,1)S(1)}, u32[]{:S(2)}, u32[]{:S(2)}) collective-permute-start(bf16[512,128]{1,0:T(8,128)(2,1)} %get-tuple-element.14), channel_id=1, source_target_pairs={{0,8},{8,16},{16,24},{24,32},{32,40},{40,48},{48,56},{56,0},{1,9},... | collective-permute-start | bytes 393224 | tf_op jit(solution)/shard_map/ppermute | solution.py:228
  5.4 4.0 %collective-permute-start.1 = (bf16[512,128]{1,0:T(8,128)(2,1)}, bf16[512,128]{1,0:T(8,128)(2,1)S(1)}, u32[]{:S(2)}, u32[]{:S(2)}) collective-permute-start(bf16[512,128]{1,0:T(8,128)(2,1)} %get-tuple-element.14), channel_id=1, source_target_pairs={{0,56},{8,0},{16,8},{24,16},{32,24},{40,32},{48,40},{56,48},{1,57}... | collective-permute-start | bytes 393224 | tf_op jit(solution)/shard_map/ppermute | solution.py:228
  9.4 3.9 %collective-permute-start.2 = (bf16[512,128]{1,0:T(8,128)(2,1)}, bf16[512,128]{1,0:T(8,128)(2,1)S(1)}, u32[]{:S(2)}, u32[]{:S(2)}) collective-permute-start(bf16[512,128]{1,0:T(8,128)(2,1)} %get-tuple-element.14), channel_id=1, source_target_pairs={{0,32},{8,40},{16,48},{24,56},{32,0},{40,8},{48,16},{56,24},{1,33}... | collective-permute-start | bytes 393224 | tf_op jit(solution)/shard_map/ppermute | solution.py:228
  13.3 0.0 copy-start.2
  13.3 6.9 %all-to-all-start = ((bf16[16,272,128]{2,1,0:T(8,128)(2,1)}), bf16[16,272,128]{2,1,0:T(8,128)(2,1)S(1)}, u32[]{:S(2)}, u32[]{:S(2)}) async-start(bf16[16,272,128]{2,1,0:T(8,128)(2,1)} %get-tuple-element.13), calls=%async_computation | async-start | bytes 2228224 | tf_op jit(solution)/shard_map/all_to_all | solution.py:220
  20.2 0.0 copy-start.1
  20.2 0.0 collective-permute-done
  20.2 0.0 collective-permute-done.1
  20.2 0.0 collective-permute-done.2
  20.3 0.0 copy-start
  20.3 0.1 collective-permute-start.4
  20.4 2.7 %collective-permute-start.5 = (bf16[2,512,128]{2,1,0:T(8,128)(2,1)S(1)}, bf16[2,512,128]{2,1,0:T(8,128)(2,1)S(1)}, u32[]{:S(2)}, u32[]{:S(2)}) collective-permute-start(bf16[2,512,128]{2,1,0:T(8,128)(2,1)S(1)} %get-tuple-element.26), channel_id=1, source_target_pairs={{0,56},{8,0},{16,8},{24,16},{32,24},{40,32},{48,40},{56,48},{1,57}... | collective-permute-start | bytes 786440 | tf_op jit(solution)/shard_map/ppermute | solution.py:228
  23.1 0.0 copy-done.2
  23.1 4.4 %collective-permute-done.4 = bf16[2,512,128]{2,1,0:T(8,128)(2,1)S(1)} collective-permute-done((bf16[2,512,128]{2,1,0:T(8,128)(2,1)S(1)}, bf16[2,512,128]{2,1,0:T(8,128)(2,1)S(1)}, u32[]{:S(2)}, u32[]{:S(2)}) %collective-permute-start.4) | collective-permute-done | bytes 262176 | tf_op jit(solution)/shard_map/ppermute | solution.py:228
  27.6 0.0 collective-permute-done.5
  27.6 2.9 %collective-permute-start.6 = (bf16[4,512,128]{2,1,0:T(8,128)(2,1)S(1)}, bf16[4,512,128]{2,1,0:T(8,128)(2,1)S(1)}, u32[]{:S(2)}, u32[]{:S(2)}) collective-permute-start(bf16[4,512,128]{2,1,0:T(8,128)(2,1)S(1)} %constant_dynamic-update-slice_fusion.refs_4_), channel_id=1, source_target_pairs={{0,1},{1,0},{2,3},{3,2},{4,5},{5,4},{6,7},{7,6},{8,9},{9,8},{10,11... | collective-permute-start | bytes 1572872 | tf_op jit(solution)/shard_map/ppermute | solution.py:224
  30.5 0.1 fusion.5
  30.6 0.1 pad_add_fusion.1.refs_0_
  30.6 0.0 copy-done.1
  30.6 0.1 pad_maximum_fusion.refs_4_
  30.7 0.1 collective-permute-start.3
  30.8 5.2 %all-to-all-done.refs_3_ = bf16[16,272,128]{2,1,0:T(8,128)(2,1)S(1)} async-done(((bf16[16,272,128]{2,1,0:T(8,128)(2,1)}), bf16[16,272,128]{2,1,0:T(8,128)(2,1)S(1)}, u32[]{:S(2)}, u32[]{:S(2)}) %all-to-all-start) | async-done | bytes 1114144 | tf_op jit(solution)/shard_map/all_to_all | solution.py:220
  36.0 0.0 collective-permute-done.6.refs_5_
  36.0 0.0 copy-done
  36.0 5.8 %shard_map.87 = (f32[4096,128]{1,0:T(8,128)S(1)}, bf16[4,512,128]{2,1,0:T(8,128)(2,1)S(1)}, bf16[4,512,128]{2,1,0:T(8,128)(2,1)S(1)}) custom-call(s32[5]{0:T(128)S(1)} %pad_add_fusion.1.refs_0_, s32[2]{0:T(128)S(1)} %copy-done, s32[16,32]{1,0:T(8,128)S(1)} %bitcast.24, bf16[16,272,128]{2,1,0:T(8,128)(2,1)S(1)} %all-to-all-done.refs_3_, ...), custom_call_target="tpu_custom_call" | custom-call | flops 3221225472 | bytes 8388608 | tf_op jit(solution)/shard_map/pallas_call | solution.py:306
  41.8 3.3 %collective-permute-start.8 = (bf16[4,512,128]{2,1,0:T(8,128)(2,1)S(1)}, bf16[4,512,128]{2,1,0:T(8,128)(2,1)S(1)}, u32[]{:S(2)}, u32[]{:S(2)}) collective-permute-start(bf16[4,512,128]{2,1,0:T(8,128)(2,1)S(1)} %get-tuple-element.20), channel_id=1, source_target_pairs={{0,1},{1,0},{2,3},{3,2},{4,5},{5,4},{6,7},{7,6},{8,9},{9,8},{10,11... | collective-permute-start | bytes 1572872 | tf_op jit(solution)/shard_map/ppermute | solution.py:224
  45.2 0.1 pad_add_fusion.refs_0_
  45.2 0.0 collective-permute-done.3.refs_5_
  45.2 5.6 %shard_map.88 = (bf16[4096,128]{1,0:T(8,128)(2,1)}, bf16[4,512,128]{2,1,0:T(8,128)(2,1)S(1)}, bf16[4,512,128]{2,1,0:T(8,128)(2,1)S(1)}) custom-call(s32[5]{0:T(128)S(1)} %pad_add_fusion.refs_0_, s32[2]{0:T(128)S(1)} %copy-done, s32[16,32]{1,0:T(8,128)S(1)} %bitcast.25, bf16[16,272,128]{2,1,0:T(8,128)(2,1)S(1)} %all-to-all-done.refs_3_, ...), custom_call_target="tpu_custom_call" | custom-call | flops 3221225472 | bytes 8388608 | tf_op jit(solution)/shard_map/pallas_call | solution.py:306
  50.9 1.4 %collective-permute-start.7 = (bf16[4,512,128]{2,1,0:T(8,128)(2,1)S(1)}, bf16[4,512,128]{2,1,0:T(8,128)(2,1)S(1)}, u32[]{:S(2)}, u32[]{:S(2)}) collective-permute-start(bf16[4,512,128]{2,1,0:T(8,128)(2,1)S(1)} %get-tuple-element.18), channel_id=1, source_target_pairs={{0,1},{1,0},{2,3},{3,2},{4,5},{5,4},{6,7},{7,6},{8,9},{9,8},{10,11... | collective-permute-start | bytes 1572872 | tf_op jit(solution)/shard_map/ppermute | solution.py:224
  52.3 0.0 collective-permute-done.8
  52.3 0.8 %add_convert_fusion = (bf16[2,512,128]{2,1,0:T(8,128)(2,1)}, bf16[2,512,128]{2,1,0:T(8,128)(2,1)S(1)}) fusion(bf16[4,512,128]{2,1,0:T(8,128)(2,1)S(1)} %collective-permute-done.8, bf16[4,512,128]{2,1,0:T(8,128)(2,1)S(1)} %get-tuple-element.19), kind=kLoop, calls=%fused_computation.1 | loop fusion | flops 1048576 | bytes 1572864 | tf_op jit(solution)/shard_map/convert_element_type | solution.py:349
  53.1 0.2 collective-permute-start.10
  53.3 1.3 %collective-permute-start.9 = (bf16[2,512,128]{2,1,0:T(8,128)(2,1)S(1)}, bf16[2,512,128]{2,1,0:T(8,128)(2,1)S(1)}, u32[]{:S(2)}, u32[]{:S(2)}) collective-permute-start(bf16[2,512,128]{2,1,0:T(8,128)(2,1)S(1)} %get-tuple-element.25), channel_id=1, source_target_pairs={{0,8},{8,16},{16,24},{24,32},{32,40},{40,48},{48,56},{56,0},{1,9},... | collective-permute-start | bytes 786440 | tf_op jit(solution)/shard_map/ppermute | solution.py:228
  54.6 4.6 %all-to-all-start.1 = ((bf16[16,256,128]{2,1,0:T(8,128)(2,1)}), bf16[16,256,128]{2,1,0:T(8,128)(2,1)S(1)}, u32[]{:S(2)}, u32[]{:S(2)}) async-start(bf16[16,256,128]{2,1,0:T(8,128)(2,1)} %bitcast.10), calls=%async_computation.1 | async-start | bytes 2097152 | tf_op jit(solution)/shard_map/all_to_all | solution.py:220
  59.2 0.0 collective-permute-done.7.other_ref
  59.2 2.0 %collective-permute-done.10.above_ref = bf16[2,512,128]{2,1,0:T(8,128)(2,1)S(1)} collective-permute-done((bf16[2,512,128]{2,1,0:T(8,128)(2,1)}, bf16[2,512,128]{2,1,0:T(8,128)(2,1)S(1)}, u32[]{:S(2)}, u32[]{:S(2)}) %collective-permute-start.10) | collective-permute-done | bytes 262176 | tf_op jit(solution)/shard_map/ppermute | solution.py:228
  61.3 0.3 collective-permute-done.9.below_ref
  61.5 0.2 shard_map.90
  61.7 3.3 %collective-permute-start.11 = (bf16[512,128]{1,0:T(8,128)(2,1)S(1)}, bf16[512,128]{1,0:T(8,128)(2,1)S(1)}, u32[]{:S(2)}, u32[]{:S(2)}) collective-permute-start(bf16[512,128]{1,0:T(8,128)(2,1)S(1)} %get-tuple-element.21), channel_id=1, source_target_pairs={{0,32},{8,40},{16,48},{24,56},{32,0},{40,8},{48,16},{56,24},{1,33}... | collective-permute-start | bytes 393224 | tf_op jit(solution)/shard_map/ppermute | solution.py:228
  65.0 0.0 collective-permute-start.12
  65.0 2.7 %collective-permute-start.13 = (bf16[512,128]{1,0:T(8,128)(2,1)S(1)}, bf16[512,128]{1,0:T(8,128)(2,1)S(1)}, u32[]{:S(2)}, u32[]{:S(2)}) collective-permute-start(bf16[512,128]{1,0:T(8,128)(2,1)S(1)} %get-tuple-element.23), channel_id=1, source_target_pairs={{0,56},{8,0},{16,8},{24,16},{32,24},{40,32},{48,40},{56,48},{1,57}... | collective-permute-start | bytes 393224 | tf_op jit(solution)/shard_map/ppermute | solution.py:228
  67.7 4.8 %collective-permute-done.11 = bf16[512,128]{1,0:T(8,128)(2,1)S(1)} collective-permute-done((bf16[512,128]{1,0:T(8,128)(2,1)S(1)}, bf16[512,128]{1,0:T(8,128)(2,1)S(1)}, u32[]{:S(2)}, u32[]{:S(2)}) %collective-permute-start.11) | collective-permute-done | bytes 131104 | tf_op jit(solution)/shard_map/ppermute | solution.py:228
  72.5 2.8 %collective-permute-done.12 = bf16[512,128]{1,0:T(8,128)(2,1)S(1)} collective-permute-done((bf16[512,128]{1,0:T(8,128)(2,1)S(1)}, bf16[512,128]{1,0:T(8,128)(2,1)S(1)}, u32[]{:S(2)}, u32[]{:S(2)}) %collective-permute-start.12) | collective-permute-done | bytes 131104 | tf_op jit(solution)/shard_map/ppermute | solution.py:228
  75.3 0.0 collective-permute-done.13
  75.3 0.8 fusion.3
  76.1 0.0 all-to-all-done.1.parts_ref
  76.1 0.8 %shard_map.89 = bf16[256,128]{1,0:T(8,128)(2,1)} custom-call(bf16[16,256,128]{2,1,0:T(8,128)(2,1)S(1)} %all-to-all-done.1.parts_ref), custom_call_target="tpu_custom_call" | custom-call | tf_op jit(solution)/shard_map/pallas_call | solution.py:357
  (5 shorter events, 0.1 us)
Async XLA Ops:
  2.8 17.4 %collective-permute-start = (bf16[512,128]{1,0:T(8,128)(2,1)}, bf16[512,128]{1,0:T(8,128)(2,1)S(1)}, u32[]{:S(2)}, u32[]{:S(2)}) collective-permute-start(bf16[512,128]{1,0:T(8,128)(2,1)} %get-tuple-element.14), channel_id=1, source_target_pairs={{0,8},{8,16},{16,24},{24,32},{32,40},{40,48},{48,56},{56,0},{1,9},... | collective-permute-start | bytes 393224 | tf_op jit(solution)/shard_map/ppermute | solution.py:228
  5.4 14.9 %collective-permute-start.1 = (bf16[512,128]{1,0:T(8,128)(2,1)}, bf16[512,128]{1,0:T(8,128)(2,1)S(1)}, u32[]{:S(2)}, u32[]{:S(2)}) collective-permute-start(bf16[512,128]{1,0:T(8,128)(2,1)} %get-tuple-element.14), channel_id=1, source_target_pairs={{0,56},{8,0},{16,8},{24,16},{32,24},{40,32},{48,40},{56,48},{1,57}... | collective-permute-start | bytes 393224 | tf_op jit(solution)/shard_map/ppermute | solution.py:228
  9.4 10.9 %collective-permute-start.2 = (bf16[512,128]{1,0:T(8,128)(2,1)}, bf16[512,128]{1,0:T(8,128)(2,1)S(1)}, u32[]{:S(2)}, u32[]{:S(2)}) collective-permute-start(bf16[512,128]{1,0:T(8,128)(2,1)} %get-tuple-element.14), channel_id=1, source_target_pairs={{0,32},{8,40},{16,48},{24,56},{32,0},{40,8},{48,16},{56,24},{1,33}... | collective-permute-start | bytes 393224 | tf_op jit(solution)/shard_map/ppermute | solution.py:228
  13.3 9.8 %copy-start.2 = (s32[8]{0:T(128)S(1)}, s32[8]{0:T(128)}, u32[]{:S(2)}) copy-start(s32[8]{0:T(128)} %constant.35.clone) | copy-start | bytes 100
  13.3 22.7 %all-to-all-start = ((bf16[16,272,128]{2,1,0:T(8,128)(2,1)}), bf16[16,272,128]{2,1,0:T(8,128)(2,1)S(1)}, u32[]{:S(2)}, u32[]{:S(2)}) async-start(bf16[16,272,128]{2,1,0:T(8,128)(2,1)} %get-tuple-element.13), calls=%async_computation | async-start | bytes 2228224 | tf_op jit(solution)/shard_map/all_to_all | solution.py:220
  20.2 10.4 %copy-start.1 = (bf16[512,128]{1,0:T(8,128)(2,1)S(1)}, bf16[512,128]{1,0:T(8,128)(2,1)}, u32[]{:S(2)}) copy-start(bf16[512,128]{1,0:T(8,128)(2,1)} %get-tuple-element.14) | copy-start | bytes 393220
  20.3 15.7 %copy-start = (s32[2]{0:T(128)S(1)}, s32[2]{0:T(128)}, u32[]{:S(2)}) copy-start(s32[2]{0:T(128)} %refs_1_.3) | copy-start | bytes 28
  20.3 7.2 %collective-permute-start.4 = (bf16[2,512,128]{2,1,0:T(8,128)(2,1)S(1)}, bf16[2,512,128]{2,1,0:T(8,128)(2,1)S(1)}, u32[]{:S(2)}, u32[]{:S(2)}) collective-permute-start(bf16[2,512,128]{2,1,0:T(8,128)(2,1)S(1)} %get-tuple-element.27), channel_id=1, source_target_pairs={{0,8},{8,16},{16,24},{24,32},{32,40},{40,48},{48,56},{56,0},{1,9},... | collective-permute-start | bytes 786440 | tf_op jit(solution)/shard_map/ppermute | solution.py:228
  20.4 7.1 %collective-permute-start.5 = (bf16[2,512,128]{2,1,0:T(8,128)(2,1)S(1)}, bf16[2,512,128]{2,1,0:T(8,128)(2,1)S(1)}, u32[]{:S(2)}, u32[]{:S(2)}) collective-permute-start(bf16[2,512,128]{2,1,0:T(8,128)(2,1)S(1)} %get-tuple-element.26), channel_id=1, source_target_pairs={{0,56},{8,0},{16,8},{24,16},{32,24},{40,32},{48,40},{56,48},{1,57}... | collective-permute-start | bytes 786440 | tf_op jit(solution)/shard_map/ppermute | solution.py:228
  27.6 8.4 %collective-permute-start.6 = (bf16[4,512,128]{2,1,0:T(8,128)(2,1)S(1)}, bf16[4,512,128]{2,1,0:T(8,128)(2,1)S(1)}, u32[]{:S(2)}, u32[]{:S(2)}) collective-permute-start(bf16[4,512,128]{2,1,0:T(8,128)(2,1)S(1)} %constant_dynamic-update-slice_fusion.refs_4_), channel_id=1, source_target_pairs={{0,1},{1,0},{2,3},{3,2},{4,5},{5,4},{6,7},{7,6},{8,9},{9,8},{10,11... | collective-permute-start | bytes 1572872 | tf_op jit(solution)/shard_map/ppermute | solution.py:224
  30.7 14.5 %collective-permute-start.3 = (bf16[4,512,128]{2,1,0:T(8,128)(2,1)S(1)}, bf16[4,512,128]{2,1,0:T(8,128)(2,1)S(1)}, u32[]{:S(2)}, u32[]{:S(2)}) collective-permute-start(bf16[4,512,128]{2,1,0:T(8,128)(2,1)S(1)} %pad_maximum_fusion.refs_4_), channel_id=1, source_target_pairs={{0,1},{1,0},{2,3},{3,2},{4,5},{5,4},{6,7},{7,6},{8,9},{9,8},{10,11... | collective-permute-start | bytes 1572872 | tf_op jit(solution)/shard_map/ppermute | solution.py:224
  41.8 10.5 %collective-permute-start.8 = (bf16[4,512,128]{2,1,0:T(8,128)(2,1)S(1)}, bf16[4,512,128]{2,1,0:T(8,128)(2,1)S(1)}, u32[]{:S(2)}, u32[]{:S(2)}) collective-permute-start(bf16[4,512,128]{2,1,0:T(8,128)(2,1)S(1)} %get-tuple-element.20), channel_id=1, source_target_pairs={{0,1},{1,0},{2,3},{3,2},{4,5},{5,4},{6,7},{7,6},{8,9},{9,8},{10,11... | collective-permute-start | bytes 1572872 | tf_op jit(solution)/shard_map/ppermute | solution.py:224
  50.9 8.3 %collective-permute-start.7 = (bf16[4,512,128]{2,1,0:T(8,128)(2,1)S(1)}, bf16[4,512,128]{2,1,0:T(8,128)(2,1)S(1)}, u32[]{:S(2)}, u32[]{:S(2)}) collective-permute-start(bf16[4,512,128]{2,1,0:T(8,128)(2,1)S(1)} %get-tuple-element.18), channel_id=1, source_target_pairs={{0,1},{1,0},{2,3},{3,2},{4,5},{5,4},{6,7},{7,6},{8,9},{9,8},{10,11... | collective-permute-start | bytes 1572872 | tf_op jit(solution)/shard_map/ppermute | solution.py:224
  53.1 8.1 %collective-permute-start.10 = (bf16[2,512,128]{2,1,0:T(8,128)(2,1)}, bf16[2,512,128]{2,1,0:T(8,128)(2,1)S(1)}, u32[]{:S(2)}, u32[]{:S(2)}) collective-permute-start(bf16[2,512,128]{2,1,0:T(8,128)(2,1)} %get-tuple-element.24), channel_id=1, source_target_pairs={{0,56},{8,0},{16,8},{24,16},{32,24},{40,32},{48,40},{56,48},{1,57}... | collective-permute-start | bytes 786440 | tf_op jit(solution)/shard_map/ppermute | solution.py:228
  53.3 8.3 %collective-permute-start.9 = (bf16[2,512,128]{2,1,0:T(8,128)(2,1)S(1)}, bf16[2,512,128]{2,1,0:T(8,128)(2,1)S(1)}, u32[]{:S(2)}, u32[]{:S(2)}) collective-permute-start(bf16[2,512,128]{2,1,0:T(8,128)(2,1)S(1)} %get-tuple-element.25), channel_id=1, source_target_pairs={{0,8},{8,16},{16,24},{24,32},{32,40},{40,48},{48,56},{56,0},{1,9},... | collective-permute-start | bytes 786440 | tf_op jit(solution)/shard_map/ppermute | solution.py:228
  54.6 21.5 %all-to-all-start.1 = ((bf16[16,256,128]{2,1,0:T(8,128)(2,1)}), bf16[16,256,128]{2,1,0:T(8,128)(2,1)S(1)}, u32[]{:S(2)}, u32[]{:S(2)}) async-start(bf16[16,256,128]{2,1,0:T(8,128)(2,1)} %bitcast.10), calls=%async_computation.1 | async-start | bytes 2097152 | tf_op jit(solution)/shard_map/all_to_all | solution.py:220
  61.7 10.8 %collective-permute-start.11 = (bf16[512,128]{1,0:T(8,128)(2,1)S(1)}, bf16[512,128]{1,0:T(8,128)(2,1)S(1)}, u32[]{:S(2)}, u32[]{:S(2)}) collective-permute-start(bf16[512,128]{1,0:T(8,128)(2,1)S(1)} %get-tuple-element.21), channel_id=1, source_target_pairs={{0,32},{8,40},{16,48},{24,56},{32,0},{40,8},{48,16},{56,24},{1,33}... | collective-permute-start | bytes 393224 | tf_op jit(solution)/shard_map/ppermute | solution.py:228
  65.0 10.3 %collective-permute-start.12 = (bf16[512,128]{1,0:T(8,128)(2,1)S(1)}, bf16[512,128]{1,0:T(8,128)(2,1)S(1)}, u32[]{:S(2)}, u32[]{:S(2)}) collective-permute-start(bf16[512,128]{1,0:T(8,128)(2,1)S(1)} %get-tuple-element.22), channel_id=1, source_target_pairs={{0,8},{8,16},{16,24},{24,32},{32,40},{40,48},{48,56},{56,0},{1,9},... | collective-permute-start | bytes 393224 | tf_op jit(solution)/shard_map/ppermute | solution.py:228
  65.0 10.3 %collective-permute-start.13 = (bf16[512,128]{1,0:T(8,128)(2,1)S(1)}, bf16[512,128]{1,0:T(8,128)(2,1)S(1)}, u32[]{:S(2)}, u32[]{:S(2)}) collective-permute-start(bf16[512,128]{1,0:T(8,128)(2,1)S(1)} %get-tuple-element.23), channel_id=1, source_target_pairs={{0,56},{8,0},{16,8},{24,16},{32,24},{40,32},{48,40},{56,48},{1,57}... | collective-permute-start | bytes 393224 | tf_op jit(solution)/shard_map/ppermute | solution.py:228

commit v11 on v10

--- a/solution.py
+++ b/solution.py
@@ -244,6 +244,12 @@
     for s in range(1, PLANE):
         total = total + parts_ref[s].astype(jnp.float32)
     out_ref[...] = total.astype(jnp.bfloat16)
+
+
+def far_kernel(mine_ref, other_ref, below_ref, above_ref):
+    far = PART // 2
+    below_ref[...] = add(mine_ref[:far], other_ref[:far]).astype(jnp.bfloat16)
+    above_ref[...] = add(mine_ref[far:], other_ref[far:]).astype(jnp.bfloat16)
 
 
 def combine_kernel(mine_ref, other_ref, below_ref, above_ref, up_ref, down_ref, over_ref):
@@ -345,8 +351,13 @@
     far_column = jnp.concatenate([heights[PART:], first_page])
     sums, far_mine, far_other = score(far_column, hot_pages, table, got, far, other_far)
     far_other = swap_cores(far_other)
-    to_above = add(far_mine[2:4], far_other[2:4]).astype(jnp.bfloat16)
-    to_below = add(far_mine[0:2], far_other[0:2]).astype(jnp.bfloat16)
+    to_below, to_above = pl.pallas_call(
+        far_kernel,
+        out_shape=(jax.ShapeDtypeStruct((PART // 2, HALF, W), jnp.bfloat16),) * 2,
+        in_specs=[vmem] * 2,
+        out_specs=(vmem,) * 2,
+        compiler_params=pltpu.CompilerParams(vmem_limit_bytes=4 << 20),
+    )(far_mine, far_other)
     from_below, from_above = move(to_above, 1), move(to_below, -1)
     query_part, near_mine, near_other = score(
         near_column, hot_pages, table, got, near, other_near, sums

time: 77.2 us -> 77.2 us (level)
  Pallas kernels: 14.5 us -> 16.4 us
  other arithmetic: 1.87 us -> 1.03 us
    ppermute x10, starting transfers between devices: 20.7 us -> 22.1 us  [move(): return lax.ppermute(array, 'z', [(i, (i + step) % NZ) for i in range(NZ)])]
    pallas_call x2, Pallas kernels: 11.4 us -> 12.5 us  [score(): pl.pallas_call(functools.partial(second_kernel if last else first_kernel,...]
    all_to_all x2, starting transfers between devices: 11.5 us -> 10.5 us  [exchange(): return lax.all_to_all(array, axes, split_axis=0, concat_axis=0, tiled=True)]
    convert_element_type x1 -> x0, other arithmetic: 0.83 us -> none  [shards(): to_below = add(far_mine[0:2], far_other[0:2]).astype(jnp.bfloat16)]
  transfers between devices with their start and end apart: 16 -> 16, of which waited for: 6 -> 6; matrix products, arithmetic and copies ran while one was open for 3% -> 1% of each run, Pallas kernels for 15% -> 17%
where the time goes in v11:
time: 77.2 us; the launch traced here: 77.6 us
  starting transfers between devices  40.4 us (52%)
  waiting for transfers between devices  18.9 us (24%)
  Pallas kernels  16.4 us (21%)
  other arithmetic  1.03 us (1%)
  between operations  0.82 us (1%)
    ppermute x10, starting transfers between devices, move(): return lax.ppermute(array, 'z', [(i, (i + step) % NZ) for i in range(NZ)])  22.1 us
    ppermute x10, waiting for transfers between devices, move(): return lax.ppermute(array, 'z', [(i, (i + step) % NZ) for i in range(NZ)])  13.7 us
    pallas_call x2, Pallas kernels, score(): pl.pallas_call(functools.partial(second_kernel if last else first_kernel,...  12.5 us
    all_to_all x2, starting transfers between devices, exchange(): return lax.all_to_all(array, axes, split_axis=0, concat_axis=0, tiled=True)  10.5 us
    ppermute x4, starting transfers between devices, swap_cores(): return lax.ppermute(array, 'core', [(0, 1), (1, 0)])  7.72 us
    all_to_all x2, waiting for transfers between devices, exchange(): return lax.all_to_all(array, axes, split_axis=0, concat_axis=0, tiled=True)  5.16 us
    pallas_call x1, Pallas kernels, shards(): pl.pallas_call(pack_kernel, out_shape=(jax.ShapeDtypeStruct((PLANE, SEND_...  2.18 us
  transfers between devices with their start and end apart: 16, of which 6 were waited for; matrix products, arithmetic and copies ran while one was open for 1% of the time, Pallas kernels for 17%

profile of v11, /device:TPU:1, one launch (start us, length us, event | category | flops | bytes accessed | tf_op | source)
XLA Modules:
  0.0 77.6 jit_solution(9644577469222993275)
XLA Ops:
  0.6 2.2 %shard_map.86 = (bf16[16,272,128]{2,1,0:T(8,128)(2,1)}, bf16[512,128]{1,0:T(8,128)(2,1)}) custom-call(s32[64]{0:T(128)} %bitcast.36, s32[64]{0:T(128)} %query_ref.1, s32[64]{0:T(128)} %label_ref.1, s32[1]{0:T(128)} %bitcast.2.core_ref, bf16[256,128]{1,0:T(8,128)(2,1)} %bitcast.34, bf16[1024,128]{1,0:T(8,128)(2,1)} %bitcast.32), custom_call_target="tpu_custom_call" | custom-call | tf_op jit(solution)/shard_map/pallas_call | solution.py:331
  2.8 2.5 %collective-permute-start = (bf16[512,128]{1,0:T(8,128)(2,1)}, bf16[512,128]{1,0:T(8,128)(2,1)S(1)}, u32[]{:S(2)}, u32[]{:S(2)}) collective-permute-start(bf16[512,128]{1,0:T(8,128)(2,1)} %get-tuple-element.16), channel_id=1, source_target_pairs={{0,8},{8,16},{16,24},{24,32},{32,40},{40,48},{48,56},{56,0},{1,9},... | collective-permute-start | bytes 393224 | tf_op jit(solution)/shard_map/ppermute | solution.py:228
  5.4 4.0 %collective-permute-start.1 = (bf16[512,128]{1,0:T(8,128)(2,1)}, bf16[512,128]{1,0:T(8,128)(2,1)S(1)}, u32[]{:S(2)}, u32[]{:S(2)}) collective-permute-start(bf16[512,128]{1,0:T(8,128)(2,1)} %get-tuple-element.16), channel_id=1, source_target_pairs={{0,56},{8,0},{16,8},{24,16},{32,24},{40,32},{48,40},{56,48},{1,57}... | collective-permute-start | bytes 393224 | tf_op jit(solution)/shard_map/ppermute | solution.py:228
  9.4 3.9 %collective-permute-start.2 = (bf16[512,128]{1,0:T(8,128)(2,1)}, bf16[512,128]{1,0:T(8,128)(2,1)S(1)}, u32[]{:S(2)}, u32[]{:S(2)}) collective-permute-start(bf16[512,128]{1,0:T(8,128)(2,1)} %get-tuple-element.16), channel_id=1, source_target_pairs={{0,32},{8,40},{16,48},{24,56},{32,0},{40,8},{48,16},{56,24},{1,33}... | collective-permute-start | bytes 393224 | tf_op jit(solution)/shard_map/ppermute | solution.py:228
  13.3 0.0 copy-start.2
  13.3 6.9 %all-to-all-start = ((bf16[16,272,128]{2,1,0:T(8,128)(2,1)}), bf16[16,272,128]{2,1,0:T(8,128)(2,1)S(1)}, u32[]{:S(2)}, u32[]{:S(2)}) async-start(bf16[16,272,128]{2,1,0:T(8,128)(2,1)} %get-tuple-element.15), calls=%async_computation | async-start | bytes 2228224 | tf_op jit(solution)/shard_map/all_to_all | solution.py:220
  20.2 0.0 copy-start.1
  20.2 0.0 collective-permute-done
  20.2 0.0 collective-permute-done.1
  20.2 0.0 collective-permute-done.2
  20.3 0.0 copy-start
  20.3 0.1 collective-permute-start.4
  20.4 0.0 copy-done.2
  20.4 2.7 %collective-permute-start.5 = (bf16[2,512,128]{2,1,0:T(8,128)(2,1)S(1)}, bf16[2,512,128]{2,1,0:T(8,128)(2,1)S(1)}, u32[]{:S(2)}, u32[]{:S(2)}) collective-permute-start(bf16[2,512,128]{2,1,0:T(8,128)(2,1)S(1)} %get-tuple-element.28), channel_id=1, source_target_pairs={{0,56},{8,0},{16,8},{24,16},{32,24},{40,32},{48,40},{56,48},{1,57}... | collective-permute-start | bytes 786440 | tf_op jit(solution)/shard_map/ppermute | solution.py:228
  23.2 0.1 fusion.5
  23.2 4.3 %collective-permute-done.4 = bf16[2,512,128]{2,1,0:T(8,128)(2,1)S(1)} collective-permute-done((bf16[2,512,128]{2,1,0:T(8,128)(2,1)S(1)}, bf16[2,512,128]{2,1,0:T(8,128)(2,1)S(1)}, u32[]{:S(2)}, u32[]{:S(2)}) %collective-permute-start.4) | collective-permute-done | bytes 262176 | tf_op jit(solution)/shard_map/ppermute | solution.py:228
  27.6 0.0 collective-permute-done.5
  27.6 2.9 %collective-permute-start.6 = (bf16[4,512,128]{2,1,0:T(8,128)(2,1)S(1)}, bf16[4,512,128]{2,1,0:T(8,128)(2,1)S(1)}, u32[]{:S(2)}, u32[]{:S(2)}) collective-permute-start(bf16[4,512,128]{2,1,0:T(8,128)(2,1)S(1)} %constant_dynamic-update-slice_fusion.refs_4_), channel_id=1, source_target_pairs={{0,1},{1,0},{2,3},{3,2},{4,5},{5,4},{6,7},{7,6},{8,9},{9,8},{10,11... | collective-permute-start | bytes 1572872 | tf_op jit(solution)/shard_map/ppermute | solution.py:224
  30.5 0.1 pad_add_fusion.1.refs_0_
  30.6 0.1 pad_add_fusion.refs_0_
  30.6 0.0 copy-done.1
  30.6 0.1 pad_maximum_fusion.refs_4_
  30.7 0.1 collective-permute-start.3
  30.8 5.2 %all-to-all-done.refs_3_ = bf16[16,272,128]{2,1,0:T(8,128)(2,1)S(1)} async-done(((bf16[16,272,128]{2,1,0:T(8,128)(2,1)}), bf16[16,272,128]{2,1,0:T(8,128)(2,1)S(1)}, u32[]{:S(2)}, u32[]{:S(2)}) %all-to-all-start) | async-done | bytes 1114144 | tf_op jit(solution)/shard_map/all_to_all | solution.py:220
  36.0 0.0 collective-permute-done.6.refs_5_
  36.0 0.0 copy-done
  36.0 6.9 %shard_map.87 = (f32[4096,128]{1,0:T(8,128)S(1)}, bf16[4,512,128]{2,1,0:T(8,128)(2,1)S(1)}, bf16[4,512,128]{2,1,0:T(8,128)(2,1)S(1)}) custom-call(s32[5]{0:T(128)S(1)} %pad_add_fusion.1.refs_0_, s32[2]{0:T(128)S(1)} %copy-done, s32[16,32]{1,0:T(8,128)S(1)} %bitcast.24, bf16[16,272,128]{2,1,0:T(8,128)(2,1)S(1)} %all-to-all-done.refs_3_, ...), custom_call_target="tpu_custom_call" | custom-call | flops 3221225472 | bytes 8388608 | tf_op jit(solution)/shard_map/pallas_call | solution.py:312
  42.9 3.3 %collective-permute-start.8 = (bf16[4,512,128]{2,1,0:T(8,128)(2,1)S(1)}, bf16[4,512,128]{2,1,0:T(8,128)(2,1)S(1)}, u32[]{:S(2)}, u32[]{:S(2)}) collective-permute-start(bf16[4,512,128]{2,1,0:T(8,128)(2,1)S(1)} %get-tuple-element.22), channel_id=1, source_target_pairs={{0,1},{1,0},{2,3},{3,2},{4,5},{5,4},{6,7},{7,6},{8,9},{9,8},{10,11... | collective-permute-start | bytes 1572872 | tf_op jit(solution)/shard_map/ppermute | solution.py:224
  46.2 0.0 collective-permute-done.3.refs_5_
  46.2 5.6 %shard_map.88 = (bf16[4096,128]{1,0:T(8,128)(2,1)}, bf16[4,512,128]{2,1,0:T(8,128)(2,1)S(1)}, bf16[4,512,128]{2,1,0:T(8,128)(2,1)S(1)}) custom-call(s32[5]{0:T(128)S(1)} %pad_add_fusion.refs_0_, s32[2]{0:T(128)S(1)} %copy-done, s32[16,32]{1,0:T(8,128)S(1)} %bitcast.25, bf16[16,272,128]{2,1,0:T(8,128)(2,1)S(1)} %all-to-all-done.refs_3_, ...), custom_call_target="tpu_custom_call" | custom-call | flops 3221225472 | bytes 8388608 | tf_op jit(solution)/shard_map/pallas_call | solution.py:312
  51.9 1.4 %collective-permute-start.7 = (bf16[4,512,128]{2,1,0:T(8,128)(2,1)S(1)}, bf16[4,512,128]{2,1,0:T(8,128)(2,1)S(1)}, u32[]{:S(2)}, u32[]{:S(2)}) collective-permute-start(bf16[4,512,128]{2,1,0:T(8,128)(2,1)S(1)} %get-tuple-element.20), channel_id=1, source_target_pairs={{0,1},{1,0},{2,3},{3,2},{4,5},{5,4},{6,7},{7,6},{8,9},{9,8},{10,11... | collective-permute-start | bytes 1572872 | tf_op jit(solution)/shard_map/ppermute | solution.py:224
  53.3 0.0 collective-permute-done.8.other_ref
  53.3 0.8 shard_map.90
  54.0 0.2 collective-permute-start.10
  54.2 1.3 %collective-permute-start.9 = (bf16[2,512,128]{2,1,0:T(8,128)(2,1)S(1)}, bf16[2,512,128]{2,1,0:T(8,128)(2,1)S(1)}, u32[]{:S(2)}, u32[]{:S(2)}) collective-permute-start(bf16[2,512,128]{2,1,0:T(8,128)(2,1)S(1)} %get-tuple-element.23), channel_id=1, source_target_pairs={{0,8},{8,16},{16,24},{24,32},{32,40},{40,48},{48,56},{56,0},{1,9},... | collective-permute-start | bytes 786440 | tf_op jit(solution)/shard_map/ppermute | solution.py:228
  55.5 3.7 %all-to-all-start.1 = ((bf16[16,256,128]{2,1,0:T(8,128)(2,1)}), bf16[16,256,128]{2,1,0:T(8,128)(2,1)S(1)}, u32[]{:S(2)}, u32[]{:S(2)}) async-start(bf16[16,256,128]{2,1,0:T(8,128)(2,1)} %bitcast.10), calls=%async_computation.1 | async-start | bytes 2097152 | tf_op jit(solution)/shard_map/all_to_all | solution.py:220
  59.2 0.0 collective-permute-done.7.other_ref
  59.2 3.0 %collective-permute-done.10.above_ref = bf16[2,512,128]{2,1,0:T(8,128)(2,1)S(1)} collective-permute-done((bf16[2,512,128]{2,1,0:T(8,128)(2,1)}, bf16[2,512,128]{2,1,0:T(8,128)(2,1)S(1)}, u32[]{:S(2)}, u32[]{:S(2)}) %collective-permute-start.10) | collective-permute-done | bytes 262176 | tf_op jit(solution)/shard_map/ppermute | solution.py:228
  62.2 0.3 collective-permute-done.9.below_ref
  62.5 0.2 shard_map.91
  62.7 4.7 %collective-permute-start.11 = (bf16[512,128]{1,0:T(8,128)(2,1)S(1)}, bf16[512,128]{1,0:T(8,128)(2,1)S(1)}, u32[]{:S(2)}, u32[]{:S(2)}) collective-permute-start(bf16[512,128]{1,0:T(8,128)(2,1)S(1)} %get-tuple-element.25), channel_id=1, source_target_pairs={{0,32},{8,40},{16,48},{24,56},{32,0},{40,8},{48,16},{56,24},{1,33}... | collective-permute-start | bytes 393224 | tf_op jit(solution)/shard_map/ppermute | solution.py:228
  67.3 0.0 collective-permute-start.12
  67.3 2.7 %collective-permute-start.13 = (bf16[512,128]{1,0:T(8,128)(2,1)S(1)}, bf16[512,128]{1,0:T(8,128)(2,1)S(1)}, u32[]{:S(2)}, u32[]{:S(2)}) collective-permute-start(bf16[512,128]{1,0:T(8,128)(2,1)S(1)} %get-tuple-element.27), channel_id=1, source_target_pairs={{0,56},{8,0},{16,8},{24,16},{32,24},{40,32},{48,40},{56,48},{1,57}... | collective-permute-start | bytes 393224 | tf_op jit(solution)/shard_map/ppermute | solution.py:228
  70.0 3.6 %collective-permute-done.11 = bf16[512,128]{1,0:T(8,128)(2,1)S(1)} collective-permute-done((bf16[512,128]{1,0:T(8,128)(2,1)S(1)}, bf16[512,128]{1,0:T(8,128)(2,1)S(1)}, u32[]{:S(2)}, u32[]{:S(2)}) %collective-permute-start.11) | collective-permute-done | bytes 131104 | tf_op jit(solution)/shard_map/ppermute | solution.py:228
  73.6 2.4 %collective-permute-done.12 = bf16[512,128]{1,0:T(8,128)(2,1)S(1)} collective-permute-done((bf16[512,128]{1,0:T(8,128)(2,1)S(1)}, bf16[512,128]{1,0:T(8,128)(2,1)S(1)}, u32[]{:S(2)}, u32[]{:S(2)}) %collective-permute-start.12) | collective-permute-done | bytes 131104 | tf_op jit(solution)/shard_map/ppermute | solution.py:228
  76.1 0.0 collective-permute-done.13
  76.1 0.7 fusion.3
  76.8 0.0 all-to-all-done.1.parts_ref
  76.8 0.8 shard_map.89
  (5 shorter events, 0.1 us)
Async XLA Ops:
  2.8 17.4 %collective-permute-start = (bf16[512,128]{1,0:T(8,128)(2,1)}, bf16[512,128]{1,0:T(8,128)(2,1)S(1)}, u32[]{:S(2)}, u32[]{:S(2)}) collective-permute-start(bf16[512,128]{1,0:T(8,128)(2,1)} %get-tuple-element.16), channel_id=1, source_target_pairs={{0,8},{8,16},{16,24},{24,32},{32,40},{40,48},{48,56},{56,0},{1,9},... | collective-permute-start | bytes 393224 | tf_op jit(solution)/shard_map/ppermute | solution.py:228
  5.4 14.9 %collective-permute-start.1 = (bf16[512,128]{1,0:T(8,128)(2,1)}, bf16[512,128]{1,0:T(8,128)(2,1)S(1)}, u32[]{:S(2)}, u32[]{:S(2)}) collective-permute-start(bf16[512,128]{1,0:T(8,128)(2,1)} %get-tuple-element.16), channel_id=1, source_target_pairs={{0,56},{8,0},{16,8},{24,16},{32,24},{40,32},{48,40},{56,48},{1,57}... | collective-permute-start | bytes 393224 | tf_op jit(solution)/shard_map/ppermute | solution.py:228
  9.4 10.9 %collective-permute-start.2 = (bf16[512,128]{1,0:T(8,128)(2,1)}, bf16[512,128]{1,0:T(8,128)(2,1)S(1)}, u32[]{:S(2)}, u32[]{:S(2)}) collective-permute-start(bf16[512,128]{1,0:T(8,128)(2,1)} %get-tuple-element.16), channel_id=1, source_target_pairs={{0,32},{8,40},{16,48},{24,56},{32,0},{40,8},{48,16},{56,24},{1,33}... | collective-permute-start | bytes 393224 | tf_op jit(solution)/shard_map/ppermute | solution.py:228
  13.3 7.1 %copy-start.2 = (s32[8]{0:T(128)S(1)}, s32[8]{0:T(128)}, u32[]{:S(2)}) copy-start(s32[8]{0:T(128)} %constant.35.clone) | copy-start | bytes 100
  13.3 22.7 %all-to-all-start = ((bf16[16,272,128]{2,1,0:T(8,128)(2,1)}), bf16[16,272,128]{2,1,0:T(8,128)(2,1)S(1)}, u32[]{:S(2)}, u32[]{:S(2)}) async-start(bf16[16,272,128]{2,1,0:T(8,128)(2,1)} %get-tuple-element.15), calls=%async_computation | async-start | bytes 2228224 | tf_op jit(solution)/shard_map/all_to_all | solution.py:220
  20.2 10.4 %copy-start.1 = (bf16[512,128]{1,0:T(8,128)(2,1)S(1)}, bf16[512,128]{1,0:T(8,128)(2,1)}, u32[]{:S(2)}) copy-start(bf16[512,128]{1,0:T(8,128)(2,1)} %get-tuple-element.16) | copy-start | bytes 393220
  20.3 15.7 %copy-start = (s32[2]{0:T(128)S(1)}, s32[2]{0:T(128)}, u32[]{:S(2)}) copy-start(s32[2]{0:T(128)} %refs_1_.3) | copy-start | bytes 28
  20.3 7.2 %collective-permute-start.4 = (bf16[2,512,128]{2,1,0:T(8,128)(2,1)S(1)}, bf16[2,512,128]{2,1,0:T(8,128)(2,1)S(1)}, u32[]{:S(2)}, u32[]{:S(2)}) collective-permute-start(bf16[2,512,128]{2,1,0:T(8,128)(2,1)S(1)} %get-tuple-element.29), channel_id=1, source_target_pairs={{0,8},{8,16},{16,24},{24,32},{32,40},{40,48},{48,56},{56,0},{1,9},... | collective-permute-start | bytes 786440 | tf_op jit(solution)/shard_map/ppermute | solution.py:228
  20.4 7.1 %collective-permute-start.5 = (bf16[2,512,128]{2,1,0:T(8,128)(2,1)S(1)}, bf16[2,512,128]{2,1,0:T(8,128)(2,1)S(1)}, u32[]{:S(2)}, u32[]{:S(2)}) collective-permute-start(bf16[2,512,128]{2,1,0:T(8,128)(2,1)S(1)} %get-tuple-element.28), channel_id=1, source_target_pairs={{0,56},{8,0},{16,8},{24,16},{32,24},{40,32},{48,40},{56,48},{1,57}... | collective-permute-start | bytes 786440 | tf_op jit(solution)/shard_map/ppermute | solution.py:228
  27.6 8.4 %collective-permute-start.6 = (bf16[4,512,128]{2,1,0:T(8,128)(2,1)S(1)}, bf16[4,512,128]{2,1,0:T(8,128)(2,1)S(1)}, u32[]{:S(2)}, u32[]{:S(2)}) collective-permute-start(bf16[4,512,128]{2,1,0:T(8,128)(2,1)S(1)} %constant_dynamic-update-slice_fusion.refs_4_), channel_id=1, source_target_pairs={{0,1},{1,0},{2,3},{3,2},{4,5},{5,4},{6,7},{7,6},{8,9},{9,8},{10,11... | collective-permute-start | bytes 1572872 | tf_op jit(solution)/shard_map/ppermute | solution.py:224
  30.7 15.5 %collective-permute-start.3 = (bf16[4,512,128]{2,1,0:T(8,128)(2,1)S(1)}, bf16[4,512,128]{2,1,0:T(8,128)(2,1)S(1)}, u32[]{:S(2)}, u32[]{:S(2)}) collective-permute-start(bf16[4,512,128]{2,1,0:T(8,128)(2,1)S(1)} %pad_maximum_fusion.refs_4_), channel_id=1, source_target_pairs={{0,1},{1,0},{2,3},{3,2},{4,5},{5,4},{6,7},{7,6},{8,9},{9,8},{10,11... | collective-permute-start | bytes 1572872 | tf_op jit(solution)/shard_map/ppermute | solution.py:224
  42.9 10.4 %collective-permute-start.8 = (bf16[4,512,128]{2,1,0:T(8,128)(2,1)S(1)}, bf16[4,512,128]{2,1,0:T(8,128)(2,1)S(1)}, u32[]{:S(2)}, u32[]{:S(2)}) collective-permute-start(bf16[4,512,128]{2,1,0:T(8,128)(2,1)S(1)} %get-tuple-element.22), channel_id=1, source_target_pairs={{0,1},{1,0},{2,3},{3,2},{4,5},{5,4},{6,7},{7,6},{8,9},{9,8},{10,11... | collective-permute-start | bytes 1572872 | tf_op jit(solution)/shard_map/ppermute | solution.py:224
  51.9 7.3 %collective-permute-start.7 = (bf16[4,512,128]{2,1,0:T(8,128)(2,1)S(1)}, bf16[4,512,128]{2,1,0:T(8,128)(2,1)S(1)}, u32[]{:S(2)}, u32[]{:S(2)}) collective-permute-start(bf16[4,512,128]{2,1,0:T(8,128)(2,1)S(1)} %get-tuple-element.20), channel_id=1, source_target_pairs={{0,1},{1,0},{2,3},{3,2},{4,5},{5,4},{6,7},{7,6},{8,9},{9,8},{10,11... | collective-permute-start | bytes 1572872 | tf_op jit(solution)/shard_map/ppermute | solution.py:224
  54.0 8.1 %collective-permute-start.10 = (bf16[2,512,128]{2,1,0:T(8,128)(2,1)}, bf16[2,512,128]{2,1,0:T(8,128)(2,1)S(1)}, u32[]{:S(2)}, u32[]{:S(2)}) collective-permute-start(bf16[2,512,128]{2,1,0:T(8,128)(2,1)} %get-tuple-element.24), channel_id=1, source_target_pairs={{0,56},{8,0},{16,8},{24,16},{32,24},{40,32},{48,40},{56,48},{1,57}... | collective-permute-start | bytes 786440 | tf_op jit(solution)/shard_map/ppermute | solution.py:228
  54.2 8.3 %collective-permute-start.9 = (bf16[2,512,128]{2,1,0:T(8,128)(2,1)S(1)}, bf16[2,512,128]{2,1,0:T(8,128)(2,1)S(1)}, u32[]{:S(2)}, u32[]{:S(2)}) collective-permute-start(bf16[2,512,128]{2,1,0:T(8,128)(2,1)S(1)} %get-tuple-element.23), channel_id=1, source_target_pairs={{0,8},{8,16},{16,24},{24,32},{32,40},{40,48},{48,56},{56,0},{1,9},... | collective-permute-start | bytes 786440 | tf_op jit(solution)/shard_map/ppermute | solution.py:228
  55.5 21.3 %all-to-all-start.1 = ((bf16[16,256,128]{2,1,0:T(8,128)(2,1)}), bf16[16,256,128]{2,1,0:T(8,128)(2,1)S(1)}, u32[]{:S(2)}, u32[]{:S(2)}) async-start(bf16[16,256,128]{2,1,0:T(8,128)(2,1)} %bitcast.10), calls=%async_computation.1 | async-start | bytes 2097152 | tf_op jit(solution)/shard_map/all_to_all | solution.py:220
  62.7 11.0 %collective-permute-start.11 = (bf16[512,128]{1,0:T(8,128)(2,1)S(1)}, bf16[512,128]{1,0:T(8,128)(2,1)S(1)}, u32[]{:S(2)}, u32[]{:S(2)}) collective-permute-start(bf16[512,128]{1,0:T(8,128)(2,1)S(1)} %get-tuple-element.25), channel_id=1, source_target_pairs={{0,32},{8,40},{16,48},{24,56},{32,0},{40,8},{48,16},{56,24},{1,33}... | collective-permute-start | bytes 393224 | tf_op jit(solution)/shard_map/ppermute | solution.py:228
  67.3 8.7 %collective-permute-start.12 = (bf16[512,128]{1,0:T(8,128)(2,1)S(1)}, bf16[512,128]{1,0:T(8,128)(2,1)S(1)}, u32[]{:S(2)}, u32[]{:S(2)}) collective-permute-start(bf16[512,128]{1,0:T(8,128)(2,1)S(1)} %get-tuple-element.26), channel_id=1, source_target_pairs={{0,8},{8,16},{16,24},{24,32},{32,40},{40,48},{48,56},{56,0},{1,9},... | collective-permute-start | bytes 393224 | tf_op jit(solution)/shard_map/ppermute | solution.py:228
  67.3 8.7 %collective-permute-start.13 = (bf16[512,128]{1,0:T(8,128)(2,1)S(1)}, bf16[512,128]{1,0:T(8,128)(2,1)S(1)}, u32[]{:S(2)}, u32[]{:S(2)}) collective-permute-start(bf16[512,128]{1,0:T(8,128)(2,1)S(1)} %get-tuple-element.27), channel_id=1, source_target_pairs={{0,56},{8,0},{16,8},{24,16},{32,24},{40,32},{48,40},{56,48},{1,57}... | collective-permute-start | bytes 393224 | tf_op jit(solution)/shard_map/ppermute | solution.py:228
